TPU v7x, 32 devices: a whole 2x2x4 slice. The times are simulated.
32 devices in a mesh: frames: 16 (over z, y, x), strips: 2 (over core).
Axes of the slice: x: 2, y: 2, z: 4, core: 2. Of those that a mesh axis runs over, the one named last changes fastest.
Arguments:
- raw_frames: bfloat16 [1024, 512, 512], P('frames', 'strips'), may hold values from -24 to 24
- dark_frame: float32 [512, 512], P('strips'), may hold values from -6 to 6
- dead_mask: int32 [512, 512], P('strips'), may hold values 0 or 1
- frame_group: int32 [1024], P('frames'), may hold values from 0 to 7
- prior_sigma: float32 [128], replicated, may hold values from 0.2 to 0.5
- start_rotation: float32 [128, 128], replicated, as said below
- basis: bfloat16 [262144, 128], P(('strips', 'frames')), may hold values from -0.01171875 to 0.01171875
Outputs:
- new_basis: bfloat16 [262144, 128], P(('strips', 'frames'))
- new_coeffs: float32 [1024, 128], P('frames')
- new_sigma: float32 [128], replicated
Inputs may be any that keep to these rules, and one draw needn't show every extreme that they name: start_rotation is nonsingular.
All inputs are finite; a program needn't handle non-finite values. No bound on the sum of `dead_mask` on one device may be relied on, other than what follows from the above.
Results may differ from a plain program's by a relative error of at most 0.0071.
Values may be sent and summed in bfloat16 or wider, within the bound.
No kernel may reach another device: no remote copies, remote signals or barrier semaphores. Data moves between devices by JAX's collectives and lax.ppermute only.
A program may use at most 192 MiB of HBM per device.

v0:
```python
import jax
import jax.numpy as jnp
from jax import lax
from jax.sharding import PartitionSpec as P

GROUPS = 8
ITERS = 4


BLUR_TAPS = (1.0 / 64, 6.0 / 64, 15.0 / 64, 20.0 / 64, 15.0 / 64, 6.0 / 64, 1.0 / 64)
DECAY_RATE = 0.7


def extended(shard, sides, width):
    for axis, dim in sides:
        size, length = (lax.axis_size(axis), shard.shape[dim])
        up = [(i, (i + 1) % size) for i in range(size - 1)]
        down = [(j, i) for i, j in up]
        last = lax.slice_in_dim(shard, length - width, length, axis=dim)
        first = lax.slice_in_dim(shard, 0, width, axis=dim)
        before = lax.ppermute(last, axis, up)
        after = lax.ppermute(first, axis, down)
        shard = jnp.concatenate([before, shard, after], axis=dim)
    return shard


def orthonormalize(product):
    normal = jnp.dot(product.T, product, precision=lax.Precision.HIGHEST)
    factor = jnp.linalg.cholesky(normal)
    return lax.linalg.triangular_solve(
        factor, product, left_side=False, lower=True, transpose_a=True
    )


def body(raw_frames, dark_frame, dead_mask, frame_group, prior_sigma, start_rotation, basis):
    frame_count, strip_rows, columns = raw_frames.shape
    corrected = (
        (raw_frames.astype(jnp.float32) - dark_frame) * (1 - dead_mask).astype(jnp.float32)
    ).astype(jnp.bfloat16)
    position = jnp.arange(columns)
    offsets = position[None, :] - position[:, None]
    banded = jnp.zeros((columns, columns), jnp.float32)
    for shift_by in range(-3, 4):
        banded = banded + jnp.where(offsets == shift_by, BLUR_TAPS[shift_by + 3], 0.0)
    banded = banded.astype(jnp.bfloat16)
    column_blur = jnp.dot(
        corrected.reshape(frame_count * strip_rows, columns),
        banded,
        preferred_element_type=jnp.float32,
    )
    column_blur = column_blur.reshape(frame_count, strip_rows, columns)
    padded = extended(column_blur, (("strips", 1),), 3)
    row_blur = BLUR_TAPS[0] * padded[:, 0:strip_rows, :]
    for offset in range(1, 7):
        row_blur = row_blur + BLUR_TAPS[offset] * padded[:, offset : offset + strip_rows, :]
    frame_weight = jnp.power(
        jnp.float32(DECAY_RATE), (GROUPS - 1 - frame_group).astype(jnp.float32)
    )
    weighted = (
        (frame_weight[:, None, None] * row_blur)
        .astype(jnp.bfloat16)
        .reshape(frame_count, strip_rows * columns)
    )
    partial_value = jnp.dot(
        weighted,
        lax.all_gather(basis, "frames", axis=0, tiled=True),
        preferred_element_type=jnp.float32,
    )
    coeffs = lax.psum(partial_value, "strips")
    total_frames = frame_count * lax.axis_size("frames")
    local_gram = jnp.dot(coeffs.T, coeffs, precision=lax.Precision.HIGHEST)
    summed_gram = lax.psum(local_gram, "frames")
    gram = jnp.diag(prior_sigma * prior_sigma) + summed_gram / total_frames
    rotation = start_rotation
    for step in range(ITERS):
        rotation = orthonormalize(jnp.dot(gram, rotation, precision=lax.Precision.HIGHEST))
    new_coeffs = jnp.dot(coeffs, rotation, precision=lax.Precision.HIGHEST)
    new_basis = jnp.dot(
        basis.astype(jnp.float32), rotation, precision=lax.Precision.HIGHEST
    ).astype(jnp.bfloat16)
    curved = jnp.dot(gram, rotation, precision=lax.Precision.HIGHEST)
    new_sigma = jnp.sqrt(jnp.sum(rotation * curved, axis=0))
    return (new_basis, new_coeffs, new_sigma)


def solution(mesh):
    placed = (
        P("frames", "strips", None),
        P("strips", None),
        P("strips", None),
        P("frames"),
        P(),
        P(),
        P(("strips", "frames"), None),
    )
    return jax.shard_map(
        body,
        mesh=mesh,
        in_specs=placed,
        out_specs=(P(("strips", "frames"), None), P("frames", None), P()),
        check_vma=False,
    )
```

profile of v0, /device:TPU:0, one launch (start us, length us, event | category | flops | bytes accessed | tf_op | source)
XLA Modules:
  0.0 603.9 jit_solution(16150601691725152074)
XLA Ops:
  7.2 0.7 all-gather.2.cloned.1.call-update
  8.0 1.1 subtract_convert_fusion
  9.1 20.7 %fusion.18 = f32[64,256,512]{2,1,0:T(8,128)} fusion(bf16[64,256,512]{2,1,0:T(8,128)(2,1)} %param.10, f32[256,512]{1,0:T(8,128)S(1)} %subtract_convert_fusion, f32[256,512]{1,0:T(8,128)} %param.11), kind=kOutput, calls=%fused_computation.25 | convolution fusion | flops 8629256192 | bytes 51380224 | tf_op jit(solution)/shard_map/dot_general | solution.py:46
  29.8 1.8 fusion.85
  31.6 2.4 collective-permute-start
  34.0 1.5 collective-permute-start.1
  35.5 2.3 collective-permute-done.1
  37.8 81.8 %fusion.5 = bf16[64,256,512]{2,1,0:T(8,128)(2,1)} fusion(f32[64,3,512]{2,1,0:T(4,128)S(1)} %collective-permute-done.1, f32[64,3,512]{2,1,0:T(4,128)S(1)} %collective-permute-done, f32[64,256,512]{2,1,0:T(8,128)} %fusion.18, f32[64]{0:T(128)S(1)} %convert_power_fusion), kind=kLoop, calls=%fused_computation.9 | loop fusion | flops 176160768 | bytes 51118336 | tf_op jit(solution)/shard_map/convert_element_type | solution.py:61
  119.6 18.4 %copy.15 = bf16[8,8,256,512]{3,1,2,0:T(8,128)(2,1)} copy(bf16[8,8,256,512]{3,2,1,0:T(8,128)(2,1)} %bitcast.77) | data formatting | bytes 33554432
  138.1 226.3 %all-gather.2.cloned.1.call-done = bf16[131072,128]{1,0:T(8,128)(2,1)} async-done(((bf16[8192,128]{1,0:T(8,128)(2,1)}), bf16[131072,128]{1,0:T(8,128)(2,1)}) %all-gather.2.cloned.1.call-update) | async-done | bytes 33554448 | tf_op jit(solution)/shard_map/all_gather | solution.py:66
  364.4 18.5 %fusion.86 = f32[64,128]{1,0:T(8,128)S(1)} fusion(bf16[64,131072]{1,0:T(8,128)(2,1)} %bitcast.76, bf16[131072,128]{1,0:T(8,128)(2,1)} %all-gather.2.cloned.1.call-done), kind=kOutput, calls=%fused_computation.112 | convolution fusion | flops 2147483648 | bytes 50364416 | tf_op jit(solution)/shard_map/dot_general | solution.py:64
  382.9 3.6 psum.14
  386.5 0.9 fusion.87
  387.5 100.3 %all-reduce.2.cloned.1.call-done = f32[128,128]{1,0:T(8,128)} async-done(((f32[128,128]{1,0:T(8,128)}), f32[128,128]{1,0:T(8,128)}) %all-reduce.2.cloned.1.call-update) | async-done | bytes 65552 | tf_op jit(solution)/shard_map/psum | solution.py:72
  487.8 1.1 fusion.83
  488.9 0.3 fusion.88
  489.2 0.1 copy.10
  489.3 11.7 %cholesky.74 = f32[128,128]{1,0:T(8,128)S(1)} custom-call(f32[128,128]{1,0:T(8,128)S(1)} %fusion.55), custom_call_target="Cholesky" | custom-call | tf_op jit(solution)/shard_map/jit(cholesky)/cholesky | solution.py:29
  501.1 0.6 compare_reduce_fusion.3
  501.7 0.7 fusion.44
  502.4 9.8 %custom-call.8 = f32[1,128,128]{1,2,0:T(8,128)S(1)} custom-call(f32[1,128,128]{2,1,0:T(8,128)S(1)} %fusion.44), custom_call_target="InvertDiagBlocksLowerTriangular" | custom-call | tf_op jit(solution)/shard_map/triangular_solve/custom-call.0 | solution.py:30
  512.2 0.3 convolution_bitcast_fusion.3
  512.5 1.1 fusion.81
  513.6 0.3 fusion.89
  514.0 11.7 %cholesky.85 = f32[128,128]{1,0:T(8,128)S(1)} custom-call(f32[128,128]{1,0:T(8,128)S(1)} %fusion.53), custom_call_target="Cholesky" | custom-call | tf_op jit(solution)/shard_map/jit(cholesky)/cholesky | solution.py:29
  525.8 0.6 compare_reduce_fusion.2
  526.4 0.7 fusion.45
  527.1 10.2 %custom-call.9 = f32[1,128,128]{1,2,0:T(8,128)S(1)} custom-call(f32[1,128,128]{2,1,0:T(8,128)S(1)} %fusion.45), custom_call_target="InvertDiagBlocksLowerTriangular" | custom-call | tf_op jit(solution)/shard_map/triangular_solve/custom-call.0 | solution.py:30
  537.3 0.3 convolution_bitcast_fusion.2
  537.6 1.1 fusion.79
  538.7 0.3 fusion.90
  539.1 11.7 %cholesky.96 = f32[128,128]{1,0:T(8,128)S(1)} custom-call(f32[128,128]{1,0:T(8,128)S(1)} %fusion.51), custom_call_target="Cholesky" | custom-call | tf_op jit(solution)/shard_map/jit(cholesky)/cholesky | solution.py:29
  550.9 0.6 compare_reduce_fusion.1
  551.5 0.7 fusion.46
  552.2 9.8 %custom-call.10 = f32[1,128,128]{1,2,0:T(8,128)S(1)} custom-call(f32[1,128,128]{2,1,0:T(8,128)S(1)} %fusion.46), custom_call_target="InvertDiagBlocksLowerTriangular" | custom-call | tf_op jit(solution)/shard_map/triangular_solve/custom-call.0 | solution.py:30
  562.0 0.3 convolution_bitcast_fusion.1
  562.3 1.1 fusion.77
  563.4 0.3 fusion.91
  563.8 11.7 %cholesky.107 = f32[128,128]{1,0:T(8,128)S(1)} custom-call(f32[128,128]{1,0:T(8,128)S(1)} %fusion.49), custom_call_target="Cholesky" | custom-call | tf_op jit(solution)/shard_map/jit(cholesky)/cholesky | solution.py:29
  575.6 0.6 compare_reduce_fusion
  576.2 0.7 fusion.47
  576.9 10.0 %custom-call.11 = f32[1,128,128]{1,2,0:T(8,128)S(1)} custom-call(f32[1,128,128]{2,1,0:T(8,128)S(1)} %fusion.47), custom_call_target="InvertDiagBlocksLowerTriangular" | custom-call | tf_op jit(solution)/shard_map/triangular_solve/custom-call.0 | solution.py:30
  586.9 0.2 convolution_bitcast_fusion
  587.1 0.8 fusion.92
  587.9 3.2 fusion.21
  591.1 1.1 fusion.22
  592.2 0.5 sqrt.3
  592.8 4.1 copy.14
  (25 shorter events, 0.6 us)
Async XLA Ops:
  7.2 480.6 %copy-start = (f32[128,128]{1,0:T(8,128)S(1)}, f32[128,128]{1,0:T(8,128)}, u32[]{:S(2)}) copy-start(f32[128,128]{1,0:T(8,128)} %param.15) | copy-start | bytes 196612
  7.2 357.2 %all-gather.2.cloned.1.call-start = ((), (), s32[]{:S(2)}) async-start(), calls=%async_computation | async-start | bytes 35651584 | tf_op jit(solution)/shard_map/all_gather | solution.py:66
  7.9 479.9 %all-reduce.2.cloned.1.call-start = ((), (), s32[]{:S(2)}) async-start(), calls=%async_computation.1 | async-start | bytes 131072 | tf_op jit(solution)/shard_map/psum | solution.py:72
  9.1 26.4 %copy-start.2 = (s32[64]{0:T(128)S(1)}, s32[64]{0:T(128)}, u32[]{:S(2)}) copy-start(s32[64]{0:T(128)} %param.13) | copy-start | bytes 772
  31.6 3.9 collective-permute-start
  34.0 3.8 collective-permute-start.1
  138.1 249.4 %copy-start.3 = (f32[128]{0:T(128)S(1)}, f32[128]{0:T(128)}, u32[]{:S(2)}) copy-start(f32[128]{0:T(128)} %param.14) | copy-start | bytes 1540
  138.1 449.8 %copy-start.1 = (bf16[8192,128]{1,0:T(8,128)(2,1)S(1)}, bf16[8192,128]{1,0:T(8,128)(2,1)}, u32[]{:S(2)}) copy-start(bf16[8192,128]{1,0:T(8,128)(2,1)} %param.16) | copy-start | bytes 6291460
Sparse Core Ops, SparseCore 0:
  10.8 353.5 all-gather.1
  387.6 100.2 all-reduce.1
where the time goes:
time: 609 us; the launch traced here: 604 us
  waiting for transfers between devices  330 us (54%)
  other arithmetic  175 us (29%)
  matrix products  52 us (9%)
  local copies, waits for them, and re-layouts  25.2 us (4%)
  between operations  14.5 us (2%)
    all_gather x1, waiting for transfers between devices, body(): lax.all_gather(basis, 'frames', axis=0, tiled=True)  226 us
    psum x1, waiting for transfers between devices, body(): summed_gram = lax.psum(local_gram, 'frames')  100 us
    convert_element_type x1, other arithmetic, body(): weighted = (frame_weight[:, None, None] * row_blur).astype(jnp.bfloat16)....  81.8 us
    another operation x12, other arithmetic, orthonormalize(): factor = jnp.linalg.cholesky(normal)  49.6 us
    another operation x8, other arithmetic, orthonormalize(): lax.linalg.triangular_solve(factor, product, left_side=False, lower=True,...  42.4 us
    unnamed x10, local copies, waits for them, and re-layouts  22.5 us
    dot_general x1, matrix products, body(): jnp.dot(corrected.reshape(frame_count * strip_rows, columns), banded, pre...  20.7 us
    dot_general x1, matrix products, body(): jnp.dot(weighted, lax.all_gather(basis, 'frames', axis=0, tiled=True), pr...  18.5 us
  transfers between devices with their start and end apart: 4, of which 3 were waited for; matrix products, arithmetic and copies ran while one was open for 21% of the time, Pallas kernels for 0%

commit v1 on v0

--- a/solution.py
+++ b/solution.py
@@ -1,6 +1,10 @@
+import functools
+
 import jax
 import jax.numpy as jnp
 from jax import lax
+from jax.experimental import pallas as pl
+from jax.experimental.pallas import tpu as pltpu
 from jax.sharding import PartitionSpec as P
 
 GROUPS = 8
@@ -9,6 +13,8 @@
 
 BLUR_TAPS = (1.0 / 64, 6.0 / 64, 15.0 / 64, 20.0 / 64, 15.0 / 64, 6.0 / 64, 1.0 / 64)
 DECAY_RATE = 0.7
+HIGHEST = lax.Precision.HIGHEST
+PANEL = 32
 
 
 def extended(shard, sides, width):
@@ -24,12 +30,119 @@
     return shard
 
 
-def orthonormalize(product):
-    normal = jnp.dot(product.T, product, precision=lax.Precision.HIGHEST)
-    factor = jnp.linalg.cholesky(normal)
-    return lax.linalg.triangular_solve(
-        factor, product, left_side=False, lower=True, transpose_a=True
-    )
+def summed_over(values, axis):
+    size = lax.axis_size(axis)
+    if size & (size - 1):
+        return lax.psum(values, axis)
+    distance = 1
+    while distance < size:
+        pairs = [(i, i ^ distance) for i in range(size)]
+        values = values + lax.ppermute(values, axis, pairs)
+        distance *= 2
+    return values
+
+
+def reciprocal(values):
+    guess = pltpu.reciprocal(values, approx=True)
+    return guess * (2.0 - values * guess)
+
+
+def orthonormal_rows(product):
+    size = product.shape[0]
+    product = product * lax.rsqrt(jnp.sum(product * product, axis=1, keepdims=True))
+    across = (((1,), (1,)), ((), ()))
+    down = (((0,), (0,)), ((), ()))
+    normal = lax.dot_general(product, product, across, precision=HIGHEST, preferred_element_type=jnp.float32)
+    state = jnp.concatenate([normal, product], axis=1)
+    rows = lax.broadcasted_iota(jnp.int32, (PANEL, size), 0)
+    lanes = lax.broadcasted_iota(jnp.int32, (PANEL, size), 1)
+    shape = (PANEL, size)
+    finished = []
+    for base in range(0, size, PANEL):
+        left, right = (state[:PANEL, :size], state[:PANEL, size:])
+        for j in range(0, PANEL, 2):
+            column = base + j
+            col0 = jnp.broadcast_to(left[:, column : column + 1], shape)
+            col1 = jnp.broadcast_to(left[:, column + 1 : column + 2], shape)
+            aa = jnp.broadcast_to(col0[j : j + 1], shape)
+            ab = jnp.broadcast_to(col1[j : j + 1], shape)
+            bb = jnp.broadcast_to(col1[j + 1 : j + 2], shape)
+            inverse = reciprocal(aa * bb - ab * ab)
+            below = rows > j + 1
+            second = rows == j + 1
+            factor0 = jnp.where(
+                below, (col0 * bb - col1 * ab) * inverse, jnp.where(second, ab * reciprocal(aa), 0.0)
+            )
+            factor1 = jnp.where(below, (col1 * aa - col0 * ab) * inverse, 0.0)
+            left0 = jnp.broadcast_to(left[j : j + 1], shape)
+            left1 = jnp.broadcast_to(left[j + 1 : j + 2], shape)
+            right0 = jnp.broadcast_to(right[j : j + 1], shape)
+            right1 = jnp.broadcast_to(right[j + 1 : j + 2], shape)
+            left = left - factor0 * left0 - factor1 * left1
+            right = right - factor0 * right0 - factor1 * right1
+        pivots = jnp.sum(jnp.where(lanes == base + rows, left, 0.0), axis=1, keepdims=True)
+        scale = lax.rsqrt(pivots)
+        left = left * scale
+        right = right * scale
+        finished.append(right)
+        if base + PANEL < size:
+            update = lax.dot_general(
+                left[:, base + PANEL :],
+                jnp.concatenate([left, right], axis=1),
+                down,
+                precision=HIGHEST,
+                preferred_element_type=jnp.float32,
+            )
+            state = state[PANEL:] - update
+    return jnp.concatenate(finished, axis=0)
+
+
+def rotate_kernel(frames, chunk, summed_ref, sigma_ref, start_ref, coeffs_ref, basis_ref, basis_out, coeffs_out, sigma_out):
+    size = summed_ref.shape[0]
+    across = (((1,), (1,)), ((), ()))
+    diagonal = lax.broadcasted_iota(jnp.int32, (size, size), 0) == lax.broadcasted_iota(jnp.int32, (size, size), 1)
+    sigma = jnp.broadcast_to(sigma_ref[...], (size, size))
+    gram = jnp.where(diagonal, sigma * sigma, 0.0) + summed_ref[...] * (1.0 / frames)
+
+    def step(_, turned):
+        return orthonormal_rows(jnp.dot(turned, gram, precision=HIGHEST, preferred_element_type=jnp.float32))
+
+    turned = lax.fori_loop(0, ITERS, step, start_ref[...].T)
+    coeffs_out[...] = lax.dot_general(
+        coeffs_ref[...], turned, across, precision=HIGHEST, preferred_element_type=jnp.float32
+    )
+    curved = jnp.dot(turned, gram, precision=HIGHEST, preferred_element_type=jnp.float32)
+    sigma_out[...] = jnp.sqrt(jnp.sum((turned * curved).T, axis=0, keepdims=True))
+    rotation = turned.T
+    high = rotation.astype(jnp.bfloat16)
+    rest = rotation - high.astype(jnp.float32)
+    middle = rest.astype(jnp.bfloat16)
+    low = (rest - middle.astype(jnp.float32)).astype(jnp.bfloat16)
+
+    @pl.loop(0, basis_ref.shape[0] // chunk)
+    def _(i):
+        at = pl.ds(pl.multiple_of(i * chunk, chunk), chunk)
+        block = basis_ref[at, :]
+        total = jnp.dot(block, low, preferred_element_type=jnp.float32)
+        total = total + jnp.dot(block, middle, preferred_element_type=jnp.float32)
+        total = total + jnp.dot(block, high, preferred_element_type=jnp.float32)
+        basis_out[at, :] = total.astype(basis_out.dtype)
+
+
+def rotated(summed_gram, total_frames, prior_sigma, start_rotation, coeffs, basis):
+    rows, size = basis.shape
+    chunk = 512 if rows % 512 == 0 else rows
+    new_basis, new_coeffs, new_sigma = pl.pallas_call(
+        functools.partial(rotate_kernel, total_frames, chunk),
+        out_shape=(
+            jax.ShapeDtypeStruct(basis.shape, basis.dtype),
+            jax.ShapeDtypeStruct(coeffs.shape, coeffs.dtype),
+            jax.ShapeDtypeStruct((1, size), jnp.float32),
+        ),
+        compiler_params=pltpu.CompilerParams(vmem_limit_bytes=32 * 1024 * 1024),
+        name="orthogonal_iteration",
+    )(summed_gram, prior_sigma.reshape(1, size), start_rotation, coeffs, basis)
+    return (new_basis, new_coeffs, new_sigma.reshape(size))
 
 
 def body(raw_frames, dark_frame, dead_mask, frame_group, prior_sigma, start_rotation, basis):
@@ -69,18 +182,8 @@
     coeffs = lax.psum(partial_value, "strips")
     total_frames = frame_count * lax.axis_size("frames")
     local_gram = jnp.dot(coeffs.T, coeffs, precision=lax.Precision.HIGHEST)
-    summed_gram = lax.psum(local_gram, "frames")
-    gram = jnp.diag(prior_sigma * prior_sigma) + summed_gram / total_frames
-    rotation = start_rotation
-    for step in range(ITERS):
-        rotation = orthonormalize(jnp.dot(gram, rotation, precision=lax.Precision.HIGHEST))
-    new_coeffs = jnp.dot(coeffs, rotation, precision=lax.Precision.HIGHEST)
-    new_basis = jnp.dot(
-        basis.astype(jnp.float32), rotation, precision=lax.Precision.HIGHEST
-    ).astype(jnp.bfloat16)
-    curved = jnp.dot(gram, rotation, precision=lax.Precision.HIGHEST)
-    new_sigma = jnp.sqrt(jnp.sum(rotation * curved, axis=0))
-    return (new_basis, new_coeffs, new_sigma)
+    summed_gram = summed_over(local_gram, "frames")
+    return rotated(summed_gram, total_frames, prior_sigma, start_rotation, coeffs, basis)
 
 
 def solution(mesh):

time: 609 us -> 459 us (0.75)
  other arithmetic: 175 us -> 83 us
  waiting for transfers between devices: 330 us -> 243 us
  Pallas kernels: 0 us -> 46.3 us
  matrix products: 52 us -> 39.5 us
    psum x1 -> x0, waiting for transfers between devices: 100 us -> none  [body(): summed_gram = lax.psum(local_gram, 'frames')]
    another operation x20 -> x0, other arithmetic: 91.9 us -> none  [the longest x12 49.6 us: orthonormalize(): factor = jnp.linalg.cholesky(normal)]
    pallas_call x0 -> x1, Pallas kernels: none -> 46.3 us  [rotated(): pl.pallas_call(functools.partial(rotate_kernel, total_frames, chunk), out...]
    ppermute x0 -> x4, waiting for transfers between devices: none -> 13.5 us  [summed_over(): values = values + lax.ppermute(values, axis, pairs)]
    dot_general x11 -> x0, matrix products: 10.8 us -> none  [the longest x4 4.52 us: body(): jnp.dot(gram, rotation, precision=lax.Precision.HIGHEST)]
    unnamed x10 -> x9, local copies, waits for them, and re-layouts: 22.5 us -> 18.4 us
  transfers between devices with their start and end apart: 4 -> 7, of which waited for: 3 -> 6; matrix products, arithmetic and copies ran while one was open for 21% -> 27% of each run, Pallas kernels for 0% -> 0%
where the time goes in v1:
time: 459 us; the launch traced here: 458 us
  waiting for transfers between devices  243 us (53%)
  other arithmetic  83 us (18%)
  Pallas kernels  46.3 us (10%)
  matrix products  39.5 us (9%)
  local copies, waits for them, and re-layouts  20.2 us (4%)
  between operations  14.2 us (3%)
  starting transfers between devices  8.87 us (2%)
    all_gather x1, waiting for transfers between devices, body(): lax.all_gather(basis, 'frames', axis=0, tiled=True)  226 us
    convert_element_type x1, other arithmetic, body(): weighted = (frame_weight[:, None, None] * row_blur).astype(jnp.bfloat16)....  81.8 us
    pallas_call x1, Pallas kernels, rotated(): pl.pallas_call(functools.partial(rotate_kernel, total_frames, chunk), out...  46.3 us
    dot_general x1, matrix products, body(): jnp.dot(corrected.reshape(frame_count * strip_rows, columns), banded, pre...  20.7 us
    dot_general x1, matrix products, body(): jnp.dot(weighted, lax.all_gather(basis, 'frames', axis=0, tiled=True), pr...  18.5 us
    unnamed x9, local copies, waits for them, and re-layouts  18.4 us
    ppermute x4, waiting for transfers between devices, summed_over(): values = values + lax.ppermute(values, axis, pairs)  13.5 us
  transfers between devices with their start and end apart: 7, of which 6 were waited for; matrix products, arithmetic and copies ran while one was open for 27% of the time, Pallas kernels for 0%

profile of v1, /device:TPU:0, one launch (start us, length us, event | category | flops | bytes accessed | tf_op | source)
XLA Modules:
  0.0 458.4 jit_solution(1244383065437918468)
XLA Ops:
  7.2 0.0 all-gather.2.cloned.1.call-start
  7.2 0.7 all-gather.2.cloned.1.call-update
  7.9 1.1 subtract_convert_fusion
  9.0 0.0 copy-start.3
  9.0 20.7 %fusion.18 = f32[64,256,512]{2,1,0:T(8,128)} fusion(bf16[64,256,512]{2,1,0:T(8,128)(2,1)} %param.7, f32[256,512]{1,0:T(8,128)S(1)} %subtract_convert_fusion, f32[256,512]{1,0:T(8,128)} %param.8), kind=kOutput, calls=%fused_computation.25 | convolution fusion | flops 8629256192 | bytes 51380224 | tf_op jit(solution)/shard_map/dot_general | solution.py:159
  29.8 1.8 fusion.54
  31.5 2.4 collective-permute-start
  34.0 1.5 collective-permute-start.1
  35.4 0.0 copy-done.3
  35.5 0.0 collective-permute-done
  35.5 2.3 collective-permute-done.1
  37.8 81.8 %fusion.5 = bf16[64,256,512]{2,1,0:T(8,128)(2,1)} fusion(f32[64,3,512]{2,1,0:T(4,128)S(1)} %collective-permute-done.1, f32[64,3,512]{2,1,0:T(4,128)S(1)} %collective-permute-done, f32[64,256,512]{2,1,0:T(8,128)} %fusion.18, f32[64]{0:T(128)S(1)} %convert_power_fusion), kind=kLoop, calls=%fused_computation.9 | loop fusion | flops 176160768 | bytes 51118336 | tf_op jit(solution)/shard_map/convert_element_type | solution.py:174
  119.6 18.4 %copy.10 = bf16[8,8,256,512]{3,1,2,0:T(8,128)(2,1)} copy(bf16[8,8,256,512]{3,2,1,0:T(8,128)(2,1)} %bitcast.13) | data formatting | bytes 33554432
  138.0 0.0 copy-start
  138.0 0.0 copy-start.1
  138.0 0.0 copy-start.2
  138.0 226.3 %all-gather.2.cloned.1.call-done = bf16[131072,128]{1,0:T(8,128)(2,1)} async-done(((bf16[8192,128]{1,0:T(8,128)(2,1)}), bf16[131072,128]{1,0:T(8,128)(2,1)}) %all-gather.2.cloned.1.call-update) | async-done | bytes 33554448 | tf_op jit(solution)/shard_map/all_gather | solution.py:179
  364.4 18.5 %fusion.55 = f32[64,128]{1,0:T(8,128)S(1)} fusion(bf16[64,131072]{1,0:T(8,128)(2,1)} %bitcast.12, bf16[131072,128]{1,0:T(8,128)(2,1)} %all-gather.2.cloned.1.call-done), kind=kOutput, calls=%fused_computation.65 | convolution fusion | flops 2147483648 | bytes 50364416 | tf_op jit(solution)/shard_map/dot_general | solution.py:177
  382.8 3.6 psum.7.coeffs_ref
  386.5 0.3 fusion.56
  386.8 1.3 collective-permute-start.2
  388.1 3.1 collective-permute-done.2
  391.2 1.5 collective-permute-start.3
  392.7 2.8 collective-permute-done.3
  395.5 0.1 collective-permute-start.4
  395.6 4.3 collective-permute-done.4
  399.9 2.0 collective-permute-start.5
  401.9 3.4 collective-permute-done.5
  405.3 0.0 copy-done
  405.3 0.0 copy-done.1
  405.3 0.0 copy-done.2
  405.3 46.3 %orthogonal_iteration.1 = (bf16[8192,128]{1,0:T(8,128)(2,1)}, f32[64,128]{1,0:T(8,128)}, f32[1,128]{1,0:T(1,128)}) custom-call(f32[128,128]{1,0:T(8,128)S(1)} %add.65.summed_ref, f32[1,128]{1,0:T(1,128)S(1)} %bitcast.11, f32[128,128]{1,0:T(8,128)S(1)} %copy-done.1, f32[64,128]{1,0:T(8,128)S(1)} %psum.7.coeffs_ref, bf16[8192,128]{1,0:T(8,128)(2,1)S(1)} %copy-done), custom_call_target="tpu_custom_call" | custom-call | tf_op jit(solution)/shard_map/orthogonal_iteration/pallas_call | solution.py:135
  (5 shorter events, 0.0 us)
Async XLA Ops:
  7.2 357.2 %all-gather.2.cloned.1.call-start = ((), (), s32[]{:S(2)}) async-start(), calls=%async_computation | async-start | bytes 35651584 | tf_op jit(solution)/shard_map/all_gather | solution.py:179
  9.0 26.4 %copy-start.3 = (s32[64]{0:T(128)S(1)}, s32[64]{0:T(128)}, u32[]{:S(2)}) copy-start(s32[64]{0:T(128)} %param.10) | copy-start | bytes 772
  31.5 3.9 collective-permute-start
  34.0 3.8 collective-permute-start.1
  138.0 267.2 %copy-start = (bf16[8192,128]{1,0:T(8,128)(2,1)S(1)}, bf16[8192,128]{1,0:T(8,128)(2,1)}, u32[]{:S(2)}) copy-start(bf16[8192,128]{1,0:T(8,128)(2,1)} %basis_ref.1) | copy-start | bytes 6291460
  138.0 267.3 %copy-start.1 = (f32[128,128]{1,0:T(8,128)S(1)}, f32[128,128]{1,0:T(8,128)}, u32[]{:S(2)}) copy-start(f32[128,128]{1,0:T(8,128)} %start_ref.1) | copy-start | bytes 196612
  138.0 267.3 %copy-start.2 = (f32[128]{0:T(128)S(1)}, f32[128]{0:T(128)}, u32[]{:S(2)}) copy-start(f32[128]{0:T(128)} %param.11) | copy-start | bytes 1540
  386.8 4.4 collective-permute-start.2
  391.2 4.3 collective-permute-start.3
  395.5 4.3 collective-permute-start.4
  399.9 5.4 %collective-permute-start.5 = (f32[128,128]{1,0:T(8,128)S(1)}, f32[128,128]{1,0:T(8,128)S(1)}, u32[]{:S(2)}, u32[]{:S(2)}) collective-permute-start(f32[128,128]{1,0:T(8,128)S(1)} %add.64), channel_id=1, source_target_pairs={{0,16},{2,18},{4,20},{6,22},{8,24},{10,26},{12,28},{14,30},{16,0},... | collective-permute-start | bytes 196616 | tf_op jit(solution)/shard_map/ppermute | solution.py:40
Sparse Core Ops, SparseCore 0:
  10.8 353.5 all-gather.1

commit v2 on v1

--- a/solution.py
+++ b/solution.py
@@ -145,7 +145,7 @@
     return (new_basis, new_coeffs, new_sigma.reshape(size))
 
 
-def body(raw_frames, dark_frame, dead_mask, frame_group, prior_sigma, start_rotation, basis):
+def gathered_body(raw_frames, dark_frame, dead_mask, frame_group, prior_sigma, start_rotation, basis):
     frame_count, strip_rows, columns = raw_frames.shape
     corrected = (
         (raw_frames.astype(jnp.float32) - dark_frame) * (1 - dead_mask).astype(jnp.float32)
@@ -186,6 +186,234 @@
     return rotated(summed_gram, total_frames, prior_sigma, start_rotation, coeffs, basis)
 
 
+RING = (0, 2, 4, 6, 7, 5, 3, 1)
+BAND = 16
+EDGE = 8
+FRAME_BLOCK = 16
+
+
+def blur_kernel(place_ref, main_ref, prev_ref, next_ref, before_ref, after_ref, dark_ref, keep_ref, banded_ref, weight_ref,
+                send_ref, own_ref, rows_ref, lines_ref, blurred_ref):
+    pair, side = (place_ref[0], place_ref[1])
+    frames, height, columns = main_ref.shape
+    span = height + 2 * EDGE
+    at = pl.ds(pl.multiple_of(pair * height + BAND - EDGE, EDGE), span)
+    dark = dark_ref[at, :]
+    keep = keep_ref[at, :]
+    top = jnp.where(pair == 0, before_ref[...], prev_ref[...]).astype(jnp.float32)[:, BAND - EDGE :]
+    bottom = jnp.where(place_ref[2] == 1, after_ref[...], next_ref[...]).astype(jnp.float32)[:, :EDGE]
+    main = (main_ref[...].astype(jnp.float32) - dark[EDGE : EDGE + height]) * keep[EDGE : EDGE + height]
+    top = (top - dark[:EDGE]) * keep[:EDGE]
+    bottom = (bottom - dark[EDGE + height :]) * keep[EDGE + height :]
+    tiles = columns // 128
+    flat_ref = rows_ref.reshape(tiles * frames * span, 128)
+    for tile in range(tiles):
+        part = slice(tile * 128, (tile + 1) * 128)
+        rows_ref[tile, :, :EDGE] = top[:, :, part]
+        rows_ref[tile, :, EDGE : EDGE + height] = main[:, :, part]
+        rows_ref[tile, :, EDGE + height :] = bottom[:, :, part]
+        for row in range(height + 6):
+            line = flat_ref[pl.ds(tile * frames * span + row + EDGE - 3, frames, stride=span), :]
+            lines_ref[row * frames : (row + 1) * frames, part] = line.astype(jnp.bfloat16)
+    blurred_ref[...] = jnp.dot(lines_ref[...], banded_ref[...], preferred_element_type=jnp.float32)
+    weight = jnp.broadcast_to(weight_ref[:, :1], (frames, columns))
+    for out_ref, first in ((send_ref, (1 - side) * BAND), (own_ref, side * BAND)):
+        for row in range(BAND):
+            parts = [
+                blurred_ref[pl.ds(pl.multiple_of((first + row + offset) * frames, frames), frames), :]
+                for offset in range(7)
+            ]
+            total = BLUR_TAPS[3] * parts[3]
+            for offset in range(3):
+                total = total + BLUR_TAPS[offset] * (parts[offset] + parts[6 - offset])
+            out_ref[row] = (weight * total).astype(jnp.bfloat16)
+
+
+def blurred_bands(place, raw_frames, before, after, dark, keep, banded, weight):
+    frame_count, strip_rows, columns = raw_frames.shape
+    bands = strip_rows // BAND
+    height = 2 * BAND
+    fixed = lambda f, place: (0, 0)
+    grid_spec = pltpu.PrefetchScalarGridSpec(
+        num_scalar_prefetch=1,
+        grid=(frame_count // FRAME_BLOCK,),
+        in_specs=[
+            pl.BlockSpec((FRAME_BLOCK, height, columns), lambda f, place: (f, place[0], 0)),
+            pl.BlockSpec((FRAME_BLOCK, BAND, columns), lambda f, place: (f, jnp.maximum(2 * place[0] - 1, 0), 0)),
+            pl.BlockSpec((FRAME_BLOCK, BAND, columns), lambda f, place: (f, jnp.minimum(2 * place[0] + 2, bands - 1), 0)),
+            pl.BlockSpec((FRAME_BLOCK, BAND, columns), lambda f, place: (f, 0, 0)),
+            pl.BlockSpec((FRAME_BLOCK, BAND, columns), lambda f, place: (f, 0, 0)),
+            pl.BlockSpec(dark.shape, fixed),
+            pl.BlockSpec(keep.shape, fixed),
+            pl.BlockSpec(banded.shape, fixed),
+            pl.BlockSpec((FRAME_BLOCK, weight.shape[1]), lambda f, place: (f, 0)),
+        ],
+        out_specs=[pl.BlockSpec((BAND, FRAME_BLOCK, columns), lambda f, place: (0, f, 0))] * 2,
+        scratch_shapes=[
+            pltpu.VMEM((columns // 128, FRAME_BLOCK, height + 2 * EDGE, 128), jnp.float32),
+            pltpu.VMEM(((height + 6) * FRAME_BLOCK, columns), jnp.bfloat16),
+            pltpu.VMEM(((height + 6) * FRAME_BLOCK, columns), jnp.float32),
+        ],
+    )
+    shape = jax.ShapeDtypeStruct((BAND, frame_count, columns), jnp.bfloat16)
+    return pl.pallas_call(
+        blur_kernel,
+        grid_spec=grid_spec,
+        out_shape=(shape, shape),
+        compiler_params=pltpu.CompilerParams(vmem_limit_bytes=32 * 1024 * 1024),
+        cost_estimate=pl.CostEstimate(
+            flops=2 * frame_count * height * columns * columns, bytes_accessed=8 * frame_count * height * columns,
+            transcendentals=0,
+        ),
+        name="blur_bands",
+    )(place, raw_frames, raw_frames, raw_frames, before, after, dark, keep, banded, weight)
+
+
+def project_kernel(total_ref, own_ref, came_ref, basis_ref, out_ref):
+    columns = own_ref.shape[2]
+
+    @pl.when(pl.program_id(0) == 0)
+    def _():
+        out_ref[...] = total_ref[...]
+
+    total = out_ref[...]
+    for row in range(own_ref.shape[0]):
+        lines = jnp.concatenate([own_ref[row], came_ref[row]], axis=0)
+        total = total + jnp.dot(
+            lines, basis_ref[row * columns : (row + 1) * columns, :], preferred_element_type=jnp.float32
+        )
+    out_ref[...] = total
+
+
+def projected(total, own, came, basis, first_row):
+    step = 4
+    _, frame_count, columns = own.shape
+    size = basis.shape[1]
+    skipped = first_row // step
+    steps = basis.shape[0] // columns // step
+    lines = pl.BlockSpec((step, frame_count, columns), lambda i: (i + skipped, 0, 0))
+    whole = pl.BlockSpec(total.shape, lambda i: (0, 0))
+    return pl.pallas_call(
+        project_kernel,
+        grid=(steps,),
+        in_specs=[whole, lines, lines, pl.BlockSpec((step * columns, size), lambda i: (i, 0))],
+        out_specs=whole,
+        out_shape=jax.ShapeDtypeStruct(total.shape, jnp.float32),
+        compiler_params=pltpu.CompilerParams(vmem_limit_bytes=32 * 1024 * 1024),
+        cost_estimate=pl.CostEstimate(
+            flops=4 * frame_count * basis.shape[0] * size, bytes_accessed=4 * own.size + 2 * basis.size, transcendentals=0
+        ),
+        name="project_band",
+    )(total, own, came, basis)
+
+
+def paired_body(raw_frames, dark_frame, dead_mask, frame_group, prior_sigma, start_rotation, basis):
+    frame_count, strip_rows, columns = raw_frames.shape
+    size = basis.shape[1]
+    count = lax.axis_size("frames")
+    strips = lax.axis_size("strips")
+    ring = len(RING)
+    index = lax.axis_index("frames")
+    side = index % 2
+    position = jnp.array([RING.index(pair) for pair in range(ring)], jnp.int32)[index // 2]
+    pair_at = jnp.array(RING, jnp.int32)
+
+    def links(by):
+        return [
+            (2 * RING[at] + x, 2 * RING[(at + by) % ring] + x) for at in range(ring) for x in range(2)
+        ]
+
+    swap = [(i, i ^ 1) for i in range(count)]
+    ahead = [(i, i + 1) for i in range(strips - 1)]
+    back = [(i + 1, i) for i in range(strips - 1)]
+    move = lambda values, pairs: lax.ppermute(values, "frames", pairs)
+    before = lax.ppermute(raw_frames[:, strip_rows - BAND :], "strips", ahead)
+    after = lax.ppermute(raw_frames[:, :BAND], "strips", back)
+    keep_frame = (1 - dead_mask).astype(jnp.float32)
+    both = jnp.concatenate([dark_frame, keep_frame], axis=1)
+    edge_before = lax.ppermute(both[strip_rows - BAND :], "strips", ahead)
+    edge_after = lax.ppermute(both[:BAND], "strips", back)
+    both = jnp.concatenate([edge_before, both, edge_after], axis=0)
+    dark, keep = (both[:, :columns], both[:, columns:])
+    column = jnp.arange(columns)
+    offsets = column[None, :] - column[:, None]
+    banded = jnp.zeros((columns, columns), jnp.float32)
+    for shift_by in range(-3, 4):
+        banded = banded + jnp.where(offsets == shift_by, BLUR_TAPS[shift_by + 3], 0.0)
+    banded = banded.astype(jnp.bfloat16)
+    frame_weight = jnp.power(jnp.float32(DECAY_RATE), (GROUPS - 1 - frame_group).astype(jnp.float32))
+    weight = jnp.broadcast_to(frame_weight[:, None], (frame_count, 128))
+
+    def bands(offset):
+        pair = pair_at[(position + offset) % ring]
+        place = jnp.stack([pair, side, (pair == ring - 1).astype(jnp.int32)]).astype(jnp.int32)
+        return blurred_bands(place, raw_frames, before, after, dark, keep, banded, weight)
+
+    order = (0, -1, 1, -2, 2, -3, 3, 4)
+    half = basis.shape[0] // 2
+    blocks = {0: (basis,)}
+    own, send, came = ([], [], [])
+    total = jnp.zeros((2 * frame_count, size), jnp.float32)
+    up, down = (basis, basis)
+    used = 0
+
+    def project(total, slot):
+        row = 0
+        for block in blocks[order[slot]]:
+            total = projected(total, own[slot], came[slot], block, row)
+            row += block.shape[0] // columns
+        return total
+
+    for stage in range(4):
+        if stage < 3:
+            up, down = (move(up, links(1)), move(down, links(-1)))
+        else:
+            up, down = (move(up[:half], links(1)), move(down[half:], links(-1)))
+        for slot in (2 * stage, 2 * stage + 1):
+            if slot >= len(own):
+                sent, kept = bands(order[slot])
+                own.append(kept)
+                send.append(sent)
+            came.append(move(send[slot], swap))
+        while stage < 2 and len(own) < (4, 8)[stage]:
+            sent, kept = bands(order[len(own)])
+            own.append(kept)
+            send.append(sent)
+        if stage > 0:
+            for slot in (2 * stage - 2, 2 * stage - 1):
+                total = project(total, slot)
+        last = 2 * stage
+        held = (up, down, total, came[last], came[last + 1]) + tuple(send[last + 2 :]) + tuple(own[last + 2 :])
+        up, down, total, came[last], came[last + 1], *others = lax.optimization_barrier(held)
+        waiting = len(send) - last - 2
+        send[last + 2 :] = others[:waiting]
+        own[last + 2 :] = others[waiting:]
+        if stage < 3:
+            blocks[-stage - 1], blocks[stage + 1] = ((up,), (down,))
+        else:
+            blocks[4] = (up, down)
+    for slot in (6, 7):
+        total = project(total, slot)
+    total = total + lax.ppermute(total, "strips", [(i, i ^ 1) for i in range(strips)])
+    other = move(total, swap)
+    mine = total[:frame_count] + other[frame_count:]
+    theirs = total[frame_count:] + other[:frame_count]
+    gram = jnp.dot(mine.T, mine, precision=HIGHEST) + jnp.dot(theirs.T, theirs, precision=HIGHEST)
+    distance = 2
+    while distance < count:
+        gram = gram + move(gram, [(i, i ^ distance) for i in range(count)])
+        distance *= 2
+    return rotated(gram, frame_count * count, prior_sigma, start_rotation, mine, basis)
+
+
+def body(raw_frames, *others):
+    _, strip_rows, columns = raw_frames.shape
+    paired = lax.axis_size("frames") == 2 * len(RING) and lax.axis_size("strips") == 2
+    if paired and strip_rows == 2 * len(RING) * BAND and raw_frames.shape[0] % FRAME_BLOCK == 0:
+        return paired_body(raw_frames, *others)
+    return gathered_body(raw_frames, *others)
+
+
 def solution(mesh):
     placed = (
         P("frames", "strips", None),

time: 459 us -> 303 us (0.66)
  waiting for transfers between devices: 243 us -> 101 us
  other arithmetic: 83 us -> 6.86 us
  Pallas kernels: 46.3 us -> 115 us
  matrix products: 39.5 us -> 0.57 us
  starting transfers between devices: 8.87 us -> 32.7 us
  local copies, waits for them, and re-layouts: 20.2 us -> 32.8 us
    all_gather x1 -> x0, waiting for transfers between devices: 226 us -> none  [body(): lax.all_gather(basis, 'frames', axis=0, tiled=True)]
    ppermute x6 -> x25, waiting for transfers between devices: 15.8 us -> 101 us  [the longest x20 99.7 us: paired_body(): move = lambda values, pairs: lax.ppermute(values, 'frames', pairs)]
    convert_element_type x2, other arithmetic: 82.9 us -> 0.26 us  [the longest x1 0.21 us: paired_body(): banded = banded.astype(jnp.bfloat16)]
    pallas_call x0 -> x17, Pallas kernels: none -> 68.7 us  [the longest x8 53.5 us: blurred_bands(): pl.pallas_call(blur_kernel, grid_spec=grid_spec, out_shape=(shape, shape)...]
    dot_general x3 -> x2, matrix products: 39.5 us -> 0.57 us  [the longest x1 0.29 us: paired_body(): jnp.dot(mine.T, mine, precision=HIGHEST)]
    ppermute x6 -> x25, starting transfers between devices: 8.83 us -> 32.7 us  [the longest x20 25.5 us: paired_body(): move = lambda values, pairs: lax.ppermute(values, 'frames', pairs)]
    unnamed x9 -> x70, local copies, waits for them, and re-layouts: 18.4 us -> 28.1 us
    another operation x0 -> x4, other arithmetic: none -> 5.41 us  [bands(): jnp.stack([pair, side, (pair == ring - 1).astype(jnp.int32)])]
  transfers between devices with their start and end apart: 7 -> 25, of which waited for: 6 -> 13; matrix products, arithmetic and copies ran while one was open for 27% -> 4% of each run, Pallas kernels for 0% -> 22%
where the time goes in v2:
time: 303 us; the launch traced here: 302 us
  Pallas kernels  115 us (38%)
  waiting for transfers between devices  101 us (33%)
  local copies, waits for them, and re-layouts  32.8 us (11%)
  starting transfers between devices  32.7 us (11%)
  between operations  13 us (4%)
  other arithmetic  6.86 us (2%)
    ppermute x20, waiting for transfers between devices, paired_body(): move = lambda values, pairs: lax.ppermute(values, 'frames', pairs)  99.7 us
    pallas_call x8, Pallas kernels, blurred_bands(): pl.pallas_call(blur_kernel, grid_spec=grid_spec, out_shape=(shape, shape)...  53.5 us
    pallas_call x1, Pallas kernels, rotated(): pl.pallas_call(functools.partial(rotate_kernel, total_frames, chunk), out...  46.3 us
    unnamed x70, local copies, waits for them, and re-layouts  28.1 us
    ppermute x20, starting transfers between devices, paired_body(): move = lambda values, pairs: lax.ppermute(values, 'frames', pairs)  25.5 us
    pallas_call x9, Pallas kernels, projected(): pl.pallas_call(project_kernel, grid=(steps,), in_specs=[whole, lines, lin...  15.2 us
  transfers between devices with their start and end apart: 25, of which 13 were waited for; matrix products, arithmetic and copies ran while one was open for 4% of the time, Pallas kernels for 22%

profile of v2, /device:TPU:0, one launch (start us, length us, event | category | flops | bytes accessed | tf_op | source)
XLA Modules:
  0.0 302.3 jit_solution(10556058377527480160)
XLA Ops:
  0.7 3.0 collective-permute-start.1
  3.8 3.1 %fusion.9 = (bf16[64,16,512]{2,1,0:T(8,128)(2,1)}, bf16[64,16,512]{2,1,0:T(8,128)(2,1)}) fusion(bf16[64,256,512]{2,1,0:T(8,128)(2,1)} %next_ref.15), kind=kLoop, calls=%fused_computation.27 | loop fusion | bytes 4194304 | tf_op jit(solution)/shard_map/slice | solution.py:331
  6.9 1.4 collective-permute-start.3
  8.3 3.2 %collective-permute-start.2 = (bf16[64,16,512]{2,1,0:T(8,128)(2,1)}, bf16[64,16,512]{2,1,0:T(8,128)(2,1)S(1)}, u32[]{:S(2)}, u32[]{:S(2)}) collective-permute-start(bf16[64,16,512]{2,1,0:T(8,128)(2,1)} %get-tuple-element.114), channel_id=1, source_target_pairs={{0,1},{2,3},{4,5},{6,7},{8,9},{10,11},{12,13},{14,15},{16,17},{18,... | collective-permute-start | bytes 3145736 | tf_op jit(solution)/shard_map/ppermute | solution.py:330
  11.5 1.3 collective-permute-start.4
  22.4 1.3 collective-permute-start.5
  23.7 1.4 pad_add_fusion
  26.9 5.8 %copy-done = bf16[64,256,512]{2,1,0:T(8,128)(2,1)S(1)} copy-done((bf16[64,256,512]{2,1,0:T(8,128)(2,1)S(1)}, bf16[64,256,512]{2,1,0:T(8,128)(2,1)}, u32[]{:S(2)}) %copy-start) | copy-done | bytes 16777240
  32.6 6.5 %blur_bands.9 = (bf16[16,64,512]{2,1,0:T(8,128)(2,1)S(1)}, bf16[16,64,512]{2,1,0:T(8,128)(2,1)S(1)}) custom-call(s32[3]{0:T(128)S(1)} %get-tuple-element.128.place_ref, bf16[64,256,512]{2,1,0:T(8,128)(2,1)S(1)} %copy-done, bf16[64,256,512]{2,1,0:T(8,128)(2,1)S(1)} %copy-done, bf16[64,256,512]{2,1,0:T(8,128)(2,1)S(1)} %copy-done, ...), custom_call_target="tpu_custom_call" | custom-call | flops 1073741824 | bytes 8388608 | tf_op jit(solution)/shard_map/blur_bands/pallas_call | solution.py:259
  39.2 1.9 collective-permute-start.7
  41.1 5.8 %copy-done.1 = bf16[64,256,512]{2,1,0:T(8,128)(2,1)S(1)} copy-done((bf16[64,256,512]{2,1,0:T(8,128)(2,1)S(1)}, bf16[64,256,512]{2,1,0:T(8,128)(2,1)}, u32[]{:S(2)}) %copy-start.1) | copy-done | bytes 16777240
  46.9 6.5 %blur_bands.8 = (bf16[16,64,512]{2,1,0:T(8,128)(2,1)S(1)}, bf16[16,64,512]{2,1,0:T(8,128)(2,1)S(1)}) custom-call(s32[3]{0:T(128)S(1)} %get-tuple-element.127.place_ref, bf16[64,256,512]{2,1,0:T(8,128)(2,1)S(1)} %copy-done.1, bf16[64,256,512]{2,1,0:T(8,128)(2,1)S(1)} %copy-done.1, bf16[64,256,512]{2,1,0:T(8,128)(2,1)S(1)} %copy-done.1, ...), custom_call_target="tpu_custom_call" | custom-call | flops 1073741824 | bytes 8388608 | tf_op jit(solution)/shard_map/blur_bands/pallas_call | solution.py:259
  55.0 1.3 pad_add_fusion.2
  56.3 5.8 %copy-done.2 = bf16[64,256,512]{2,1,0:T(8,128)(2,1)S(1)} copy-done((bf16[64,256,512]{2,1,0:T(8,128)(2,1)S(1)}, bf16[64,256,512]{2,1,0:T(8,128)(2,1)}, u32[]{:S(2)}) %copy-start.2) | copy-done | bytes 16777240
  62.0 7.2 %blur_bands.11 = (bf16[16,64,512]{2,1,0:T(8,128)(2,1)}, bf16[16,64,512]{2,1,0:T(8,128)(2,1)S(1)}) custom-call(s32[3]{0:T(128)S(1)} %get-tuple-element.130.place_ref, bf16[64,256,512]{2,1,0:T(8,128)(2,1)S(1)} %copy-done.2, bf16[64,256,512]{2,1,0:T(8,128)(2,1)S(1)} %copy-done.2, bf16[64,256,512]{2,1,0:T(8,128)(2,1)S(1)} %copy-done.2, ...), custom_call_target="tpu_custom_call" | custom-call | flops 1073741824 | bytes 8388608 | tf_op jit(solution)/shard_map/blur_bands/pallas_call | solution.py:259
  69.2 7.2 %blur_bands.10 = (bf16[16,64,512]{2,1,0:T(8,128)(2,1)}, bf16[16,64,512]{2,1,0:T(8,128)(2,1)S(1)}) custom-call(s32[3]{0:T(128)S(1)} %get-tuple-element.129.place_ref, bf16[64,256,512]{2,1,0:T(8,128)(2,1)S(1)} %copy-done.2, bf16[64,256,512]{2,1,0:T(8,128)(2,1)S(1)} %copy-done.2, bf16[64,256,512]{2,1,0:T(8,128)(2,1)S(1)} %copy-done.2, ...), custom_call_target="tpu_custom_call" | custom-call | flops 1073741824 | bytes 8388608 | tf_op jit(solution)/shard_map/blur_bands/pallas_call | solution.py:259
  76.4 11.2 %collective-permute-done.6.came_ref = bf16[16,64,512]{2,1,0:T(8,128)(2,1)S(1)} collective-permute-done((bf16[16,64,512]{2,1,0:T(8,128)(2,1)S(1)}, bf16[16,64,512]{2,1,0:T(8,128)(2,1)S(1)}, u32[]{:S(2)}, u32[]{:S(2)}) %collective-permute-start.6) | collective-permute-done | bytes 1048608 | tf_op jit(solution)/shard_map/ppermute | solution.py:329
  88.6 1.8 collective-permute-start.8
  90.6 1.7 collective-permute-start.10
  95.3 1.3 pad_add_fusion.6
  96.6 1.4 pad_add_fusion.4
  98.0 6.5 %blur_bands.15 = (bf16[16,64,512]{2,1,0:T(8,128)(2,1)S(1)}, bf16[16,64,512]{2,1,0:T(8,128)(2,1)S(1)}) custom-call(s32[3]{0:T(128)S(1)} %get-tuple-element.134.place_ref, bf16[64,256,512]{2,1,0:T(8,128)(2,1)S(1)} %copy-done.2, bf16[64,256,512]{2,1,0:T(8,128)(2,1)S(1)} %copy-done.2, bf16[64,256,512]{2,1,0:T(8,128)(2,1)S(1)} %copy-done.2, ...), custom_call_target="tpu_custom_call" | custom-call | flops 1073741824 | bytes 8388608 | tf_op jit(solution)/shard_map/blur_bands/pallas_call | solution.py:259
  105.6 6.5 %blur_bands.14 = (bf16[16,64,512]{2,1,0:T(8,128)(2,1)S(1)}, bf16[16,64,512]{2,1,0:T(8,128)(2,1)S(1)}) custom-call(s32[3]{0:T(128)S(1)} %get-tuple-element.133.place_ref, bf16[64,256,512]{2,1,0:T(8,128)(2,1)S(1)} %copy-done.2, bf16[64,256,512]{2,1,0:T(8,128)(2,1)S(1)} %copy-done.2, bf16[64,256,512]{2,1,0:T(8,128)(2,1)S(1)} %copy-done.2, ...), custom_call_target="tpu_custom_call" | custom-call | flops 1073741824 | bytes 8388608 | tf_op jit(solution)/shard_map/blur_bands/pallas_call | solution.py:259
  114.2 6.5 %blur_bands.13 = (bf16[16,64,512]{2,1,0:T(8,128)(2,1)S(1)}, bf16[16,64,512]{2,1,0:T(8,128)(2,1)S(1)}) custom-call(s32[3]{0:T(128)S(1)} %get-tuple-element.132.place_ref, bf16[64,256,512]{2,1,0:T(8,128)(2,1)S(1)} %copy-done.2, bf16[64,256,512]{2,1,0:T(8,128)(2,1)S(1)} %copy-done.2, bf16[64,256,512]{2,1,0:T(8,128)(2,1)S(1)} %copy-done.2, ...), custom_call_target="tpu_custom_call" | custom-call | flops 1073741824 | bytes 8388608 | tf_op jit(solution)/shard_map/blur_bands/pallas_call | solution.py:259
  122.6 6.5 %blur_bands.12 = (bf16[16,64,512]{2,1,0:T(8,128)(2,1)S(1)}, bf16[16,64,512]{2,1,0:T(8,128)(2,1)S(1)}) custom-call(s32[3]{0:T(128)S(1)} %get-tuple-element.131.place_ref, bf16[64,256,512]{2,1,0:T(8,128)(2,1)S(1)} %copy-done.2, bf16[64,256,512]{2,1,0:T(8,128)(2,1)S(1)} %copy-done.2, bf16[64,256,512]{2,1,0:T(8,128)(2,1)S(1)} %copy-done.2, ...), custom_call_target="tpu_custom_call" | custom-call | flops 1073741824 | bytes 8388608 | tf_op jit(solution)/shard_map/blur_bands/pallas_call | solution.py:259
  132.4 1.2 copy-done.15
  135.2 3.2 %project_band.10.total_ref = f32[128,128]{1,0:T(8,128)S(1)} custom-call(f32[128,128]{1,0:T(8,128)S(1)} %project_band.9.total_ref, bf16[16,64,512]{2,1,0:T(8,128)(2,1)S(1)} %copy-done.9, bf16[16,64,512]{2,1,0:T(8,128)(2,1)S(1)} %copy-done.11, bf16[8192,128]{1,0:T(8,128)(2,1)} %collective-permute-done.basis_ref), custom_call_target="tpu_custom_call" | custom-call | flops 268435456 | bytes 4194304 | tf_op jit(solution)/shard_map/project_band/pallas_call | solution.py:296
  138.4 1.9 collective-permute-start.12
  140.5 1.7 collective-permute-start.14
  142.5 3.2 %project_band.11.total_ref = f32[128,128]{1,0:T(8,128)S(1)} custom-call(f32[128,128]{1,0:T(8,128)S(1)} %project_band.10.total_ref, bf16[16,64,512]{2,1,0:T(8,128)(2,1)S(1)} %copy-done.5, bf16[16,64,512]{2,1,0:T(8,128)(2,1)} %collective-permute-done.10.came_ref, bf16[8192,128]{1,0:T(8,128)(2,1)} %collective-permute-done.1.basis_ref), custom_call_target="tpu_custom_call" | custom-call | flops 268435456 | bytes 4194304 | tf_op jit(solution)/shard_map/project_band/pallas_call | solution.py:296
  145.7 2.8 project_band.12.total_ref
  148.6 18.0 %collective-permute-done.14.came_ref = bf16[16,64,512]{2,1,0:T(8,128)(2,1)S(1)} collective-permute-done((bf16[16,64,512]{2,1,0:T(8,128)(2,1)S(1)}, bf16[16,64,512]{2,1,0:T(8,128)(2,1)S(1)}, u32[]{:S(2)}, u32[]{:S(2)}) %collective-permute-start.14) | collective-permute-done | bytes 1048608 | tf_op jit(solution)/shard_map/ppermute | solution.py:329
  166.6 19.8 %collective-permute-done.15.came_ref = bf16[16,64,512]{2,1,0:T(8,128)(2,1)S(1)} collective-permute-done((bf16[16,64,512]{2,1,0:T(8,128)(2,1)S(1)}, bf16[16,64,512]{2,1,0:T(8,128)(2,1)S(1)}, u32[]{:S(2)}, u32[]{:S(2)}) %collective-permute-start.15) | collective-permute-done | bytes 1048608 | tf_op jit(solution)/shard_map/ppermute | solution.py:329
  186.6 1.6 collective-permute-start.17
  188.6 1.5 collective-permute-start.18
  193.1 16.0 %collective-permute-done.17.basis_ref = bf16[4096,128]{1,0:T(8,128)(2,1)S(1)} collective-permute-done((bf16[4096,128]{1,0:T(8,128)(2,1)S(1)}, bf16[4096,128]{1,0:T(8,128)(2,1)S(1)}, u32[]{:S(2)}, u32[]{:S(2)}) %collective-permute-start.17) | collective-permute-done | bytes 1048608 | tf_op jit(solution)/shard_map/ppermute | solution.py:329
  210.3 4.5 %collective-permute-done.18.came_ref = bf16[16,64,512]{2,1,0:T(8,128)(2,1)S(1)} collective-permute-done((bf16[16,64,512]{2,1,0:T(8,128)(2,1)S(1)}, bf16[16,64,512]{2,1,0:T(8,128)(2,1)S(1)}, u32[]{:S(2)}, u32[]{:S(2)}) %collective-permute-start.18) | collective-permute-done | bytes 1048608 | tf_op jit(solution)/shard_map/ppermute | solution.py:329
  214.7 18.4 %collective-permute-done.19.came_ref = bf16[16,64,512]{2,1,0:T(8,128)(2,1)S(1)} collective-permute-done((bf16[16,64,512]{2,1,0:T(8,128)(2,1)S(1)}, bf16[16,64,512]{2,1,0:T(8,128)(2,1)S(1)}, u32[]{:S(2)}, u32[]{:S(2)}) %collective-permute-start.19) | collective-permute-done | bytes 1048608 | tf_op jit(solution)/shard_map/ppermute | solution.py:329
  235.7 1.2 collective-permute-done.20
  236.9 1.5 collective-permute-start.21
  238.4 2.8 collective-permute-done.21
  241.8 1.5 collective-permute-start.22
  243.3 2.9 collective-permute-done.22
  246.2 1.6 collective-permute-start.23
  247.8 2.7 collective-permute-done.23
  250.5 3.2 %collective-permute-start.24 = (f32[128,128]{1,0:T(8,128)S(1)}, f32[128,128]{1,0:T(8,128)S(1)}, u32[]{:S(2)}, u32[]{:S(2)}) collective-permute-start(f32[128,128]{1,0:T(8,128)S(1)} %add.236), channel_id=1, source_target_pairs={{0,16},{2,18},{4,20},{6,22},{8,24},{10,26},{12,28},{14,30},{16,0},... | collective-permute-start | bytes 196616 | tf_op jit(solution)/shard_map/ppermute | solution.py:329
  253.8 2.2 collective-permute-done.24
  256.0 46.3 %orthogonal_iteration.1 = (bf16[8192,128]{1,0:T(8,128)(2,1)}, f32[64,128]{1,0:T(8,128)}, f32[1,128]{1,0:T(1,128)}) custom-call(f32[128,128]{1,0:T(8,128)S(1)} %add.237.summed_ref, f32[1,128]{1,0:T(1,128)S(1)} %bitcast.6, f32[128,128]{1,0:T(8,128)S(1)} %copy-done.20, f32[64,128]{1,0:T(8,128)S(1)} %slice_add_fusion.2.coeffs_ref, bf16[8192,128]{1,0:T(8,128)(2,1)S(1)} %copy-done.3), custom_call_target="tpu_custom_call" | custom-call | tf_op jit(solution)/shard_map/orthogonal_iteration/pallas_call | solution.py:135
  (114 shorter events, 23.3 us)
Async XLA Ops:
  0.6 10.8 %copy-start.31 = (s32[256,512]{1,0:T(8,128)S(1)}, s32[256,512]{1,0:T(8,128)}, u32[]{:S(2)}) copy-start(s32[256,512]{1,0:T(8,128)} %param.11) | copy-start | bytes 1572868
  0.6 10.9 %copy-start.30 = (f32[256,512]{1,0:T(8,128)S(1)}, f32[256,512]{1,0:T(8,128)}, u32[]{:S(2)}) copy-start(f32[256,512]{1,0:T(8,128)} %param.10) | copy-start | bytes 1572868
  0.7 88.0 %collective-permute-start.1 = (bf16[8192,128]{1,0:T(8,128)(2,1)}, bf16[8192,128]{1,0:T(8,128)(2,1)}, u32[]{:S(2)}, u32[]{:S(2)}) collective-permute-start(bf16[8192,128]{1,0:T(8,128)(2,1)} %basis_ref.3), channel_id=1, source_target_pairs={{0,4},{2,6},{8,0},{10,2},{16,8},{18,10},{24,16},{26,18},{28,24},{3... | collective-permute-start | bytes 6291464 | tf_op jit(solution)/shard_map/ppermute | solution.py:329
  3.7 84.9 %collective-permute-start = (bf16[8192,128]{1,0:T(8,128)(2,1)}, bf16[8192,128]{1,0:T(8,128)(2,1)}, u32[]{:S(2)}, u32[]{:S(2)}) collective-permute-start(bf16[8192,128]{1,0:T(8,128)(2,1)} %basis_ref.3), channel_id=1, source_target_pairs={{0,8},{2,10},{8,16},{10,18},{16,24},{18,26},{24,28},{26,30},{28,20... | collective-permute-start | bytes 6291464 | tf_op jit(solution)/shard_map/ppermute | solution.py:329
  6.9 6.0 %copy-start.33 = (s32[64]{0:T(128)S(1)}, s32[64]{0:T(128)}, u32[]{:S(2)}) copy-start(s32[64]{0:T(128)} %param.12) | copy-start | bytes 772
  6.9 6.3 %copy-start.34 = (s32[8]{0:T(128)S(1)}, s32[8]{0:T(128)}, u32[]{:S(2)}) copy-start(s32[8]{0:T(128)} %constant.115.clone) | copy-start | bytes 100
  6.9 13.5 %copy-start.32 = (s32[8]{0:T(128)S(1)}, s32[8]{0:T(128)}, u32[]{:S(2)}) copy-start(s32[8]{0:T(128)} %constant.116.clone) | copy-start | bytes 100
  6.9 19.9 %collective-permute-start.3 = (bf16[64,16,512]{2,1,0:T(8,128)(2,1)}, bf16[64,16,512]{2,1,0:T(8,128)(2,1)S(1)}, u32[]{:S(2)}, u32[]{:S(2)}) collective-permute-start(bf16[64,16,512]{2,1,0:T(8,128)(2,1)} %get-tuple-element.113), channel_id=1, source_target_pairs={{1,0},{3,2},{5,4},{7,6},{9,8},{11,10},{13,12},{15,14},{17,16},{19,... | collective-permute-start | bytes 3145736 | tf_op jit(solution)/shard_map/ppermute | solution.py:331
  8.3 18.5 %collective-permute-start.2 = (bf16[64,16,512]{2,1,0:T(8,128)(2,1)}, bf16[64,16,512]{2,1,0:T(8,128)(2,1)S(1)}, u32[]{:S(2)}, u32[]{:S(2)}) collective-permute-start(bf16[64,16,512]{2,1,0:T(8,128)(2,1)} %get-tuple-element.114), channel_id=1, source_target_pairs={{0,1},{2,3},{4,5},{6,7},{8,9},{10,11},{12,13},{14,15},{16,17},{18,... | collective-permute-start | bytes 3145736 | tf_op jit(solution)/shard_map/ppermute | solution.py:330
  11.5 10.8 %collective-permute-start.4 = (f32[16,1024]{1,0:T(8,128)S(1)}, f32[16,1024]{1,0:T(8,128)S(1)}, u32[]{:S(2)}, u32[]{:S(2)}) collective-permute-start(f32[16,1024]{1,0:T(8,128)S(1)} %get-tuple-element.117), channel_id=1, source_target_pairs={{0,1},{2,3},{4,5},{6,7},{8,9},{10,11},{12,13},{14,15},{16,17},{18,... | collective-permute-start | bytes 196616 | tf_op jit(solution)/shard_map/ppermute | solution.py:334
  22.4 3.1 %collective-permute-start.5 = (f32[16,1024]{1,0:T(8,128)S(1)}, f32[16,1024]{1,0:T(8,128)S(1)}, u32[]{:S(2)}, u32[]{:S(2)}) collective-permute-start(f32[16,1024]{1,0:T(8,128)S(1)} %get-tuple-element.118), channel_id=1, source_target_pairs={{1,0},{3,2},{5,4},{7,6},{9,8},{11,10},{13,12},{15,14},{17,16},{19,... | collective-permute-start | bytes 196616 | tf_op jit(solution)/shard_map/ppermute | solution.py:335
  26.9 5.8 %copy-start = (bf16[64,256,512]{2,1,0:T(8,128)(2,1)S(1)}, bf16[64,256,512]{2,1,0:T(8,128)(2,1)}, u32[]{:S(2)}) copy-start(bf16[64,256,512]{2,1,0:T(8,128)(2,1)} %next_ref.15) | copy-start | bytes 50331652
  39.2 14.3 %copy-start.8 = (bf16[16,64,512]{2,1,0:T(8,128)(2,1)}, bf16[16,64,512]{2,1,0:T(8,128)(2,1)S(1)}, u32[]{:S(2)}) copy-start(bf16[16,64,512]{2,1,0:T(8,128)(2,1)S(1)} %get-tuple-element.69.own_ref) | copy-start | bytes 3145732
  39.2 37.2 %collective-permute-start.7 = (bf16[16,64,512]{2,1,0:T(8,128)(2,1)S(1)}, bf16[16,64,512]{2,1,0:T(8,128)(2,1)S(1)}, u32[]{:S(2)}, u32[]{:S(2)}) collective-permute-start(bf16[16,64,512]{2,1,0:T(8,128)(2,1)S(1)} %get-tuple-element.59), channel_id=1, source_target_pairs={{0,2},{2,0},{4,6},{6,4},{8,10},{10,8},{12,14},{14,12},{16,18},{18,... | collective-permute-start | bytes 3145736 | tf_op jit(solution)/shard_map/ppermute | solution.py:329
  41.1 5.8 %copy-start.1 = (bf16[64,256,512]{2,1,0:T(8,128)(2,1)S(1)}, bf16[64,256,512]{2,1,0:T(8,128)(2,1)}, u32[]{:S(2)}) copy-start(bf16[64,256,512]{2,1,0:T(8,128)(2,1)} %next_ref.15) | copy-start | bytes 50331652
  53.4 15.8 %copy-start.12 = (bf16[16,64,512]{2,1,0:T(8,128)(2,1)}, bf16[16,64,512]{2,1,0:T(8,128)(2,1)S(1)}, u32[]{:S(2)}) copy-start(bf16[16,64,512]{2,1,0:T(8,128)(2,1)S(1)} %get-tuple-element.67.own_ref) | copy-start | bytes 3145732
  53.4 34.2 %collective-permute-start.6 = (bf16[16,64,512]{2,1,0:T(8,128)(2,1)S(1)}, bf16[16,64,512]{2,1,0:T(8,128)(2,1)S(1)}, u32[]{:S(2)}, u32[]{:S(2)}) collective-permute-start(bf16[16,64,512]{2,1,0:T(8,128)(2,1)S(1)} %get-tuple-element.58), channel_id=1, source_target_pairs={{0,2},{2,0},{4,6},{6,4},{8,10},{10,8},{12,14},{14,12},{16,18},{18,... | collective-permute-start | bytes 3145736 | tf_op jit(solution)/shard_map/ppermute | solution.py:329
  56.3 5.8 %copy-start.2 = (bf16[64,256,512]{2,1,0:T(8,128)(2,1)S(1)}, bf16[64,256,512]{2,1,0:T(8,128)(2,1)}, u32[]{:S(2)}) copy-start(bf16[64,256,512]{2,1,0:T(8,128)(2,1)} %next_ref.15) | copy-start | bytes 50331652
  76.4 28.2 %copy-start.4 = (bf16[16,64,512]{2,1,0:T(8,128)(2,1)}, bf16[16,64,512]{2,1,0:T(8,128)(2,1)S(1)}, u32[]{:S(2)}) copy-start(bf16[16,64,512]{2,1,0:T(8,128)(2,1)S(1)} %get-tuple-element.84.own_ref) | copy-start | bytes 3145732
  76.4 28.2 %copy-start.10 = (bf16[16,64,512]{2,1,0:T(8,128)(2,1)}, bf16[16,64,512]{2,1,0:T(8,128)(2,1)S(1)}, u32[]{:S(2)}) copy-start(bf16[16,64,512]{2,1,0:T(8,128)(2,1)S(1)} %collective-permute-done.7.came_ref) | copy-start | bytes 3145732
  88.6 49.8 %collective-permute-start.8 = (bf16[8192,128]{1,0:T(8,128)(2,1)}, bf16[8192,128]{1,0:T(8,128)(2,1)S(1)}, u32[]{:S(2)}, u32[]{:S(2)}) collective-permute-start(bf16[8192,128]{1,0:T(8,128)(2,1)} %collective-permute-done.basis_ref), channel_id=1, source_target_pairs={{0,8},{2,10},{8,16},{10,18},{16,24},{18,26},{24,28},{26,30},{28,20... | collective-permute-start | bytes 6291464 | tf_op jit(solution)/shard_map/ppermute | solution.py:329
  90.4 47.9 %collective-permute-start.9 = (bf16[8192,128]{1,0:T(8,128)(2,1)}, bf16[8192,128]{1,0:T(8,128)(2,1)S(1)}, u32[]{:S(2)}, u32[]{:S(2)}) collective-permute-start(bf16[8192,128]{1,0:T(8,128)(2,1)} %collective-permute-done.1.basis_ref), channel_id=1, source_target_pairs={{0,4},{2,6},{8,0},{10,2},{16,8},{18,10},{24,16},{26,18},{28,24},{3... | collective-permute-start | bytes 6291464 | tf_op jit(solution)/shard_map/ppermute | solution.py:329
  90.6 47.7 %collective-permute-start.10 = (bf16[16,64,512]{2,1,0:T(8,128)(2,1)}, bf16[16,64,512]{2,1,0:T(8,128)(2,1)}, u32[]{:S(2)}, u32[]{:S(2)}) collective-permute-start(bf16[16,64,512]{2,1,0:T(8,128)(2,1)} %get-tuple-element.71), channel_id=1, source_target_pairs={{0,2},{2,0},{4,6},{6,4},{8,10},{10,8},{12,14},{14,12},{16,18},{18,... | collective-permute-start | bytes 3145736 | tf_op jit(solution)/shard_map/ppermute | solution.py:329
  92.4 46.0 %collective-permute-start.11 = (bf16[16,64,512]{2,1,0:T(8,128)(2,1)}, bf16[16,64,512]{2,1,0:T(8,128)(2,1)}, u32[]{:S(2)}, u32[]{:S(2)}) collective-permute-start(bf16[16,64,512]{2,1,0:T(8,128)(2,1)} %get-tuple-element.72), channel_id=1, source_target_pairs={{0,2},{2,0},{4,6},{6,4},{8,10},{10,8},{12,14},{14,12},{16,18},{18,... | collective-permute-start | bytes 3145736 | tf_op jit(solution)/shard_map/ppermute | solution.py:329
  122.6 8.5 %copy-start.3 = (bf16[8192,128]{1,0:T(8,128)(2,1)S(1)}, bf16[8192,128]{1,0:T(8,128)(2,1)}, u32[]{:S(2)}) copy-start(bf16[8192,128]{1,0:T(8,128)(2,1)} %basis_ref.3) | copy-start | bytes 6291460
  135.2 5.3 %copy-start.29 = (bf16[16,64,512]{2,1,0:T(8,128)(2,1)S(1)}, bf16[16,64,512]{2,1,0:T(8,128)(2,1)}, u32[]{:S(2)}) copy-start(bf16[16,64,512]{2,1,0:T(8,128)(2,1)} %copy-done.28) | copy-start | bytes 3145732
  135.2 7.1 %copy-start.27 = (bf16[16,64,512]{2,1,0:T(8,128)(2,1)S(1)}, bf16[16,64,512]{2,1,0:T(8,128)(2,1)}, u32[]{:S(2)}) copy-start(bf16[16,64,512]{2,1,0:T(8,128)(2,1)} %copy-done.26) | copy-start | bytes 3145732
  135.2 7.3 %copy-start.5 = (bf16[16,64,512]{2,1,0:T(8,128)(2,1)S(1)}, bf16[16,64,512]{2,1,0:T(8,128)(2,1)}, u32[]{:S(2)}) copy-start(bf16[16,64,512]{2,1,0:T(8,128)(2,1)} %copy-done.4) | copy-start | bytes 3145732
  138.4 48.0 %collective-permute-start.12 = (bf16[8192,128]{1,0:T(8,128)(2,1)S(1)}, bf16[8192,128]{1,0:T(8,128)(2,1)S(1)}, u32[]{:S(2)}, u32[]{:S(2)}) collective-permute-start(bf16[8192,128]{1,0:T(8,128)(2,1)S(1)} %collective-permute-done.8.basis_ref), channel_id=1, source_target_pairs={{0,8},{2,10},{8,16},{10,18},{16,24},{18,26},{24,28},{26,30},{28,20... | collective-permute-start | bytes 6291464 | tf_op jit(solution)/shard_map/ppermute | solution.py:329
  140.3 46.1 %collective-permute-start.13 = (bf16[8192,128]{1,0:T(8,128)(2,1)S(1)}, bf16[8192,128]{1,0:T(8,128)(2,1)S(1)}, u32[]{:S(2)}, u32[]{:S(2)}) collective-permute-start(bf16[8192,128]{1,0:T(8,128)(2,1)S(1)} %collective-permute-done.9.basis_ref), channel_id=1, source_target_pairs={{0,4},{2,6},{8,0},{10,2},{16,8},{18,10},{24,16},{26,18},{28,24},{3... | collective-permute-start | bytes 6291464 | tf_op jit(solution)/shard_map/ppermute | solution.py:329
  140.5 26.1 %collective-permute-start.14 = (bf16[16,64,512]{2,1,0:T(8,128)(2,1)S(1)}, bf16[16,64,512]{2,1,0:T(8,128)(2,1)S(1)}, u32[]{:S(2)}, u32[]{:S(2)}) collective-permute-start(bf16[16,64,512]{2,1,0:T(8,128)(2,1)S(1)} %copy-done.29), channel_id=1, source_target_pairs={{0,2},{2,0},{4,6},{6,4},{8,10},{10,8},{12,14},{14,12},{16,18},{18,... | collective-permute-start | bytes 3145736 | tf_op jit(solution)/shard_map/ppermute | solution.py:329
  142.2 44.2 %collective-permute-start.15 = (bf16[16,64,512]{2,1,0:T(8,128)(2,1)S(1)}, bf16[16,64,512]{2,1,0:T(8,128)(2,1)S(1)}, u32[]{:S(2)}, u32[]{:S(2)}) collective-permute-start(bf16[16,64,512]{2,1,0:T(8,128)(2,1)S(1)} %copy-done.27), channel_id=1, source_target_pairs={{0,2},{2,0},{4,6},{6,4},{8,10},{10,8},{12,14},{14,12},{16,18},{18,... | collective-permute-start | bytes 3145736 | tf_op jit(solution)/shard_map/ppermute | solution.py:329
  148.6 40.1 %copy-start.25 = (bf16[16,64,512]{2,1,0:T(8,128)(2,1)S(1)}, bf16[16,64,512]{2,1,0:T(8,128)(2,1)}, u32[]{:S(2)}) copy-start(bf16[16,64,512]{2,1,0:T(8,128)(2,1)} %copy-done.24) | copy-start | bytes 3145732
  148.6 41.6 %copy-start.23 = (bf16[16,64,512]{2,1,0:T(8,128)(2,1)S(1)}, bf16[16,64,512]{2,1,0:T(8,128)(2,1)}, u32[]{:S(2)}) copy-start(bf16[16,64,512]{2,1,0:T(8,128)(2,1)} %copy-done.22) | copy-start | bytes 3145732
  148.6 42.1 %copy-start.19 = (bf16[16,64,512]{2,1,0:T(8,128)(2,1)S(1)}, bf16[16,64,512]{2,1,0:T(8,128)(2,1)}, u32[]{:S(2)}) copy-start(bf16[16,64,512]{2,1,0:T(8,128)(2,1)} %copy-done.18) | copy-start | bytes 3145732
  186.6 5.3 %copy-start.17 = (bf16[16,64,512]{2,1,0:T(8,128)(2,1)S(1)}, bf16[16,64,512]{2,1,0:T(8,128)(2,1)}, u32[]{:S(2)}) copy-start(bf16[16,64,512]{2,1,0:T(8,128)(2,1)} %copy-done.16) | copy-start | bytes 3145732
  186.6 22.6 %collective-permute-start.17 = (bf16[4096,128]{1,0:T(8,128)(2,1)S(1)}, bf16[4096,128]{1,0:T(8,128)(2,1)S(1)}, u32[]{:S(2)}, u32[]{:S(2)}) collective-permute-start(bf16[4096,128]{1,0:T(8,128)(2,1)S(1)} %slice.43), channel_id=1, source_target_pairs={{0,4},{2,6},{8,0},{10,2},{16,8},{18,10},{24,16},{26,18},{28,24},{3... | collective-permute-start | bytes 3145736 | tf_op jit(solution)/shard_map/ppermute | solution.py:329
  188.2 22.1 %collective-permute-start.16 = (bf16[4096,128]{1,0:T(8,128)(2,1)S(1)}, bf16[4096,128]{1,0:T(8,128)(2,1)S(1)}, u32[]{:S(2)}, u32[]{:S(2)}) collective-permute-start(bf16[4096,128]{1,0:T(8,128)(2,1)S(1)} %slice.42), channel_id=1, source_target_pairs={{0,8},{2,10},{8,16},{10,18},{16,24},{18,26},{24,28},{26,30},{28,20... | collective-permute-start | bytes 3145736 | tf_op jit(solution)/shard_map/ppermute | solution.py:329
  188.6 26.1 %collective-permute-start.18 = (bf16[16,64,512]{2,1,0:T(8,128)(2,1)S(1)}, bf16[16,64,512]{2,1,0:T(8,128)(2,1)S(1)}, u32[]{:S(2)}, u32[]{:S(2)}) collective-permute-start(bf16[16,64,512]{2,1,0:T(8,128)(2,1)S(1)} %copy-done.25), channel_id=1, source_target_pairs={{0,2},{2,0},{4,6},{6,4},{8,10},{10,8},{12,14},{14,12},{16,18},{18,... | collective-permute-start | bytes 3145736 | tf_op jit(solution)/shard_map/ppermute | solution.py:329
  190.2 42.9 %collective-permute-start.19 = (bf16[16,64,512]{2,1,0:T(8,128)(2,1)S(1)}, bf16[16,64,512]{2,1,0:T(8,128)(2,1)S(1)}, u32[]{:S(2)}, u32[]{:S(2)}) collective-permute-start(bf16[16,64,512]{2,1,0:T(8,128)(2,1)S(1)} %copy-done.23), channel_id=1, source_target_pairs={{0,2},{2,0},{4,6},{6,4},{8,10},{10,8},{12,14},{14,12},{16,18},{18,... | collective-permute-start | bytes 3145736 | tf_op jit(solution)/shard_map/ppermute | solution.py:329
  191.9 41.2 %copy-start.7 = (bf16[16,64,512]{2,1,0:T(8,128)(2,1)S(1)}, bf16[16,64,512]{2,1,0:T(8,128)(2,1)}, u32[]{:S(2)}) copy-start(bf16[16,64,512]{2,1,0:T(8,128)(2,1)} %copy-done.6) | copy-start | bytes 3145732
  234.9 21.1 %copy-start.20 = (f32[128,128]{1,0:T(8,128)S(1)}, f32[128,128]{1,0:T(8,128)}, u32[]{:S(2)}) copy-start(f32[128,128]{1,0:T(8,128)} %start_ref.1) | copy-start | bytes 196612
  234.9 21.1 %copy-start.21 = (f32[128]{0:T(128)S(1)}, f32[128]{0:T(128)}, u32[]{:S(2)}) copy-start(f32[128]{0:T(128)} %param.13) | copy-start | bytes 1540
  235.6 1.3 collective-permute-start.20
  236.9 4.3 %collective-permute-start.21 = (f32[128,128]{1,0:T(8,128)S(1)}, f32[128,128]{1,0:T(8,128)S(1)}, u32[]{:S(2)}, u32[]{:S(2)}) collective-permute-start(f32[128,128]{1,0:T(8,128)S(1)} %add.231), channel_id=1, source_target_pairs={{0,2},{2,0},{4,6},{6,4},{8,10},{10,8},{12,14},{14,12},{16,18},{18,... | collective-permute-start | bytes 196616 | tf_op jit(solution)/shard_map/ppermute | solution.py:329
  241.8 4.3 %collective-permute-start.22 = (f32[128,128]{1,0:T(8,128)S(1)}, f32[128,128]{1,0:T(8,128)S(1)}, u32[]{:S(2)}, u32[]{:S(2)}) collective-permute-start(f32[128,128]{1,0:T(8,128)S(1)} %convolution_add_fusion), channel_id=1, source_target_pairs={{0,4},{2,6},{4,0},{6,2},{8,12},{10,14},{12,8},{14,10},{16,20},{18,... | collective-permute-start | bytes 196616 | tf_op jit(solution)/shard_map/ppermute | solution.py:329
  246.2 4.3 %collective-permute-start.23 = (f32[128,128]{1,0:T(8,128)S(1)}, f32[128,128]{1,0:T(8,128)S(1)}, u32[]{:S(2)}, u32[]{:S(2)}) collective-permute-start(f32[128,128]{1,0:T(8,128)S(1)} %add.235), channel_id=1, source_target_pairs={{0,8},{2,10},{4,12},{6,14},{8,0},{10,2},{12,4},{14,6},{16,24},{18,... | collective-permute-start | bytes 196616 | tf_op jit(solution)/shard_map/ppermute | solution.py:329
  250.5 5.5 %collective-permute-start.24 = (f32[128,128]{1,0:T(8,128)S(1)}, f32[128,128]{1,0:T(8,128)S(1)}, u32[]{:S(2)}, u32[]{:S(2)}) collective-permute-start(f32[128,128]{1,0:T(8,128)S(1)} %add.236), channel_id=1, source_target_pairs={{0,16},{2,18},{4,20},{6,22},{8,24},{10,26},{12,28},{14,30},{16,0},... | collective-permute-start | bytes 196616 | tf_op jit(solution)/shard_map/ppermute | solution.py:329
  (12 other events, 13.2 us)

commit v3 on v1

--- a/solution.py
+++ b/solution.py
@@ -2,6 +2,7 @@
 
 import jax
 import jax.numpy as jnp
+import numpy as np
 from jax import lax
 from jax.experimental import pallas as pl
 from jax.experimental.pallas import tpu as pltpu
@@ -14,7 +15,9 @@
 BLUR_TAPS = (1.0 / 64, 6.0 / 64, 15.0 / 64, 20.0 / 64, 15.0 / 64, 6.0 / 64, 1.0 / 64)
 DECAY_RATE = 0.7
 HIGHEST = lax.Precision.HIGHEST
-PANEL = 32
+PANEL = 64
+VMEM_BYTES = 32 * 1024 * 1024
+BLUR_BYTES = 49 * 1024 * 1024
 
 
 def extended(shard, sides, width):
@@ -54,32 +57,45 @@
     down = (((0,), (0,)), ((), ()))
     normal = lax.dot_general(product, product, across, precision=HIGHEST, preferred_element_type=jnp.float32)
     state = jnp.concatenate([normal, product], axis=1)
-    rows = lax.broadcasted_iota(jnp.int32, (PANEL, size), 0)
-    lanes = lax.broadcasted_iota(jnp.int32, (PANEL, size), 1)
     shape = (PANEL, size)
+    rows = lax.broadcasted_iota(jnp.int32, shape, 0)
+    lanes = lax.broadcasted_iota(jnp.int32, shape, 1)
     finished = []
     for base in range(0, size, PANEL):
         left, right = (state[:PANEL, :size], state[:PANEL, size:])
-        for j in range(0, PANEL, 2):
-            column = base + j
-            col0 = jnp.broadcast_to(left[:, column : column + 1], shape)
-            col1 = jnp.broadcast_to(left[:, column + 1 : column + 2], shape)
-            aa = jnp.broadcast_to(col0[j : j + 1], shape)
-            ab = jnp.broadcast_to(col1[j : j + 1], shape)
-            bb = jnp.broadcast_to(col1[j + 1 : j + 2], shape)
-            inverse = reciprocal(aa * bb - ab * ab)
-            below = rows > j + 1
-            second = rows == j + 1
-            factor0 = jnp.where(
-                below, (col0 * bb - col1 * ab) * inverse, jnp.where(second, ab * reciprocal(aa), 0.0)
-            )
-            factor1 = jnp.where(below, (col1 * aa - col0 * ab) * inverse, 0.0)
-            left0 = jnp.broadcast_to(left[j : j + 1], shape)
-            left1 = jnp.broadcast_to(left[j + 1 : j + 2], shape)
-            right0 = jnp.broadcast_to(right[j : j + 1], shape)
-            right1 = jnp.broadcast_to(right[j + 1 : j + 2], shape)
-            left = left - factor0 * left0 - factor1 * left1
-            right = right - factor0 * right0 - factor1 * right1
+        for j in range(0, PANEL, 4):
+            at = base + j
+            col = [jnp.broadcast_to(left[:, at + i : at + i + 1], shape) for i in range(4)]
+            p = {(r, s): jnp.broadcast_to(col[s][j + r : j + r + 1], shape) for s in range(4) for r in range(s + 1)}
+            inverse = reciprocal(p[0, 0] * p[1, 1] - p[0, 1] * p[0, 1])
+            a00, a01, a11 = (p[1, 1] * inverse, -p[0, 1] * inverse, p[0, 0] * inverse)
+            t00, t10 = (a00 * p[0, 2] + a01 * p[1, 2], a01 * p[0, 2] + a11 * p[1, 2])
+            t01, t11 = (a00 * p[0, 3] + a01 * p[1, 3], a01 * p[0, 3] + a11 * p[1, 3])
+            q00 = p[2, 2] - p[0, 2] * t00 - p[1, 2] * t10
+            q01 = p[2, 3] - p[0, 2] * t01 - p[1, 2] * t11
+            q11 = p[3, 3] - p[0, 3] * t01 - p[1, 3] * t11
+            inverse = reciprocal(q00 * q11 - q01 * q01)
+            b00, b01, b11 = (q11 * inverse, -q01 * inverse, q00 * inverse)
+            first = p[0, 1] * reciprocal(p[0, 0])
+            third = q01 * reciprocal(q00)
+            col2 = col[2] - col[0] * t00 - col[1] * t10
+            col3 = col[3] - col[0] * t01 - col[1] * t11
+            f2 = col2 * b00 + col3 * b01
+            f3 = col2 * b01 + col3 * b11
+            f0 = col[0] * a00 + col[1] * a01 - f2 * t00 - f3 * t01
+            f1 = col[0] * a01 + col[1] * a11 - f2 * t10 - f3 * t11
+            below = rows > j + 3
+            row1, row2, row3 = (rows == j + 1, rows == j + 2, rows == j + 3)
+            zero = jnp.zeros(shape, jnp.float32)
+            inner = jnp.where(row2, t00, jnp.where(row3, t01 - third * t00, zero))
+            f0 = jnp.where(below, f0, jnp.where(row1, first, inner))
+            f1 = jnp.where(below, f1, jnp.where(row2, t10, jnp.where(row3, t11 - third * t10, zero)))
+            f2 = jnp.where(below, f2, jnp.where(row3, third, zero))
+            f3 = jnp.where(below, f3, zero)
+            lines = [jnp.broadcast_to(left[j + i : j + i + 1], shape) for i in range(4)]
+            left = left - ((f0 * lines[0] + f1 * lines[1]) + (f2 * lines[2] + f3 * lines[3]))
+            lines = [jnp.broadcast_to(right[j + i : j + i + 1], shape) for i in range(4)]
+            right = right - ((f0 * lines[0] + f1 * lines[1]) + (f2 * lines[2] + f3 * lines[3]))
         pivots = jnp.sum(jnp.where(lanes == base + rows, left, 0.0), axis=1, keepdims=True)
         scale = lax.rsqrt(pivots)
         left = left * scale
@@ -97,55 +113,68 @@
     return jnp.concatenate(finished, axis=0)
 
 
-def rotate_kernel(frames, chunk, summed_ref, sigma_ref, start_ref, coeffs_ref, basis_ref, basis_out, coeffs_out, sigma_out):
+def rotate_kernel(frames, chunk, summed_ref, more_ref, sigma_ref, start_ref, coeffs_ref, basis_ref, basis_out, coeffs_out, sigma_out,
+                  held_ref, turned_ref, come_sem, go_sem):
+    come = pltpu.make_async_copy(basis_ref, held_ref, come_sem)
+    come.start()
     size = summed_ref.shape[0]
     across = (((1,), (1,)), ((), ()))
     diagonal = lax.broadcasted_iota(jnp.int32, (size, size), 0) == lax.broadcasted_iota(jnp.int32, (size, size), 1)
     sigma = jnp.broadcast_to(sigma_ref[...], (size, size))
-    gram = jnp.where(diagonal, sigma * sigma, 0.0) + summed_ref[...] * (1.0 / frames)
+    gram = jnp.where(diagonal, sigma * sigma, 0.0) + (summed_ref[...] + more_ref[...]) * (1.0 / frames)
 
     def step(_, turned):
         return orthonormal_rows(jnp.dot(turned, gram, precision=HIGHEST, preferred_element_type=jnp.float32))
 
     turned = lax.fori_loop(0, ITERS, step, start_ref[...].T)
+    rotation = turned.T
+    high = rotation.astype(jnp.bfloat16)
+    low = (rotation - high.astype(jnp.float32)).astype(jnp.bfloat16)
+    pair = jnp.concatenate([high, low], axis=1)
+    come.wait()
+    goes = []
+    for i in range(held_ref.shape[0] // chunk):
+        at = pl.ds(i * chunk, chunk)
+        total = jnp.dot(held_ref[at, :], pair, preferred_element_type=jnp.float32)
+        turned_ref[at, :] = (total[:, :size] + total[:, size:]).astype(turned_ref.dtype)
+        goes.append(pltpu.make_async_copy(turned_ref.at[at, :], basis_out.at[at, :], go_sem.at[i]))
+        goes[-1].start()
     coeffs_out[...] = lax.dot_general(
         coeffs_ref[...], turned, across, precision=HIGHEST, preferred_element_type=jnp.float32
     )
     curved = jnp.dot(turned, gram, precision=HIGHEST, preferred_element_type=jnp.float32)
     sigma_out[...] = jnp.sqrt(jnp.sum((turned * curved).T, axis=0, keepdims=True))
-    rotation = turned.T
-    high = rotation.astype(jnp.bfloat16)
-    rest = rotation - high.astype(jnp.float32)
-    middle = rest.astype(jnp.bfloat16)
-    low = (rest - middle.astype(jnp.float32)).astype(jnp.bfloat16)
-
-    @pl.loop(0, basis_ref.shape[0] // chunk)
-    def _(i):
-        at = pl.ds(pl.multiple_of(i * chunk, chunk), chunk)
-        block = basis_ref[at, :]
-        total = jnp.dot(block, low, preferred_element_type=jnp.float32)
-        total = total + jnp.dot(block, middle, preferred_element_type=jnp.float32)
-        total = total + jnp.dot(block, high, preferred_element_type=jnp.float32)
-        basis_out[at, :] = total.astype(basis_out.dtype)
-
-
-def rotated(summed_gram, total_frames, prior_sigma, start_rotation, coeffs, basis):
+    for go in goes:
+        go.wait()
+
+
+def rotated(summed_gram, more_gram, total_frames, prior_sigma, start_rotation, coeffs, basis):
     rows, size = basis.shape
-    chunk = 512 if rows % 512 == 0 else rows
+    chunk = 1024 if rows % 1024 == 0 else rows
+    inside = pl.BlockSpec(memory_space=pltpu.VMEM)
+    outside = pl.BlockSpec(memory_space=pl.ANY)
     new_basis, new_coeffs, new_sigma = pl.pallas_call(
         functools.partial(rotate_kernel, total_frames, chunk),
+        in_specs=[inside, inside, inside, inside, inside, outside],
+        out_specs=(outside, inside, inside),
         out_shape=(
             jax.ShapeDtypeStruct(basis.shape, basis.dtype),
             jax.ShapeDtypeStruct(coeffs.shape, coeffs.dtype),
             jax.ShapeDtypeStruct((1, size), jnp.float32),
         ),
-        compiler_params=pltpu.CompilerParams(vmem_limit_bytes=32 * 1024 * 1024),
+        scratch_shapes=[
+            pltpu.VMEM(basis.shape, basis.dtype),
+            pltpu.VMEM(basis.shape, basis.dtype),
+            pltpu.SemaphoreType.DMA,
+            pltpu.SemaphoreType.DMA((rows // chunk,)),
+        ],
+        compiler_params=pltpu.CompilerParams(vmem_limit_bytes=VMEM_BYTES),
         name="orthogonal_iteration",
-    )(summed_gram, prior_sigma.reshape(1, size), start_rotation, coeffs, basis)
+    )(summed_gram, more_gram, prior_sigma.reshape(1, size), start_rotation, coeffs, basis)
     return (new_basis, new_coeffs, new_sigma.reshape(size))
 
 
-def body(raw_frames, dark_frame, dead_mask, frame_group, prior_sigma, start_rotation, basis):
+def gathered_body(raw_frames, dark_frame, dead_mask, frame_group, prior_sigma, start_rotation, basis):
     frame_count, strip_rows, columns = raw_frames.shape
     corrected = (
         (raw_frames.astype(jnp.float32) - dark_frame) * (1 - dead_mask).astype(jnp.float32)
@@ -183,7 +212,312 @@
     total_frames = frame_count * lax.axis_size("frames")
     local_gram = jnp.dot(coeffs.T, coeffs, precision=lax.Precision.HIGHEST)
     summed_gram = summed_over(local_gram, "frames")
-    return rotated(summed_gram, total_frames, prior_sigma, start_rotation, coeffs, basis)
+    return rotated(summed_gram, jnp.zeros_like(summed_gram), total_frames, prior_sigma, start_rotation, coeffs, basis)
+
+
+RING = (0, 2, 4, 6, 7, 5, 3, 1)
+PLACES = 4 * len(RING) + 2
+BAND = 16
+EDGE = 8
+FRAME_BLOCK = 16
+
+
+def entry(place, at):
+    return place[1 + place[0] * PLACES + at]
+
+
+def blur_kernel(slot, outputs, begin, place_ref, group_ref, main_ref, prev_ref, next_ref, *refs):
+    edge_ref, refs = (refs[0], refs[1:]) if slot else (None, refs)
+    darks, masks, banded_ref, refs = (refs[:3], refs[3:6], refs[6], refs[7:])
+    out_refs, (rows_ref, lines_ref, blurred_ref) = (refs[: len(outputs)], refs[len(outputs) :])
+    side = entry(place_ref, 4 * slot + 2)
+    frames, height, columns = main_ref.shape
+    span = height + 2 * EDGE
+    parts = [main_ref[...], prev_ref[...], next_ref[...]]
+    main, top, bottom = [
+        (part.astype(jnp.float32) - dark_ref[...]) * (1 - mask_ref[...]).astype(jnp.float32)
+        for part, dark_ref, mask_ref in zip(parts, darks, masks)
+    ]
+    top, bottom = (top[:, BAND - EDGE :], bottom[:, :EDGE])
+    if slot:
+        upper = entry(place_ref, 0) == 0
+        edge = edge_ref[...].astype(jnp.float32)
+        top = jnp.where(entry(place_ref, 4 * slot + 3) == 1, jnp.where(upper, 0.0, edge[:, BAND - EDGE :]), top)
+        bottom = jnp.where(entry(place_ref, 4 * slot + 4) == 1, jnp.where(upper, edge[:, :EDGE], 0.0), bottom)
+    tiles = columns // 128
+    flat_ref = rows_ref.reshape(tiles * frames * span, 128)
+    for tile in range(tiles):
+        part = slice(tile * 128, (tile + 1) * 128)
+        rows_ref[tile, :, :EDGE] = top[:, :, part]
+        rows_ref[tile, :, EDGE : EDGE + height] = main[:, :, part]
+        rows_ref[tile, :, EDGE + height :] = bottom[:, :, part]
+        for row in range(height + 6):
+            line = flat_ref[pl.ds(tile * frames * span + row + EDGE - 3, frames, stride=span), :]
+            lines_ref[row * frames : (row + 1) * frames, part] = line.astype(jnp.bfloat16)
+    blurred_ref[...] = jnp.dot(lines_ref[...], banded_ref[...], preferred_element_type=jnp.float32)
+    frame = lax.broadcasted_iota(jnp.int32, (frames, columns), 0)
+    group = jnp.zeros((frames, columns), jnp.int32)
+    for i in range(frames):
+        group = jnp.where(frame == i, group_ref[pl.program_id(0) * frames + (begin + i)], group)
+    weight = jnp.ones((frames, columns), jnp.float32)
+    for value in range(GROUPS - 1):
+        weight = jnp.where(group == value, DECAY_RATE ** (GROUPS - 1 - value), weight)
+    for name, out_ref in zip(outputs, out_refs):
+        first = 0 if len(outputs) == 1 else (side if name == "own" else 1 - side) * BAND
+        for row in range(BAND):
+            taken = [
+                blurred_ref[pl.ds(pl.multiple_of((first + row + offset) * frames, frames), frames), :]
+                for offset in range(7)
+            ]
+            total = BLUR_TAPS[3] * taken[3]
+            for offset in range(3):
+                total = total + BLUR_TAPS[offset] * (taken[offset] + taken[6 - offset])
+            out_ref[row] = (weight * total).astype(jnp.bfloat16)
+
+
+def blurred_bands(slot, outputs, begin, frame_count, place, raw_frames, edge, dark_frame, dead_mask, banded, frame_group):
+    _, strip_rows, columns = raw_frames.shape
+    bands = strip_rows // BAND
+    height = len(outputs) * BAND
+    skipped = begin // FRAME_BLOCK
+    lines = height + 6
+
+    def at_main(place):
+        if len(outputs) == 2:
+            return entry(place, 4 * slot + 1)
+        side = entry(place, 4 * slot + 2)
+        return 2 * entry(place, 4 * slot + 1) + (side if outputs[0] == "own" else 1 - side)
+
+    at_prev = lambda place: jnp.maximum(len(outputs) * at_main(place) - 1, 0)
+    at_next = lambda place: jnp.minimum(len(outputs) * (at_main(place) + 1), bands - 1)
+    rows = ((height, at_main), (BAND, at_prev), (BAND, at_next))
+    edges = () if edge is None else (edge,)
+
+    def pixels(size, at):
+        return pl.BlockSpec((size, columns), lambda f, place, group: (at(place), 0))
+
+    def frames(size, at):
+        return pl.BlockSpec((FRAME_BLOCK, size, columns), lambda f, place, group: (f + skipped, at(place), 0))
+
+    grid_spec = pltpu.PrefetchScalarGridSpec(
+        num_scalar_prefetch=2,
+        grid=(frame_count // FRAME_BLOCK,),
+        in_specs=[frames(*row) for row in rows]
+        + [frames(BAND, lambda place: 0)] * len(edges)
+        + [pixels(*row) for row in rows] * 2
+        + [pl.BlockSpec(banded.shape, lambda f, place, group: (0, 0))],
+        out_specs=[pl.BlockSpec((BAND, FRAME_BLOCK, columns), lambda f, place, group: (0, f, 0))] * len(outputs),
+        scratch_shapes=[
+            pltpu.VMEM((columns // 128, FRAME_BLOCK, height + 2 * EDGE, 128), jnp.float32),
+            pltpu.VMEM((lines * FRAME_BLOCK, columns), jnp.bfloat16),
+            pltpu.VMEM((lines * FRAME_BLOCK, columns), jnp.float32),
+        ],
+    )
+    shape = jax.ShapeDtypeStruct((BAND, frame_count, columns), jnp.bfloat16)
+    starts = slot == 0 and outputs[0] == "sent"
+    return pl.pallas_call(
+        functools.partial(blur_kernel, slot, outputs, begin),
+        grid_spec=grid_spec,
+        out_shape=[shape] * len(outputs),
+        compiler_params=pltpu.CompilerParams(vmem_limit_bytes=60 * 1024 * 1024 if starts else BLUR_BYTES),
+        cost_estimate=pl.CostEstimate(flops=1024, bytes_accessed=1024, transcendentals=0),
+        name="blur_bands",
+    )(place, frame_group, *[raw_frames] * 3, *edges, *[dark_frame] * 3, *[dead_mask] * 3, banded)
+
+
+def project_kernel(slot, at, parts, place_ref, total_ref, *refs):
+    line_refs, basis_refs, out_ref = (refs[:parts], refs[parts:-1], refs[-1])
+    columns = line_refs[0].shape[2]
+
+    @pl.when(pl.program_id(0) == 0)
+    def _():
+        out_ref[...] = total_ref[...]
+
+    def add(basis_ref):
+        total = out_ref[at, :]
+        for row in range(line_refs[0].shape[0]):
+            lines = jnp.concatenate([line_ref[row] for line_ref in line_refs], axis=0)
+            total = total + jnp.dot(
+                lines, basis_ref[row * columns : (row + 1) * columns, :], preferred_element_type=jnp.float32
+            )
+        out_ref[at, :] = total
+
+    if len(basis_refs) == 1:
+        add(basis_refs[0])
+    else:
+        here = entry(place_ref, PLACES - 1) == slot
+        pl.when(here)(lambda: add(basis_refs[0]))
+        pl.when(jnp.logical_not(here))(lambda: add(basis_refs[1]))
+
+
+def projected(total, own, came, basis, first_row, choice=None):
+    step = 4
+    begin = 0 if own else total.shape[0] // 2
+    lines = (*own, *came)
+    columns = lines[0].shape[2]
+    at = slice(begin, begin + sum(values.shape[1] for values in lines))
+    size = basis.shape[1]
+    skipped = first_row // step
+    steps = basis.shape[0] // columns // step
+    whole = pl.BlockSpec(total.shape, lambda i, place: (0, 0))
+    other, place, slot = choice or (None, jnp.zeros((1,), jnp.int32), 0)
+    blocks = (basis,) if choice is None else (basis, other)
+    return pl.pallas_call(
+        functools.partial(project_kernel, slot, at, len(lines)),
+        grid_spec=pltpu.PrefetchScalarGridSpec(
+            num_scalar_prefetch=1,
+            grid=(steps,),
+            in_specs=[whole]
+            + [pl.BlockSpec((step, *values.shape[1:]), lambda i, place: (i + skipped, 0, 0)) for values in lines]
+            + [pl.BlockSpec((step * columns, size), lambda i, place: (i, 0))] * len(blocks),
+            out_specs=whole,
+        ),
+        out_shape=jax.ShapeDtypeStruct(total.shape, jnp.float32),
+        compiler_params=pltpu.CompilerParams(vmem_limit_bytes=VMEM_BYTES),
+        cost_estimate=pl.CostEstimate(flops=1024, bytes_accessed=1024, transcendentals=0),
+        name="project_band",
+    )(place, total, *lines, *blocks)
+
+
+def merge_kernel(total_ref, strip_ref, side_ref, both_ref, coeffs_out, gram_out):
+    half = coeffs_out.shape[0]
+    down = (((0,), (0,)), ((), ()))
+    near = total_ref[...] + strip_ref[...]
+    far = side_ref[...] + both_ref[...]
+    grams = []
+    for at, other in ((slice(0, half), slice(half, None)), (slice(half, None), slice(0, half))):
+        coeffs = near[at] + far[other]
+        if not grams:
+            coeffs_out[...] = coeffs
+        grams.append(lax.dot_general(coeffs, coeffs, down, precision=HIGHEST, preferred_element_type=jnp.float32))
+    gram_out[...] = grams[0] + grams[1]
+
+
+def placement():
+    ring = len(RING)
+    table = np.zeros((2 * ring, 2, PLACES), np.int32)
+    for at in range(ring):
+        order = [0, -1, 1, -2, 2, -3, 3, 4]
+        if RING[at] in (0, ring - 1):
+            order[:2] = order[1::-1]
+        for strip in range(2):
+            for x in range(2):
+                row = table[2 * RING[at] + x, strip]
+                row[0], row[-1] = (strip, order.index(0))
+                for slot, by in enumerate(order):
+                    pair = RING[(at + by) % ring]
+                    row[4 * slot + 1 : 4 * slot + 5] = (pair, x, pair == 0, pair == ring - 1)
+    return table.reshape(-1)
+
+
+def paired_body(raw_frames, dark_frame, dead_mask, frame_group, prior_sigma, start_rotation, basis):
+    frame_count, strip_rows, columns = raw_frames.shape
+    size = basis.shape[1]
+    count = lax.axis_size("frames")
+    strips = lax.axis_size("strips")
+    ring = len(RING)
+    strip = lax.axis_index("strips")
+    index = lax.axis_index(("frames", "strips"))
+    place = jnp.concatenate([index.reshape(1).astype(jnp.int32), jnp.asarray(placement())])
+
+    def links(by):
+        return [
+            (2 * RING[at] + x, 2 * RING[(at + by) % ring] + x) for at in range(ring) for x in range(2)
+        ]
+
+    swap = [(i, i ^ 1) for i in range(count)]
+    move = lambda values, pairs: lax.ppermute(values, "frames", pairs)
+    column = np.arange(columns)
+    taps = np.array(BLUR_TAPS + (0.0,), np.float32)
+    offsets = column[None, :] - column[:, None] + 3
+    banded = jnp.asarray(taps[np.where((offsets >= 0) & (offsets < 7), offsets, 7)], jnp.bfloat16)
+
+    def bands(slot, outputs, edge, begin=0, held=frame_count):
+        return blurred_bands(
+            slot, outputs, begin, held, place, raw_frames, edge, dark_frame, dead_mask, banded, frame_group
+        )
+
+    first = frame_count // 2
+    (sent_first,) = bands(0, ("sent",), None, 0, first)
+    sent_first, near_raw, near_dark, near_mask = lax.optimization_barrier(
+        (sent_first, raw_frames, dark_frame, dead_mask)
+    )
+    came_first = move(sent_first, swap)
+    (sent_rest,) = bands(0, ("sent",), None, first, first)
+    near = jnp.where(strip == 0, strip_rows - BAND, 0)
+    rows = [lax.dynamic_slice_in_dim(values, near, BAND, axis=-2) for values in (near_raw, near_dark, near_mask)]
+    border = ((rows[0].astype(jnp.float32) - rows[1]) * (1 - rows[2]).astype(jnp.float32)).astype(jnp.bfloat16)
+    came_first, sent_rest, border = lax.optimization_barrier((came_first, sent_rest, border))
+    came_rest = move(sent_rest, swap)
+    edge = lax.ppermute(border, "strips", [(0, 1), (1, 0)])
+    sent_next, own_next = bands(1, ("sent", "own"), edge)
+    came_rest, sent_next, own_next, passing = lax.optimization_barrier((came_rest, sent_next, own_next, basis))
+    half = basis.shape[0] // 2
+    blocks = {0: basis}
+    send, own, came = ([None, sent_next], [None, own_next], [came_rest])
+    total = jnp.zeros((2 * frame_count, size), jnp.float32)
+    up, down = (passing, passing)
+
+    def project(total, slot):
+        parts = (came[slot],) if slot else (came_first, came[0])
+        if slot < 2:
+            return projected(total, (own[slot],), parts, blocks[0], 0, (blocks[-1], place, slot))
+        return projected(total, (own[slot],), parts, blocks[(0, -1, 1, -2, 2, -3, 3)[slot]], 0)
+
+    for stage in range(4):
+        if stage < 3:
+            up, down = (move(up, links(1)), move(down, links(-1)))
+        else:
+            up, down = (move(up[:half], links(1)), move(down[half:], links(-1)))
+        for slot in range(len(came), min(2 * stage + 3, ring)):
+            if slot == len(send):
+                sent, kept = bands(slot, ("sent", "own"), edge)
+                own.append(kept)
+                send.append(sent)
+            came.append(move(send[slot], swap))
+        if stage == 0:
+            (own[0],) = bands(0, ("own",), None)
+        while stage < 2 and len(own) < (5, 8)[stage]:
+            sent, kept = bands(len(own), ("sent", "own"), edge)
+            own.append(kept)
+            send.append(sent)
+        for slot in ((), (0, 1, 2), (3, 4), (5, 6))[stage]:
+            total = project(total, slot)
+        if stage == 3:
+            break
+        last = len(came)
+        held = (up, down, total, came[last - 2], came[last - 1]) + tuple(send[last:]) + tuple(own[last:])
+        up, down, total, came[last - 2], came[last - 1], *others = lax.optimization_barrier(held)
+        waiting = len(send) - last
+        send[last:] = others[:waiting]
+        own[last:] = others[waiting:]
+        blocks[-stage - 1], blocks[stage + 1] = (up, down)
+    for lines in (((own[7],), ()), ((), (came[7],))):
+        for n, block in enumerate((up, down)):
+            total = projected(total, *lines, block, n * BAND // 2)
+    flips = [
+        lax.ppermute(total, ("frames", "strips"), [(i, i ^ flip) for i in range(count * strips)]) for flip in (1, 2, 3)
+    ]
+    coeffs, gram = pl.pallas_call(
+        merge_kernel,
+        out_shape=(
+            jax.ShapeDtypeStruct((frame_count, size), jnp.float32),
+            jax.ShapeDtypeStruct((size, size), jnp.float32),
+        ),
+        name="merge",
+    )(total, *flips)
+    near = [move(gram, [(i, i ^ flip) for i in range(count)]) for flip in (2, 4, 6)]
+    gram = (gram + near[0]) + (near[1] + near[2])
+    far = move(gram, [(i, i ^ 8) for i in range(count)])
+    return rotated(gram, far, frame_count * count, prior_sigma, start_rotation, coeffs, basis)
+
+
+def body(raw_frames, *others):
+    _, strip_rows, columns = raw_frames.shape
+    paired = lax.axis_size("frames") == 2 * len(RING) and lax.axis_size("strips") == 2
+    if paired and strip_rows == 2 * len(RING) * BAND and raw_frames.shape[0] % FRAME_BLOCK == 0:
+        return paired_body(raw_frames, *others)
+    return gathered_body(raw_frames, *others)
 
 
 def solution(mesh):

time: 459 us -> 259 us (0.56)
  waiting for transfers between devices: 243 us -> 95 us
  other arithmetic: 83 us -> 3.85 us
  Pallas kernels: 46.3 us -> 121 us
  matrix products: 39.5 us -> 0 us
  starting transfers between devices: 8.87 us -> 28.6 us
  between operations: 14.2 us -> 1.31 us
  local copies, waits for them, and re-layouts: 20.2 us -> 8.55 us
    all_gather x1 -> x0, waiting for transfers between devices: 226 us -> none  [body(): lax.all_gather(basis, 'frames', axis=0, tiled=True)]
    convert_element_type x2, other arithmetic: 82.9 us -> 1.61 us  [the longest x1 1.6 us: paired_body(): ((rows[0].astype(jnp.float32) - rows[1]) * (1 - rows[2]).astype(jnp.float...]
    ppermute x6 -> x25, waiting for transfers between devices: 15.8 us -> 95 us  [the longest x21 90.3 us: paired_body(): move = lambda values, pairs: lax.ppermute(values, 'frames', pairs)]
    pallas_call x1 -> x23, Pallas kernels: 46.3 us -> 121 us  [the longest x10 71.6 us: blurred_bands(): pl.pallas_call(functools.partial(blur_kernel, slot, outputs, begin), grid...]
    dot_general x3 -> x0, matrix products: 39.5 us -> none  [the longest x1 20.7 us: body(): jnp.dot(corrected.reshape(frame_count * strip_rows, columns), banded, pre...]
    ppermute x6 -> x25, starting transfers between devices: 8.83 us -> 28.6 us  [the longest x21 26.7 us: paired_body(): move = lambda values, pairs: lax.ppermute(values, 'frames', pairs)]
    unnamed x9 -> x66, local copies, waits for them, and re-layouts: 18.4 us -> 8.4 us
  transfers between devices with their start and end apart: 7 -> 25, of which waited for: 6 -> 15; matrix products, arithmetic and copies ran while one was open for 27% -> 1% of each run, Pallas kernels for 0% -> 32%
where the time goes in v3:
time: 259 us; the launch traced here: 258 us
  Pallas kernels  121 us (47%)
  waiting for transfers between devices  95 us (37%)
  starting transfers between devices  28.6 us (11%)
  local copies, waits for them, and re-layouts  8.55 us (3%)
  other arithmetic  3.85 us (1%)
    ppermute x21, waiting for transfers between devices, paired_body(): move = lambda values, pairs: lax.ppermute(values, 'frames', pairs)  90.3 us
    pallas_call x10, Pallas kernels, blurred_bands(): pl.pallas_call(functools.partial(blur_kernel, slot, outputs, begin), grid...  71.6 us
    pallas_call x1, Pallas kernels, rotated(): pl.pallas_call(functools.partial(rotate_kernel, total_frames, chunk), in_...  30 us
    ppermute x21, starting transfers between devices, paired_body(): move = lambda values, pairs: lax.ppermute(values, 'frames', pairs)  26.7 us
    pallas_call x11, Pallas kernels, projected(): pl.pallas_call(functools.partial(project_kernel, slot, at, len(lines)), g...  17.3 us
    unnamed x66, local copies, waits for them, and re-layouts  8.4 us
  transfers between devices with their start and end apart: 25, of which 15 were waited for; matrix products, arithmetic and copies ran while one was open for 1% of the time, Pallas kernels for 32%

profile of v3, /device:TPU:0, one launch (start us, length us, event | category | flops | bytes accessed | tf_op | source)
XLA Modules:
  0.0 258.1 jit_solution(11463971375740462826)
XLA Ops:
  0.6 1.4 pad_add_fusion.place_ref
  2.0 5.1 %blur_bands.10 = bf16[16,32,512]{2,1,0:T(8,128)(2,1)} custom-call(s32[1089]{0:T(1024)} %pad_add_fusion.place_ref, s32[64]{0:T(128)} %group_ref.19, bf16[64,256,512]{2,1,0:T(8,128)(2,1)} %next_ref.19, bf16[64,256,512]{2,1,0:T(8,128)(2,1)} %next_ref.19, bf16[64,256,512]{2,1,0:T(8,128)(2,1)} %next_ref.19, f32[256,512]{1,0:T(8,128)} %refs_3_.21, ...), custom_call_target="tpu_custom_call" | custom-call | flops 1024 | bytes 1024 | tf_op jit(solution)/shard_map/blur_bands/pallas_call | solution.py:318
  7.1 3.0 %collective-permute-start = (bf16[16,32,512]{2,1,0:T(8,128)(2,1)}, bf16[16,32,512]{2,1,0:T(8,128)(2,1)S(1)}, u32[]{:S(2)}, u32[]{:S(2)}) collective-permute-start(bf16[16,32,512]{2,1,0:T(8,128)(2,1)} %blur_bands.10), channel_id=1, source_target_pairs={{0,2},{2,0},{4,6},{6,4},{8,10},{10,8},{12,14},{14,12},{16,18},{18,... | collective-permute-start | bytes 1572872 | tf_op jit(solution)/shard_map/ppermute | solution.py:429
  10.1 5.1 %blur_bands.11 = bf16[16,32,512]{2,1,0:T(8,128)(2,1)} custom-call(s32[1089]{0:T(1024)} %pad_add_fusion.place_ref, s32[64]{0:T(128)} %group_ref.19, bf16[64,256,512]{2,1,0:T(8,128)(2,1)} %next_ref.19, bf16[64,256,512]{2,1,0:T(8,128)(2,1)} %next_ref.19, bf16[64,256,512]{2,1,0:T(8,128)(2,1)} %next_ref.19, f32[256,512]{1,0:T(8,128)} %refs_3_.21, ...), custom_call_target="tpu_custom_call" | custom-call | flops 1024 | bytes 1024 | tf_op jit(solution)/shard_map/blur_bands/pallas_call | solution.py:318
  15.4 1.6 multiply_convert_fusion
  17.0 5.3 %collective-permute-done.refs_1_ = bf16[16,32,512]{2,1,0:T(8,128)(2,1)S(1)} collective-permute-done((bf16[16,32,512]{2,1,0:T(8,128)(2,1)}, bf16[16,32,512]{2,1,0:T(8,128)(2,1)S(1)}, u32[]{:S(2)}, u32[]{:S(2)}) %collective-permute-start) | collective-permute-done | bytes 524320 | tf_op jit(solution)/shard_map/ppermute | solution.py:429
  22.3 1.7 collective-permute-start.1
  24.9 7.7 %blur_bands.12 = (bf16[16,64,512]{2,1,0:T(8,128)(2,1)S(1)}, bf16[16,64,512]{2,1,0:T(8,128)(2,1)S(1)}) custom-call(s32[1089]{0:T(1024)S(1)} %copy-done.5, s32[64]{0:T(128)S(1)} %copy-done.20, bf16[64,256,512]{2,1,0:T(8,128)(2,1)} %next_ref.19, bf16[64,256,512]{2,1,0:T(8,128)(2,1)} %next_ref.19, bf16[64,256,512]{2,1,0:T(8,128)(2,1)} %next_ref.19, ...), custom_call_target="tpu_custom_call" | custom-call | flops 1024 | bytes 1024 | tf_op jit(solution)/shard_map/blur_bands/pallas_call | solution.py:318
  32.7 3.9 %collective-permute-done.1.refs_2_ = bf16[16,32,512]{2,1,0:T(8,128)(2,1)S(1)} collective-permute-done((bf16[16,32,512]{2,1,0:T(8,128)(2,1)S(1)}, bf16[16,32,512]{2,1,0:T(8,128)(2,1)S(1)}, u32[]{:S(2)}, u32[]{:S(2)}) %collective-permute-start.1) | collective-permute-done | bytes 524320 | tf_op jit(solution)/shard_map/ppermute | solution.py:429
  36.6 1.8 collective-permute-start.3
  38.6 1.7 collective-permute-start.5
  40.4 7.7 %blur_bands.13 = (bf16[16,64,512]{2,1,0:T(8,128)(2,1)S(1)}, bf16[16,64,512]{2,1,0:T(8,128)(2,1)S(1)}) custom-call(s32[1089]{0:T(1024)S(1)} %copy-done.5, s32[64]{0:T(128)S(1)} %copy-done.20, bf16[64,256,512]{2,1,0:T(8,128)(2,1)} %next_ref.19, bf16[64,256,512]{2,1,0:T(8,128)(2,1)} %next_ref.19, bf16[64,256,512]{2,1,0:T(8,128)(2,1)} %next_ref.19, ...), custom_call_target="tpu_custom_call" | custom-call | flops 1024 | bytes 1024 | tf_op jit(solution)/shard_map/blur_bands/pallas_call | solution.py:318
  49.4 8.4 %blur_bands.14 = (bf16[16,64,512]{2,1,0:T(8,128)(2,1)}, bf16[16,64,512]{2,1,0:T(8,128)(2,1)S(1)}) custom-call(s32[1089]{0:T(1024)S(1)} %copy-done.5, s32[64]{0:T(128)S(1)} %copy-done.20, bf16[64,256,512]{2,1,0:T(8,128)(2,1)} %next_ref.19, bf16[64,256,512]{2,1,0:T(8,128)(2,1)} %next_ref.19, bf16[64,256,512]{2,1,0:T(8,128)(2,1)} %next_ref.19, ...), custom_call_target="tpu_custom_call" | custom-call | flops 1024 | bytes 1024 | tf_op jit(solution)/shard_map/blur_bands/pallas_call | solution.py:318
  57.7 8.4 %blur_bands.15 = (bf16[16,64,512]{2,1,0:T(8,128)(2,1)}, bf16[16,64,512]{2,1,0:T(8,128)(2,1)S(1)}) custom-call(s32[1089]{0:T(1024)S(1)} %copy-done.5, s32[64]{0:T(128)S(1)} %copy-done.20, bf16[64,256,512]{2,1,0:T(8,128)(2,1)} %next_ref.19, bf16[64,256,512]{2,1,0:T(8,128)(2,1)} %next_ref.19, bf16[64,256,512]{2,1,0:T(8,128)(2,1)} %next_ref.19, ...), custom_call_target="tpu_custom_call" | custom-call | flops 1024 | bytes 1024 | tf_op jit(solution)/shard_map/blur_bands/pallas_call | solution.py:318
  67.1 18.3 %collective-permute-done.6.refs_1_ = bf16[16,64,512]{2,1,0:T(8,128)(2,1)S(1)} collective-permute-done((bf16[16,64,512]{2,1,0:T(8,128)(2,1)S(1)}, bf16[16,64,512]{2,1,0:T(8,128)(2,1)S(1)}, u32[]{:S(2)}, u32[]{:S(2)}) %collective-permute-start.6) | collective-permute-done | bytes 1048608 | tf_op jit(solution)/shard_map/ppermute | solution.py:429
  86.4 1.7 collective-permute-start.7
  88.4 1.7 collective-permute-start.10
  90.4 5.9 %blur_bands.16.refs_0_ = bf16[16,64,512]{2,1,0:T(8,128)(2,1)S(1)} custom-call(s32[1089]{0:T(1024)S(1)} %copy-done.5, s32[64]{0:T(128)S(1)} %copy-done.20, bf16[64,256,512]{2,1,0:T(8,128)(2,1)} %next_ref.19, bf16[64,256,512]{2,1,0:T(8,128)(2,1)} %next_ref.19, bf16[64,256,512]{2,1,0:T(8,128)(2,1)} %next_ref.19, f32[256,512]{1,0:T(8,128)S(1)} %copy-done, ...), custom_call_target="tpu_custom_call" | custom-call | flops 1024 | bytes 1024 | tf_op jit(solution)/shard_map/blur_bands/pallas_call | solution.py:318
  96.4 7.7 %blur_bands.17 = (bf16[16,64,512]{2,1,0:T(8,128)(2,1)S(1)}, bf16[16,64,512]{2,1,0:T(8,128)(2,1)S(1)}) custom-call(s32[1089]{0:T(1024)S(1)} %copy-done.5, s32[64]{0:T(128)S(1)} %copy-done.20, bf16[64,256,512]{2,1,0:T(8,128)(2,1)} %next_ref.19, bf16[64,256,512]{2,1,0:T(8,128)(2,1)} %next_ref.19, bf16[64,256,512]{2,1,0:T(8,128)(2,1)} %next_ref.19, ...), custom_call_target="tpu_custom_call" | custom-call | flops 1024 | bytes 1024 | tf_op jit(solution)/shard_map/blur_bands/pallas_call | solution.py:318
  106.1 7.7 %blur_bands.18 = (bf16[16,64,512]{2,1,0:T(8,128)(2,1)S(1)}, bf16[16,64,512]{2,1,0:T(8,128)(2,1)S(1)}) custom-call(s32[1089]{0:T(1024)S(1)} %copy-done.5, s32[64]{0:T(128)S(1)} %copy-done.20, bf16[64,256,512]{2,1,0:T(8,128)(2,1)} %next_ref.19, bf16[64,256,512]{2,1,0:T(8,128)(2,1)} %next_ref.19, bf16[64,256,512]{2,1,0:T(8,128)(2,1)} %next_ref.19, ...), custom_call_target="tpu_custom_call" | custom-call | flops 1024 | bytes 1024 | tf_op jit(solution)/shard_map/blur_bands/pallas_call | solution.py:318
  114.8 7.7 %blur_bands.19 = (bf16[16,64,512]{2,1,0:T(8,128)(2,1)S(1)}, bf16[16,64,512]{2,1,0:T(8,128)(2,1)S(1)}) custom-call(s32[1089]{0:T(1024)S(1)} %copy-done.5, s32[64]{0:T(128)S(1)} %copy-done.20, bf16[64,256,512]{2,1,0:T(8,128)(2,1)} %next_ref.19, bf16[64,256,512]{2,1,0:T(8,128)(2,1)} %next_ref.19, bf16[64,256,512]{2,1,0:T(8,128)(2,1)} %next_ref.19, ...), custom_call_target="tpu_custom_call" | custom-call | flops 1024 | bytes 1024 | tf_op jit(solution)/shard_map/blur_bands/pallas_call | solution.py:318
  122.6 1.0 copy-done.23
  123.6 1.9 project_band.11.total_ref
  125.6 1.9 project_band.12.total_ref
  127.5 3.2 %project_band.13.total_ref = f32[128,128]{1,0:T(8,128)S(1)} custom-call(s32[1]{0:T(128)} %constant.10.clone.1.place_ref, f32[128,128]{1,0:T(8,128)S(1)} %project_band.12.total_ref, bf16[16,64,512]{2,1,0:T(8,128)(2,1)S(1)} %copy-done.13, bf16[16,64,512]{2,1,0:T(8,128)(2,1)S(1)} %copy-done.17, bf16[8192,128]{1,0:T(8,128)(2,1)} %collective-permute-done.4.refs_2_), custom_call_target="tpu_custom_call" | custom-call | flops 1024 | bytes 1024 | tf_op jit(solution)/shard_map/project_band/pallas_call | solution.py:365
  130.7 3.5 %collective-permute-done.9.refs_1_ = bf16[16,64,512]{2,1,0:T(8,128)(2,1)} collective-permute-done((bf16[16,64,512]{2,1,0:T(8,128)(2,1)}, bf16[16,64,512]{2,1,0:T(8,128)(2,1)}, u32[]{:S(2)}, u32[]{:S(2)}) %collective-permute-start.9) | collective-permute-done | bytes 1048608 | tf_op jit(solution)/shard_map/ppermute | solution.py:429
  134.2 1.6 collective-permute-start.11
  136.3 1.5 collective-permute-start.13
  138.3 2.8 %project_band.14.total_ref = f32[128,128]{1,0:T(8,128)S(1)} custom-call(s32[1]{0:T(128)} %constant.10.clone.1.place_ref, f32[128,128]{1,0:T(8,128)S(1)} %project_band.13.total_ref, bf16[16,64,512]{2,1,0:T(8,128)(2,1)S(1)} %copy-done.7, bf16[16,64,512]{2,1,0:T(8,128)(2,1)} %collective-permute-done.9.refs_1_, bf16[8192,128]{1,0:T(8,128)(2,1)S(1)} %collective-permute-done.7.refs_2_), custom_call_target="tpu_custom_call" | custom-call | flops 1024 | bytes 1024 | tf_op jit(solution)/shard_map/project_band/pallas_call | solution.py:365
  141.1 3.2 %project_band.15.total_ref = f32[128,128]{1,0:T(8,128)S(1)} custom-call(s32[1]{0:T(128)} %constant.10.clone.1.place_ref, f32[128,128]{1,0:T(8,128)S(1)} %project_band.14.total_ref, bf16[16,64,512]{2,1,0:T(8,128)(2,1)S(1)} %get-tuple-element.97.refs_0_, bf16[16,64,512]{2,1,0:T(8,128)(2,1)} %collective-permute-done.10.refs_1_, ...), custom_call_target="tpu_custom_call" | custom-call | flops 1024 | bytes 1024 | tf_op jit(solution)/shard_map/project_band/pallas_call | solution.py:365
  144.4 18.0 %collective-permute-done.13.refs_1_ = bf16[16,64,512]{2,1,0:T(8,128)(2,1)S(1)} collective-permute-done((bf16[16,64,512]{2,1,0:T(8,128)(2,1)S(1)}, bf16[16,64,512]{2,1,0:T(8,128)(2,1)S(1)}, u32[]{:S(2)}, u32[]{:S(2)}) %collective-permute-start.13) | collective-permute-done | bytes 1048608 | tf_op jit(solution)/shard_map/ppermute | solution.py:429
  162.4 17.9 %collective-permute-done.14.refs_1_ = bf16[16,64,512]{2,1,0:T(8,128)(2,1)S(1)} collective-permute-done((bf16[16,64,512]{2,1,0:T(8,128)(2,1)S(1)}, bf16[16,64,512]{2,1,0:T(8,128)(2,1)S(1)}, u32[]{:S(2)}, u32[]{:S(2)}) %collective-permute-start.14) | collective-permute-done | bytes 1048608 | tf_op jit(solution)/shard_map/ppermute | solution.py:429
  180.4 1.6 collective-permute-start.15
  182.8 1.4 collective-permute-start.17
  184.2 1.2 project_band.16.total_ref
  185.4 1.2 project_band.17.total_ref
  186.7 14.6 %collective-permute-done.15.refs_1_ = bf16[4096,128]{1,0:T(8,128)(2,1)S(1)} collective-permute-done((bf16[4096,128]{1,0:T(8,128)(2,1)S(1)}, bf16[4096,128]{1,0:T(8,128)(2,1)S(1)}, u32[]{:S(2)}, u32[]{:S(2)}) %collective-permute-start.15) | collective-permute-done | bytes 1048608 | tf_op jit(solution)/shard_map/ppermute | solution.py:429
  201.8 1.1 collective-permute-done.16.refs_1_
  204.4 1.6 collective-permute-start.19
  206.3 2.6 %collective-permute-done.19.side_ref = f32[128,128]{1,0:T(8,128)S(1)} collective-permute-done((f32[128,128]{1,0:T(8,128)S(1)}, f32[128,128]{1,0:T(8,128)S(1)}, u32[]{:S(2)}, u32[]{:S(2)}) %collective-permute-start.19) | collective-permute-done | bytes 65568 | tf_op jit(solution)/shard_map/ppermute | solution.py:499
  209.0 1.1 collective-permute-done.20.both_ref
  210.7 1.9 merge.1
  213.4 1.6 collective-permute-start.22
  215.0 1.1 collective-permute-start.23
  217.9 2.5 collective-permute-done.23
  221.2 2.5 collective-permute-start.24
  223.7 3.4 %collective-permute-done.24.more_ref = f32[128,128]{1,0:T(8,128)S(1)} collective-permute-done((f32[128,128]{1,0:T(8,128)S(1)}, f32[128,128]{1,0:T(8,128)S(1)}, u32[]{:S(2)}, u32[]{:S(2)}) %collective-permute-start.24) | collective-permute-done | bytes 65568 | tf_op jit(solution)/shard_map/ppermute | solution.py:429
  227.9 30.0 %orthogonal_iteration.1 = (bf16[8192,128]{1,0:T(8,128)(2,1)}, f32[64,128]{1,0:T(8,128)}, f32[1,128]{1,0:T(1,128)}) custom-call(f32[128,128]{1,0:T(8,128)S(1)} %add_add_fusion.summed_ref, f32[128,128]{1,0:T(8,128)S(1)} %collective-permute-done.24.more_ref, f32[1,128]{1,0:T(1,128)S(1)} %bitcast.3, f32[128,128]{1,0:T(8,128)S(1)} %copy-done.19, ...), custom_call_target="tpu_custom_call" | custom-call | tf_op jit(solution)/shard_map/orthogonal_iteration/pallas_call | solution.py:156
  (99 shorter events, 17.2 us)
Async XLA Ops:
  7.1 8.2 %copy-start = (f32[256,512]{1,0:T(8,128)S(1)}, f32[256,512]{1,0:T(8,128)}, u32[]{:S(2)}) copy-start(f32[256,512]{1,0:T(8,128)} %refs_3_.21) | copy-start | bytes 1572868
  7.1 8.2 %copy-start.1 = (s32[256,512]{1,0:T(8,128)S(1)}, s32[256,512]{1,0:T(8,128)}, u32[]{:S(2)}) copy-start(s32[256,512]{1,0:T(8,128)} %refs_6_.16) | copy-start | bytes 1572868
  7.1 15.1 %collective-permute-start = (bf16[16,32,512]{2,1,0:T(8,128)(2,1)}, bf16[16,32,512]{2,1,0:T(8,128)(2,1)S(1)}, u32[]{:S(2)}, u32[]{:S(2)}) collective-permute-start(bf16[16,32,512]{2,1,0:T(8,128)(2,1)} %blur_bands.10), channel_id=1, source_target_pairs={{0,2},{2,0},{4,6},{6,4},{8,10},{10,8},{12,14},{14,12},{16,18},{18,... | collective-permute-start | bytes 1572872 | tf_op jit(solution)/shard_map/ppermute | solution.py:429
  15.3 7.0 %copy-start.29 = (bf16[16,32,512]{2,1,0:T(8,128)(2,1)S(1)}, bf16[16,32,512]{2,1,0:T(8,128)(2,1)}, u32[]{:S(2)}) copy-start(bf16[16,32,512]{2,1,0:T(8,128)(2,1)} %blur_bands.11) | copy-start | bytes 1572868
  15.3 9.7 %copy-start.2 = (bf16[512,512]{1,0:T(8,128)(2,1)S(1)}, bf16[512,512]{1,0:T(8,128)(2,1)}, u32[]{:S(2)}) copy-start(bf16[512,512]{1,0:T(8,128)(2,1)} %constant.27.clone.refs_6_.refs_7_) | copy-start | bytes 1572868
  15.3 9.7 %copy-start.5 = (s32[1089]{0:T(1024)S(1)}, s32[1089]{0:T(1024)}, u32[]{:S(2)}) copy-start(s32[1089]{0:T(1024)} %pad_add_fusion.place_ref) | copy-start | bytes 13072
  15.3 9.6 %copy-start.20 = (s32[64]{0:T(128)S(1)}, s32[64]{0:T(128)}, u32[]{:S(2)}) copy-start(s32[64]{0:T(128)} %group_ref.19) | copy-start | bytes 772
  17.0 19.6 %copy-start.3 = (bf16[8192,128]{1,0:T(8,128)(2,1)S(1)}, bf16[8192,128]{1,0:T(8,128)(2,1)}, u32[]{:S(2)}) copy-start(bf16[8192,128]{1,0:T(8,128)(2,1)} %basis_ref.1) | copy-start | bytes 6291460
  22.2 2.7 %collective-permute-start.2 = (bf16[64,16,512]{2,1,0:T(8,128)(2,1)S(1)}, bf16[64,16,512]{2,1,0:T(8,128)(2,1)S(1)}, u32[]{:S(2)}, u32[]{:S(2)}) collective-permute-start(bf16[64,16,512]{2,1,0:T(8,128)(2,1)S(1)} %multiply_convert_fusion), channel_id=1, source_target_pairs={{0,1},{1,0},{2,3},{3,2},{4,5},{5,4},{6,7},{7,6},{8,9},{9,8},{10,11... | collective-permute-start | bytes 3145736 | tf_op jit(solution)/shard_map/ppermute | solution.py:452
  22.3 14.3 %collective-permute-start.1 = (bf16[16,32,512]{2,1,0:T(8,128)(2,1)S(1)}, bf16[16,32,512]{2,1,0:T(8,128)(2,1)S(1)}, u32[]{:S(2)}, u32[]{:S(2)}) collective-permute-start(bf16[16,32,512]{2,1,0:T(8,128)(2,1)S(1)} %copy-done.29), channel_id=1, source_target_pairs={{0,2},{2,0},{4,6},{6,4},{8,10},{10,8},{12,14},{14,12},{16,18},{18,... | collective-permute-start | bytes 1572872 | tf_op jit(solution)/shard_map/ppermute | solution.py:429
  32.7 15.4 %copy-start.10 = (bf16[16,64,512]{2,1,0:T(8,128)(2,1)}, bf16[16,64,512]{2,1,0:T(8,128)(2,1)S(1)}, u32[]{:S(2)}) copy-start(bf16[16,64,512]{2,1,0:T(8,128)(2,1)S(1)} %get-tuple-element.80.refs_0_) | copy-start | bytes 3145732
  36.6 49.8 %collective-permute-start.3 = (bf16[8192,128]{1,0:T(8,128)(2,1)S(1)}, bf16[8192,128]{1,0:T(8,128)(2,1)S(1)}, u32[]{:S(2)}, u32[]{:S(2)}) collective-permute-start(bf16[8192,128]{1,0:T(8,128)(2,1)S(1)} %copy-done.3), channel_id=1, source_target_pairs={{0,8},{2,10},{8,16},{10,18},{16,24},{18,26},{24,28},{26,30},{28,20... | collective-permute-start | bytes 6291464 | tf_op jit(solution)/shard_map/ppermute | solution.py:429
  38.4 48.0 %collective-permute-start.4 = (bf16[8192,128]{1,0:T(8,128)(2,1)S(1)}, bf16[8192,128]{1,0:T(8,128)(2,1)}, u32[]{:S(2)}, u32[]{:S(2)}) collective-permute-start(bf16[8192,128]{1,0:T(8,128)(2,1)S(1)} %copy-done.3), channel_id=1, source_target_pairs={{0,4},{2,6},{8,0},{10,2},{16,8},{18,10},{24,16},{26,18},{28,24},{3... | collective-permute-start | bytes 6291464 | tf_op jit(solution)/shard_map/ppermute | solution.py:429
  38.6 27.5 %collective-permute-start.5 = (bf16[16,64,512]{2,1,0:T(8,128)(2,1)S(1)}, bf16[16,64,512]{2,1,0:T(8,128)(2,1)S(1)}, u32[]{:S(2)}, u32[]{:S(2)}) collective-permute-start(bf16[16,64,512]{2,1,0:T(8,128)(2,1)S(1)} %get-tuple-element.69), channel_id=1, source_target_pairs={{0,2},{2,0},{4,6},{6,4},{8,10},{10,8},{12,14},{14,12},{16,18},{18,... | collective-permute-start | bytes 3145736 | tf_op jit(solution)/shard_map/ppermute | solution.py:429
  49.1 36.3 %collective-permute-start.6 = (bf16[16,64,512]{2,1,0:T(8,128)(2,1)S(1)}, bf16[16,64,512]{2,1,0:T(8,128)(2,1)S(1)}, u32[]{:S(2)}, u32[]{:S(2)}) collective-permute-start(bf16[16,64,512]{2,1,0:T(8,128)(2,1)S(1)} %get-tuple-element.70), channel_id=1, source_target_pairs={{0,2},{2,0},{4,6},{6,4},{8,10},{10,8},{12,14},{14,12},{16,18},{18,... | collective-permute-start | bytes 3145736 | tf_op jit(solution)/shard_map/ppermute | solution.py:429
  57.7 8.4 %copy-start.6 = (bf16[16,64,512]{2,1,0:T(8,128)(2,1)}, bf16[16,64,512]{2,1,0:T(8,128)(2,1)S(1)}, u32[]{:S(2)}) copy-start(bf16[16,64,512]{2,1,0:T(8,128)(2,1)S(1)} %get-tuple-element.95.refs_0_) | copy-start | bytes 3145732
  86.4 47.9 %collective-permute-start.7 = (bf16[8192,128]{1,0:T(8,128)(2,1)S(1)}, bf16[8192,128]{1,0:T(8,128)(2,1)S(1)}, u32[]{:S(2)}, u32[]{:S(2)}) collective-permute-start(bf16[8192,128]{1,0:T(8,128)(2,1)S(1)} %collective-permute-done.3.refs_4_.refs_3_), channel_id=1, source_target_pairs={{0,8},{2,10},{8,16},{10,18},{16,24},{18,26},{24,28},{26,30},{28,20... | collective-permute-start | bytes 6291464 | tf_op jit(solution)/shard_map/ppermute | solution.py:429
  88.1 46.1 %collective-permute-start.8 = (bf16[8192,128]{1,0:T(8,128)(2,1)}, bf16[8192,128]{1,0:T(8,128)(2,1)}, u32[]{:S(2)}, u32[]{:S(2)}) collective-permute-start(bf16[8192,128]{1,0:T(8,128)(2,1)} %collective-permute-done.4.refs_2_), channel_id=1, source_target_pairs={{0,4},{2,6},{8,0},{10,2},{16,8},{18,10},{24,16},{26,18},{28,24},{3... | collective-permute-start | bytes 6291464 | tf_op jit(solution)/shard_map/ppermute | solution.py:429
  88.4 42.3 %collective-permute-start.10 = (bf16[16,64,512]{2,1,0:T(8,128)(2,1)}, bf16[16,64,512]{2,1,0:T(8,128)(2,1)}, u32[]{:S(2)}, u32[]{:S(2)}) collective-permute-start(bf16[16,64,512]{2,1,0:T(8,128)(2,1)} %get-tuple-element.85), channel_id=1, source_target_pairs={{0,2},{2,0},{4,6},{6,4},{8,10},{10,8},{12,14},{14,12},{16,18},{18,... | collective-permute-start | bytes 3145736 | tf_op jit(solution)/shard_map/ppermute | solution.py:429
  90.1 44.2 %collective-permute-start.9 = (bf16[16,64,512]{2,1,0:T(8,128)(2,1)}, bf16[16,64,512]{2,1,0:T(8,128)(2,1)}, u32[]{:S(2)}, u32[]{:S(2)}) collective-permute-start(bf16[16,64,512]{2,1,0:T(8,128)(2,1)} %get-tuple-element.84), channel_id=1, source_target_pairs={{0,2},{2,0},{4,6},{6,4},{8,10},{10,8},{12,14},{14,12},{16,18},{18,... | collective-permute-start | bytes 3145736 | tf_op jit(solution)/shard_map/ppermute | solution.py:429
  123.6 1.9 copy-start.11
  123.6 1.9 copy-start.15
  125.5 1.9 copy-start.13
  125.6 1.9 copy-start.17
  127.5 8.8 %copy-start.28 = (bf16[16,64,512]{2,1,0:T(8,128)(2,1)S(1)}, bf16[16,64,512]{2,1,0:T(8,128)(2,1)}, u32[]{:S(2)}) copy-start(bf16[16,64,512]{2,1,0:T(8,128)(2,1)} %copy-done.27) | copy-start | bytes 3145732
  127.5 10.3 %copy-start.26 = (bf16[16,64,512]{2,1,0:T(8,128)(2,1)S(1)}, bf16[16,64,512]{2,1,0:T(8,128)(2,1)}, u32[]{:S(2)}) copy-start(bf16[16,64,512]{2,1,0:T(8,128)(2,1)} %copy-done.25) | copy-start | bytes 3145732
  127.5 10.8 %copy-start.7 = (bf16[16,64,512]{2,1,0:T(8,128)(2,1)S(1)}, bf16[16,64,512]{2,1,0:T(8,128)(2,1)}, u32[]{:S(2)}) copy-start(bf16[16,64,512]{2,1,0:T(8,128)(2,1)} %copy-done.6) | copy-start | bytes 3145732
  134.2 46.1 %collective-permute-start.11 = (bf16[8192,128]{1,0:T(8,128)(2,1)S(1)}, bf16[8192,128]{1,0:T(8,128)(2,1)S(1)}, u32[]{:S(2)}, u32[]{:S(2)}) collective-permute-start(bf16[8192,128]{1,0:T(8,128)(2,1)S(1)} %collective-permute-done.7.refs_2_), channel_id=1, source_target_pairs={{0,8},{2,10},{8,16},{10,18},{16,24},{18,26},{24,28},{26,30},{28,20... | collective-permute-start | bytes 6291464 | tf_op jit(solution)/shard_map/ppermute | solution.py:429
  135.8 44.5 %collective-permute-start.12 = (bf16[8192,128]{1,0:T(8,128)(2,1)}, bf16[8192,128]{1,0:T(8,128)(2,1)S(1)}, u32[]{:S(2)}, u32[]{:S(2)}) collective-permute-start(bf16[8192,128]{1,0:T(8,128)(2,1)} %collective-permute-done.8.refs_2_), channel_id=1, source_target_pairs={{0,4},{2,6},{8,0},{10,2},{16,8},{18,10},{24,16},{26,18},{28,24},{3... | collective-permute-start | bytes 6291464 | tf_op jit(solution)/shard_map/ppermute | solution.py:429
  136.3 26.1 %collective-permute-start.13 = (bf16[16,64,512]{2,1,0:T(8,128)(2,1)S(1)}, bf16[16,64,512]{2,1,0:T(8,128)(2,1)S(1)}, u32[]{:S(2)}, u32[]{:S(2)}) collective-permute-start(bf16[16,64,512]{2,1,0:T(8,128)(2,1)S(1)} %copy-done.28), channel_id=1, source_target_pairs={{0,2},{2,0},{4,6},{6,4},{8,10},{10,8},{12,14},{14,12},{16,18},{18,... | collective-permute-start | bytes 3145736 | tf_op jit(solution)/shard_map/ppermute | solution.py:429
  137.8 42.5 %collective-permute-start.14 = (bf16[16,64,512]{2,1,0:T(8,128)(2,1)S(1)}, bf16[16,64,512]{2,1,0:T(8,128)(2,1)S(1)}, u32[]{:S(2)}, u32[]{:S(2)}) collective-permute-start(bf16[16,64,512]{2,1,0:T(8,128)(2,1)S(1)} %copy-done.26), channel_id=1, source_target_pairs={{0,2},{2,0},{4,6},{6,4},{8,10},{10,8},{12,14},{14,12},{16,18},{18,... | collective-permute-start | bytes 3145736 | tf_op jit(solution)/shard_map/ppermute | solution.py:429
  144.4 38.4 %copy-start.24 = (bf16[16,64,512]{2,1,0:T(8,128)(2,1)S(1)}, bf16[16,64,512]{2,1,0:T(8,128)(2,1)}, u32[]{:S(2)}) copy-start(bf16[16,64,512]{2,1,0:T(8,128)(2,1)} %copy-done.23) | copy-start | bytes 3145732
  144.4 39.8 %copy-start.9 = (bf16[16,64,512]{2,1,0:T(8,128)(2,1)S(1)}, bf16[16,64,512]{2,1,0:T(8,128)(2,1)}, u32[]{:S(2)}) copy-start(bf16[16,64,512]{2,1,0:T(8,128)(2,1)} %copy-done.8) | copy-start | bytes 3145732
  180.4 20.9 %collective-permute-start.15 = (bf16[4096,128]{1,0:T(8,128)(2,1)S(1)}, bf16[4096,128]{1,0:T(8,128)(2,1)S(1)}, u32[]{:S(2)}, u32[]{:S(2)}) collective-permute-start(bf16[4096,128]{1,0:T(8,128)(2,1)S(1)} %slice.6), channel_id=1, source_target_pairs={{0,8},{2,10},{8,16},{10,18},{16,24},{18,26},{24,28},{26,30},{28,20... | collective-permute-start | bytes 3145736 | tf_op jit(solution)/shard_map/ppermute | solution.py:429
  182.0 20.8 %collective-permute-start.16 = (bf16[4096,128]{1,0:T(8,128)(2,1)S(1)}, bf16[4096,128]{1,0:T(8,128)(2,1)S(1)}, u32[]{:S(2)}, u32[]{:S(2)}) collective-permute-start(bf16[4096,128]{1,0:T(8,128)(2,1)S(1)} %slice.7), channel_id=1, source_target_pairs={{0,4},{2,6},{8,0},{10,2},{16,8},{18,10},{24,16},{26,18},{28,24},{3... | collective-permute-start | bytes 3145736 | tf_op jit(solution)/shard_map/ppermute | solution.py:429
  182.8 20.5 %collective-permute-start.17 = (bf16[16,64,512]{2,1,0:T(8,128)(2,1)S(1)}, bf16[16,64,512]{2,1,0:T(8,128)(2,1)S(1)}, u32[]{:S(2)}, u32[]{:S(2)}) collective-permute-start(bf16[16,64,512]{2,1,0:T(8,128)(2,1)S(1)} %copy-done.24), channel_id=1, source_target_pairs={{0,2},{2,0},{4,6},{6,4},{8,10},{10,8},{12,14},{14,12},{16,18},{18,... | collective-permute-start | bytes 3145736 | tf_op jit(solution)/shard_map/ppermute | solution.py:429
  203.3 23.9 %copy-start.4 = (bf16[8192,128]{1,0:T(8,128)(2,1)S(1)}, bf16[8192,128]{1,0:T(8,128)(2,1)}, u32[]{:S(2)}) copy-start(bf16[8192,128]{1,0:T(8,128)(2,1)} %basis_ref.1) | copy-start | bytes 6291460
  203.3 23.8 %copy-start.19 = (f32[128,128]{1,0:T(8,128)S(1)}, f32[128,128]{1,0:T(8,128)}, u32[]{:S(2)}) copy-start(f32[128,128]{1,0:T(8,128)} %start_ref.1) | copy-start | bytes 196612
  203.3 23.8 %copy-start.22 = (f32[128]{0:T(128)S(1)}, f32[128]{0:T(128)}, u32[]{:S(2)}) copy-start(f32[128]{0:T(128)} %param.13) | copy-start | bytes 1540
  204.3 5.7 %copy-start.18 = (f32[128,128]{1,0:T(8,128)}, f32[128,128]{1,0:T(8,128)S(1)}, u32[]{:S(2)}) copy-start(f32[128,128]{1,0:T(8,128)S(1)} %project_band.21.total_ref) | copy-start | bytes 196612
  204.4 1.9 collective-permute-start.18
  204.4 4.5 %collective-permute-start.19 = (f32[128,128]{1,0:T(8,128)S(1)}, f32[128,128]{1,0:T(8,128)S(1)}, u32[]{:S(2)}, u32[]{:S(2)}) collective-permute-start(f32[128,128]{1,0:T(8,128)S(1)} %project_band.21.total_ref), channel_id=1, source_target_pairs={{0,2},{1,3},{2,0},{3,1},{4,6},{5,7},{6,4},{7,5},{8,10},{9,11},{10,... | collective-permute-start | bytes 196616 | tf_op jit(solution)/shard_map/ppermute | solution.py:499
  206.0 4.0 %collective-permute-start.20 = (f32[128,128]{1,0:T(8,128)S(1)}, f32[128,128]{1,0:T(8,128)S(1)}, u32[]{:S(2)}, u32[]{:S(2)}) collective-permute-start(f32[128,128]{1,0:T(8,128)S(1)} %project_band.21.total_ref), channel_id=1, source_target_pairs={{0,3},{1,2},{2,1},{3,0},{4,7},{5,6},{6,5},{7,4},{8,11},{9,10},{10,... | collective-permute-start | bytes 196616 | tf_op jit(solution)/shard_map/ppermute | solution.py:499
  206.3 3.8 %copy-start.30 = (f32[128,128]{1,0:T(8,128)}, f32[128,128]{1,0:T(8,128)S(1)}, u32[]{:S(2)}) copy-start(f32[128,128]{1,0:T(8,128)S(1)} %collective-permute-done.18.strip_ref) | copy-start | bytes 196612
  212.6 4.5 %collective-permute-start.21 = (f32[128,128]{1,0:T(8,128)}, f32[128,128]{1,0:T(8,128)S(1)}, u32[]{:S(2)}, u32[]{:S(2)}) collective-permute-start(f32[128,128]{1,0:T(8,128)} %get-tuple-element.112), channel_id=1, source_target_pairs={{0,4},{2,6},{4,0},{6,2},{8,12},{10,14},{12,8},{14,10},{16,20},{18,... | collective-permute-start | bytes 196616 | tf_op jit(solution)/shard_map/ppermute | solution.py:429
  213.4 4.5 %collective-permute-start.22 = (f32[128,128]{1,0:T(8,128)}, f32[128,128]{1,0:T(8,128)S(1)}, u32[]{:S(2)}, u32[]{:S(2)}) collective-permute-start(f32[128,128]{1,0:T(8,128)} %get-tuple-element.112), channel_id=1, source_target_pairs={{0,8},{2,10},{4,12},{6,14},{8,0},{10,2},{12,4},{14,6},{16,24},{18,... | collective-permute-start | bytes 196616 | tf_op jit(solution)/shard_map/ppermute | solution.py:429
  215.0 5.4 %collective-permute-start.23 = (f32[128,128]{1,0:T(8,128)}, f32[128,128]{1,0:T(8,128)S(1)}, u32[]{:S(2)}, u32[]{:S(2)}) collective-permute-start(f32[128,128]{1,0:T(8,128)} %get-tuple-element.112), channel_id=1, source_target_pairs={{0,12},{2,14},{4,8},{6,10},{8,4},{10,6},{12,0},{14,2},{16,28},{18,... | collective-permute-start | bytes 196616 | tf_op jit(solution)/shard_map/ppermute | solution.py:429
  221.2 5.9 %collective-permute-start.24 = (f32[128,128]{1,0:T(8,128)S(1)}, f32[128,128]{1,0:T(8,128)S(1)}, u32[]{:S(2)}, u32[]{:S(2)}) collective-permute-start(f32[128,128]{1,0:T(8,128)S(1)} %add_add_fusion.summed_ref), channel_id=1, source_target_pairs={{0,16},{2,18},{4,20},{6,22},{8,24},{10,26},{12,28},{14,30},{16,0},... | collective-permute-start | bytes 196616 | tf_op jit(solution)/shard_map/ppermute | solution.py:429
  (10 other events, 9.5 us)

commit v4 on v3

--- a/solution.py
+++ b/solution.py
@@ -16,6 +16,7 @@
 DECAY_RATE = 0.7
 HIGHEST = lax.Precision.HIGHEST
 PANEL = 64
+BLOCK = 8
 VMEM_BYTES = 32 * 1024 * 1024
 BLUR_BYTES = 49 * 1024 * 1024
 
@@ -57,49 +58,55 @@
     down = (((0,), (0,)), ((), ()))
     normal = lax.dot_general(product, product, across, precision=HIGHEST, preferred_element_type=jnp.float32)
     state = jnp.concatenate([normal, product], axis=1)
-    shape = (PANEL, size)
+    shape = (BLOCK, size)
     rows = lax.broadcasted_iota(jnp.int32, shape, 0)
     lanes = lax.broadcasted_iota(jnp.int32, shape, 1)
+    wide = lambda values: jnp.broadcast_to(values, shape)
     finished = []
     for base in range(0, size, PANEL):
-        left, right = (state[:PANEL, :size], state[:PANEL, size:])
-        for j in range(0, PANEL, 4):
-            at = base + j
-            col = [jnp.broadcast_to(left[:, at + i : at + i + 1], shape) for i in range(4)]
-            p = {(r, s): jnp.broadcast_to(col[s][j + r : j + r + 1], shape) for s in range(4) for r in range(s + 1)}
-            inverse = reciprocal(p[0, 0] * p[1, 1] - p[0, 1] * p[0, 1])
-            a00, a01, a11 = (p[1, 1] * inverse, -p[0, 1] * inverse, p[0, 0] * inverse)
-            t00, t10 = (a00 * p[0, 2] + a01 * p[1, 2], a01 * p[0, 2] + a11 * p[1, 2])
-            t01, t11 = (a00 * p[0, 3] + a01 * p[1, 3], a01 * p[0, 3] + a11 * p[1, 3])
-            q00 = p[2, 2] - p[0, 2] * t00 - p[1, 2] * t10
-            q01 = p[2, 3] - p[0, 2] * t01 - p[1, 2] * t11
-            q11 = p[3, 3] - p[0, 3] * t01 - p[1, 3] * t11
-            inverse = reciprocal(q00 * q11 - q01 * q01)
-            b00, b01, b11 = (q11 * inverse, -q01 * inverse, q00 * inverse)
-            first = p[0, 1] * reciprocal(p[0, 0])
-            third = q01 * reciprocal(q00)
-            col2 = col[2] - col[0] * t00 - col[1] * t10
-            col3 = col[3] - col[0] * t01 - col[1] * t11
-            f2 = col2 * b00 + col3 * b01
-            f3 = col2 * b01 + col3 * b11
-            f0 = col[0] * a00 + col[1] * a01 - f2 * t00 - f3 * t01
-            f1 = col[0] * a01 + col[1] * a11 - f2 * t10 - f3 * t11
-            below = rows > j + 3
-            row1, row2, row3 = (rows == j + 1, rows == j + 2, rows == j + 3)
-            zero = jnp.zeros(shape, jnp.float32)
-            inner = jnp.where(row2, t00, jnp.where(row3, t01 - third * t00, zero))
-            f0 = jnp.where(below, f0, jnp.where(row1, first, inner))
-            f1 = jnp.where(below, f1, jnp.where(row2, t10, jnp.where(row3, t11 - third * t10, zero)))
-            f2 = jnp.where(below, f2, jnp.where(row3, third, zero))
-            f3 = jnp.where(below, f3, zero)
-            lines = [jnp.broadcast_to(left[j + i : j + i + 1], shape) for i in range(4)]
-            left = left - ((f0 * lines[0] + f1 * lines[1]) + (f2 * lines[2] + f3 * lines[3]))
-            lines = [jnp.broadcast_to(right[j + i : j + i + 1], shape) for i in range(4)]
-            right = right - ((f0 * lines[0] + f1 * lines[1]) + (f2 * lines[2] + f3 * lines[3]))
-        pivots = jnp.sum(jnp.where(lanes == base + rows, left, 0.0), axis=1, keepdims=True)
-        scale = lax.rsqrt(pivots)
-        left = left * scale
-        right = right * scale
+        left = [state[row : row + BLOCK, :size] for row in range(0, PANEL, BLOCK)]
+        right = [state[row : row + BLOCK, size:] for row in range(0, PANEL, BLOCK)]
+        for at in range(PANEL // BLOCK):
+            column = base + at * BLOCK
+            below = range(at + 1, PANEL // BLOCK)
+            col = [
+                {i: wide(left[i][:, column + s : column + s + 1]) for i in (at, *below)} for s in range(BLOCK)
+            ]
+            p = {(r, s): wide(col[s][at][r : r + 1]) for s in range(BLOCK) for r in range(s + 1)}
+            lines = [(wide(left[at][s : s + 1]), wide(right[at][s : s + 1])) for s in range(BLOCK)]
+            for u in range(0, BLOCK, 2):
+                v = u + 1
+                inverse = reciprocal(p[u, u] * p[v, v] - p[u, v] * p[u, v])
+                a00, a01, a11 = (p[v, v] * inverse, -p[u, v] * inverse, p[u, u] * inverse)
+                within = p[u, v] * reciprocal(p[u, u])
+                later = range(v + 1, BLOCK)
+                t0 = {s: a00 * p[u, s] + a01 * p[v, s] for s in later}
+                t1 = {s: a01 * p[u, s] + a11 * p[v, s] for s in later}
+                for s in later:
+                    for r in range(v + 1, s + 1):
+                        p[r, s] = p[r, s] - (p[u, r] * t0[s] + p[v, r] * t1[s])
+                    for i in below:
+                        col[s][i] = col[s][i] - (col[u][i] * t0[s] + col[v][i] * t1[s])
+                    lines[s] = tuple(
+                        line - (t0[s] * first + t1[s] * second)
+                        for line, first, second in zip(lines[s], lines[u], lines[v])
+                    )
+                for i in below:
+                    f0 = col[u][i] * a00 + col[v][i] * a01
+                    f1 = col[u][i] * a01 + col[v][i] * a11
+                    left[i] = left[i] - (f0 * lines[u][0] + f1 * lines[v][0])
+                    right[i] = right[i] - (f0 * lines[u][1] + f1 * lines[v][1])
+                lines[v] = tuple(second - within * first for first, second in zip(lines[u], lines[v]))
+            new_left, new_right = lines[0]
+            for s in range(1, BLOCK):
+                new_left = jnp.where(rows == s, lines[s][0], new_left)
+                new_right = jnp.where(rows == s, lines[s][1], new_right)
+            pivots = jnp.sum(jnp.where(lanes == column + rows, new_left, 0.0), axis=1, keepdims=True)
+            scale = lax.rsqrt(pivots)
+            left[at] = new_left * scale
+            right[at] = new_right * scale
+        left = jnp.concatenate(left, axis=0)
+        right = jnp.concatenate(right, axis=0)
         finished.append(right)
         if base + PANEL < size:
             update = lax.dot_general(
@@ -113,15 +120,39 @@
     return jnp.concatenate(finished, axis=0)
 
 
+def packed(matrix):
+    half = matrix.shape[0] // 2
+    rows = lax.broadcasted_iota(jnp.int32, (half, 2 * half), 0)
+    lanes = lax.broadcasted_iota(jnp.int32, (half, 2 * half), 1)
+    lower = pltpu.roll(matrix[half:], half, 1)
+    diagonal = jnp.sum(jnp.where(lanes == rows, lower, 0.0), axis=0, keepdims=True)
+    return jnp.concatenate(
+        [jnp.where(lanes < rows, lower, matrix[:half]), jnp.broadcast_to(diagonal, (BLOCK, 2 * half))], axis=0
+    )
+
+
+def unpacked(values):
+    size = values.shape[1]
+    half = size // 2
+    rows = lax.broadcasted_iota(jnp.int32, (half, size), 0)
+    lanes = lax.broadcasted_iota(jnp.int32, (half, size), 1)
+    entries = values[:half]
+    diagonal = jnp.broadcast_to(values[half : half + 1], (half, size))
+    lower = jnp.where(lanes < rows, entries, jnp.where(lanes == rows, diagonal, 0.0))
+    part = jnp.concatenate([jnp.where(lanes >= rows, entries, 0.0), pltpu.roll(lower, half, 1)], axis=0)
+    on = lax.broadcasted_iota(jnp.int32, (size, size), 0) == lax.broadcasted_iota(jnp.int32, (size, size), 1)
+    return part + part.T - jnp.where(on, part, 0.0)
+
+
 def rotate_kernel(frames, chunk, summed_ref, more_ref, sigma_ref, start_ref, coeffs_ref, basis_ref, basis_out, coeffs_out, sigma_out,
                   held_ref, turned_ref, come_sem, go_sem):
     come = pltpu.make_async_copy(basis_ref, held_ref, come_sem)
     come.start()
-    size = summed_ref.shape[0]
+    size = summed_ref.shape[1]
     across = (((1,), (1,)), ((), ()))
     diagonal = lax.broadcasted_iota(jnp.int32, (size, size), 0) == lax.broadcasted_iota(jnp.int32, (size, size), 1)
     sigma = jnp.broadcast_to(sigma_ref[...], (size, size))
-    gram = jnp.where(diagonal, sigma * sigma, 0.0) + (summed_ref[...] + more_ref[...]) * (1.0 / frames)
+    gram = jnp.where(diagonal, sigma * sigma, 0.0) + unpacked(summed_ref[...] + more_ref[...]) * (1.0 / frames)
 
     def step(_, turned):
         return orthonormal_rows(jnp.dot(turned, gram, precision=HIGHEST, preferred_element_type=jnp.float32))
@@ -174,6 +205,15 @@
     return (new_basis, new_coeffs, new_sigma.reshape(size))
 
 
+def packed_alone(matrix):
+    def kernel(matrix_ref, out_ref):
+        out_ref[...] = packed(matrix_ref[...])
+
+    size = matrix.shape[0]
+    shape = jax.ShapeDtypeStruct((size // 2 + BLOCK, size), jnp.float32)
+    return pl.pallas_call(kernel, out_shape=shape, name="pack")(matrix)
+
+
 def gathered_body(raw_frames, dark_frame, dead_mask, frame_group, prior_sigma, start_rotation, basis):
     frame_count, strip_rows, columns = raw_frames.shape
     corrected = (
@@ -212,6 +252,7 @@
     total_frames = frame_count * lax.axis_size("frames")
     local_gram = jnp.dot(coeffs.T, coeffs, precision=lax.Precision.HIGHEST)
     summed_gram = summed_over(local_gram, "frames")
+    summed_gram = packed_alone(summed_gram)
     return rotated(summed_gram, jnp.zeros_like(summed_gram), total_frames, prior_sigma, start_rotation, coeffs, basis)
 
 
@@ -223,14 +264,16 @@
 
 
 def entry(place, at):
-    return place[1 + place[0] * PLACES + at]
-
-
-def blur_kernel(slot, outputs, begin, place_ref, group_ref, main_ref, prev_ref, next_ref, *refs):
+    index, table = place
+    return table[index[0] * PLACES + at]
+
+
+def blur_kernel(slot, outputs, begin, index_ref, table_ref, group_ref, main_ref, prev_ref, next_ref, *refs):
+    place = (index_ref, table_ref)
     edge_ref, refs = (refs[0], refs[1:]) if slot else (None, refs)
     darks, masks, banded_ref, refs = (refs[:3], refs[3:6], refs[6], refs[7:])
     out_refs, (rows_ref, lines_ref, blurred_ref) = (refs[: len(outputs)], refs[len(outputs) :])
-    side = entry(place_ref, 4 * slot + 2)
+    side = entry(place, 4 * slot + 2)
     frames, height, columns = main_ref.shape
     span = height + 2 * EDGE
     parts = [main_ref[...], prev_ref[...], next_ref[...]]
@@ -240,10 +283,10 @@
     ]
     top, bottom = (top[:, BAND - EDGE :], bottom[:, :EDGE])
     if slot:
-        upper = entry(place_ref, 0) == 0
+        upper = entry(place, 0) == 0
         edge = edge_ref[...].astype(jnp.float32)
-        top = jnp.where(entry(place_ref, 4 * slot + 3) == 1, jnp.where(upper, 0.0, edge[:, BAND - EDGE :]), top)
-        bottom = jnp.where(entry(place_ref, 4 * slot + 4) == 1, jnp.where(upper, edge[:, :EDGE], 0.0), bottom)
+        top = jnp.where(entry(place, 4 * slot + 3) == 1, jnp.where(upper, 0.0, edge[:, BAND - EDGE :]), top)
+        bottom = jnp.where(entry(place, 4 * slot + 4) == 1, jnp.where(upper, edge[:, :EDGE], 0.0), bottom)
     tiles = columns // 128
     flat_ref = rows_ref.reshape(tiles * frames * span, 128)
     for tile in range(tiles):
@@ -294,19 +337,19 @@
     edges = () if edge is None else (edge,)
 
     def pixels(size, at):
-        return pl.BlockSpec((size, columns), lambda f, place, group: (at(place), 0))
+        return pl.BlockSpec((size, columns), lambda f, index, table, group: (at((index, table)), 0))
 
     def frames(size, at):
-        return pl.BlockSpec((FRAME_BLOCK, size, columns), lambda f, place, group: (f + skipped, at(place), 0))
+        return pl.BlockSpec((FRAME_BLOCK, size, columns), lambda f, index, table, group: (f + skipped, at((index, table)), 0))
 
     grid_spec = pltpu.PrefetchScalarGridSpec(
-        num_scalar_prefetch=2,
+        num_scalar_prefetch=3,
         grid=(frame_count // FRAME_BLOCK,),
         in_specs=[frames(*row) for row in rows]
         + [frames(BAND, lambda place: 0)] * len(edges)
         + [pixels(*row) for row in rows] * 2
-        + [pl.BlockSpec(banded.shape, lambda f, place, group: (0, 0))],
-        out_specs=[pl.BlockSpec((BAND, FRAME_BLOCK, columns), lambda f, place, group: (0, f, 0))] * len(outputs),
+        + [pl.BlockSpec(banded.shape, lambda f, index, table, group: (0, 0))],
+        out_specs=[pl.BlockSpec((BAND, FRAME_BLOCK, columns), lambda f, index, table, group: (0, f, 0))] * len(outputs),
         scratch_shapes=[
             pltpu.VMEM((columns // 128, FRAME_BLOCK, height + 2 * EDGE, 128), jnp.float32),
             pltpu.VMEM((lines * FRAME_BLOCK, columns), jnp.bfloat16),
@@ -322,10 +365,10 @@
         compiler_params=pltpu.CompilerParams(vmem_limit_bytes=60 * 1024 * 1024 if starts else BLUR_BYTES),
         cost_estimate=pl.CostEstimate(flops=1024, bytes_accessed=1024, transcendentals=0),
         name="blur_bands",
-    )(place, frame_group, *[raw_frames] * 3, *edges, *[dark_frame] * 3, *[dead_mask] * 3, banded)
-
-
-def project_kernel(slot, at, parts, place_ref, total_ref, *refs):
+    )(*place, frame_group, *[raw_frames] * 3, *edges, *[dark_frame] * 3, *[dead_mask] * 3, banded)
+
+
+def project_kernel(slot, at, parts, index_ref, table_ref, total_ref, *refs):
     line_refs, basis_refs, out_ref = (refs[:parts], refs[parts:-1], refs[-1])
     columns = line_refs[0].shape[2]
 
@@ -345,7 +388,7 @@
     if len(basis_refs) == 1:
         add(basis_refs[0])
     else:
-        here = entry(place_ref, PLACES - 1) == slot
+        here = entry((index_ref, table_ref), PLACES - 1) == slot
         pl.when(here)(lambda: add(basis_refs[0]))
         pl.when(jnp.logical_not(here))(lambda: add(basis_refs[1]))
 
@@ -359,24 +402,24 @@
     size = basis.shape[1]
     skipped = first_row // step
     steps = basis.shape[0] // columns // step
-    whole = pl.BlockSpec(total.shape, lambda i, place: (0, 0))
-    other, place, slot = choice or (None, jnp.zeros((1,), jnp.int32), 0)
+    whole = pl.BlockSpec(total.shape, lambda i, index, table: (0, 0))
+    other, place, slot = choice or (None, [jnp.zeros((1,), jnp.int32)] * 2, 0)
     blocks = (basis,) if choice is None else (basis, other)
     return pl.pallas_call(
         functools.partial(project_kernel, slot, at, len(lines)),
         grid_spec=pltpu.PrefetchScalarGridSpec(
-            num_scalar_prefetch=1,
+            num_scalar_prefetch=2,
             grid=(steps,),
             in_specs=[whole]
-            + [pl.BlockSpec((step, *values.shape[1:]), lambda i, place: (i + skipped, 0, 0)) for values in lines]
-            + [pl.BlockSpec((step * columns, size), lambda i, place: (i, 0))] * len(blocks),
+            + [pl.BlockSpec((step, *values.shape[1:]), lambda i, index, table: (i + skipped, 0, 0)) for values in lines]
+            + [pl.BlockSpec((step * columns, size), lambda i, index, table: (i, 0))] * len(blocks),
             out_specs=whole,
         ),
         out_shape=jax.ShapeDtypeStruct(total.shape, jnp.float32),
         compiler_params=pltpu.CompilerParams(vmem_limit_bytes=VMEM_BYTES),
         cost_estimate=pl.CostEstimate(flops=1024, bytes_accessed=1024, transcendentals=0),
         name="project_band",
-    )(place, total, *lines, *blocks)
+    )(*place, total, *lines, *blocks)
 
 
 def merge_kernel(total_ref, strip_ref, side_ref, both_ref, coeffs_out, gram_out):
@@ -390,7 +433,7 @@
         if not grams:
             coeffs_out[...] = coeffs
         grams.append(lax.dot_general(coeffs, coeffs, down, precision=HIGHEST, preferred_element_type=jnp.float32))
-    gram_out[...] = grams[0] + grams[1]
+    gram_out[...] = packed(grams[0] + grams[1])
 
 
 def placement():
@@ -418,7 +461,7 @@
     ring = len(RING)
     strip = lax.axis_index("strips")
     index = lax.axis_index(("frames", "strips"))
-    place = jnp.concatenate([index.reshape(1).astype(jnp.int32), jnp.asarray(placement())])
+    place = (index.reshape(1).astype(jnp.int32), jnp.asarray(placement()))
 
     def links(by):
         return [
@@ -502,7 +545,7 @@
         merge_kernel,
         out_shape=(
             jax.ShapeDtypeStruct((frame_count, size), jnp.float32),
-            jax.ShapeDtypeStruct((size, size), jnp.float32),
+            jax.ShapeDtypeStruct((size // 2 + BLOCK, size), jnp.float32),
         ),
         name="merge",
     )(total, *flips)

time: 259 us -> 250 us (0.965)
  Pallas kernels: 121 us -> 114 us
    pallas_call x1, Pallas kernels: 30 us -> 22.9 us  [rotated(): pl.pallas_call(functools.partial(rotate_kernel, total_frames, chunk), in_...]
  transfers between devices with their start and end apart: 25 -> 25, of which waited for: 15 -> 15; matrix products, arithmetic and copies ran while one was open for 1% -> 1% of each run, Pallas kernels for 32% -> 34%
where the time goes in v4:
time: 250 us; the launch traced here: 249 us
  Pallas kernels  114 us (46%)
  waiting for transfers between devices  93.4 us (37%)
  starting transfers between devices  28.6 us (11%)
  local copies, waits for them, and re-layouts  8.55 us (3%)
    ppermute x21, waiting for transfers between devices, paired_body(): move = lambda values, pairs: lax.ppermute(values, 'frames', pairs)  88.7 us
    pallas_call x10, Pallas kernels, blurred_bands(): pl.pallas_call(functools.partial(blur_kernel, slot, outputs, begin), grid...  72.3 us
    ppermute x21, starting transfers between devices, paired_body(): move = lambda values, pairs: lax.ppermute(values, 'frames', pairs)  26.7 us
    pallas_call x1, Pallas kernels, rotated(): pl.pallas_call(functools.partial(rotate_kernel, total_frames, chunk), in_...  22.9 us
    pallas_call x11, Pallas kernels, projected(): pl.pallas_call(functools.partial(project_kernel, slot, at, len(lines)), g...  17.3 us
    unnamed x66, local copies, waits for them, and re-layouts  8.39 us
  transfers between devices with their start and end apart: 25, of which 15 were waited for; matrix products, arithmetic and copies ran while one was open for 1% of the time, Pallas kernels for 34%

profile of v4, /device:TPU:0, one launch (start us, length us, event | category | flops | bytes accessed | tf_op | source)
XLA Modules:
  0.0 248.7 jit_solution(15601107757093896294)
XLA Ops:
  0.6 5.1 %blur_bands.10 = bf16[16,32,512]{2,1,0:T(8,128)(2,1)} custom-call(s32[1]{0:T(128)} %bitcast.index_ref, s32[1088]{0:T(1024)} %constant.26.clone.table_ref, s32[64]{0:T(128)} %group_ref.19, bf16[64,256,512]{2,1,0:T(8,128)(2,1)} %next_ref.19, bf16[64,256,512]{2,1,0:T(8,128)(2,1)} %next_ref.19, bf16[64,256,512]{2,1,0:T(8,128)(2,1)} %next_ref.19, ...), custom_call_target="tpu_custom_call" | custom-call | flops 1024 | bytes 1024 | tf_op jit(solution)/shard_map/blur_bands/pallas_call | solution.py:361
  5.8 3.0 %collective-permute-start = (bf16[16,32,512]{2,1,0:T(8,128)(2,1)}, bf16[16,32,512]{2,1,0:T(8,128)(2,1)S(1)}, u32[]{:S(2)}, u32[]{:S(2)}) collective-permute-start(bf16[16,32,512]{2,1,0:T(8,128)(2,1)} %blur_bands.10), channel_id=1, source_target_pairs={{0,2},{2,0},{4,6},{6,4},{8,10},{10,8},{12,14},{14,12},{16,18},{18,... | collective-permute-start | bytes 1572872 | tf_op jit(solution)/shard_map/ppermute | solution.py:472
  8.8 5.1 %blur_bands.11 = bf16[16,32,512]{2,1,0:T(8,128)(2,1)} custom-call(s32[1]{0:T(128)} %bitcast.index_ref, s32[1088]{0:T(1024)} %constant.26.clone.table_ref, s32[64]{0:T(128)} %group_ref.19, bf16[64,256,512]{2,1,0:T(8,128)(2,1)} %next_ref.19, bf16[64,256,512]{2,1,0:T(8,128)(2,1)} %next_ref.19, bf16[64,256,512]{2,1,0:T(8,128)(2,1)} %next_ref.19, ...), custom_call_target="tpu_custom_call" | custom-call | flops 1024 | bytes 1024 | tf_op jit(solution)/shard_map/blur_bands/pallas_call | solution.py:361
  14.0 1.6 multiply_convert_fusion
  15.6 5.3 %collective-permute-done.refs_1_ = bf16[16,32,512]{2,1,0:T(8,128)(2,1)S(1)} collective-permute-done((bf16[16,32,512]{2,1,0:T(8,128)(2,1)}, bf16[16,32,512]{2,1,0:T(8,128)(2,1)S(1)}, u32[]{:S(2)}, u32[]{:S(2)}) %collective-permute-start) | collective-permute-done | bytes 524320 | tf_op jit(solution)/shard_map/ppermute | solution.py:472
  20.9 1.7 collective-permute-start.1
  23.6 7.7 %blur_bands.12 = (bf16[16,64,512]{2,1,0:T(8,128)(2,1)S(1)}, bf16[16,64,512]{2,1,0:T(8,128)(2,1)S(1)}) custom-call(s32[1]{0:T(128)} %bitcast.index_ref, s32[1088]{0:T(1024)S(1)} %copy-done.5, s32[64]{0:T(128)S(1)} %copy-done.20, bf16[64,256,512]{2,1,0:T(8,128)(2,1)} %next_ref.19, bf16[64,256,512]{2,1,0:T(8,128)(2,1)} %next_ref.19, ...), custom_call_target="tpu_custom_call" | custom-call | flops 1024 | bytes 1024 | tf_op jit(solution)/shard_map/blur_bands/pallas_call | solution.py:361
  31.3 3.9 %collective-permute-done.1.refs_2_ = bf16[16,32,512]{2,1,0:T(8,128)(2,1)S(1)} collective-permute-done((bf16[16,32,512]{2,1,0:T(8,128)(2,1)S(1)}, bf16[16,32,512]{2,1,0:T(8,128)(2,1)S(1)}, u32[]{:S(2)}, u32[]{:S(2)}) %collective-permute-start.1) | collective-permute-done | bytes 524320 | tf_op jit(solution)/shard_map/ppermute | solution.py:472
  35.2 1.8 collective-permute-start.3
  37.3 1.7 collective-permute-start.5
  39.0 8.4 %blur_bands.13 = (bf16[16,64,512]{2,1,0:T(8,128)(2,1)}, bf16[16,64,512]{2,1,0:T(8,128)(2,1)S(1)}) custom-call(s32[1]{0:T(128)} %bitcast.index_ref, s32[1088]{0:T(1024)S(1)} %copy-done.5, s32[64]{0:T(128)S(1)} %copy-done.20, bf16[64,256,512]{2,1,0:T(8,128)(2,1)} %next_ref.19, bf16[64,256,512]{2,1,0:T(8,128)(2,1)} %next_ref.19, ...), custom_call_target="tpu_custom_call" | custom-call | flops 1024 | bytes 1024 | tf_op jit(solution)/shard_map/blur_bands/pallas_call | solution.py:361
  48.6 8.4 %blur_bands.14 = (bf16[16,64,512]{2,1,0:T(8,128)(2,1)}, bf16[16,64,512]{2,1,0:T(8,128)(2,1)S(1)}) custom-call(s32[1]{0:T(128)} %bitcast.index_ref, s32[1088]{0:T(1024)S(1)} %copy-done.5, s32[64]{0:T(128)S(1)} %copy-done.20, bf16[64,256,512]{2,1,0:T(8,128)(2,1)} %next_ref.19, bf16[64,256,512]{2,1,0:T(8,128)(2,1)} %next_ref.19, ...), custom_call_target="tpu_custom_call" | custom-call | flops 1024 | bytes 1024 | tf_op jit(solution)/shard_map/blur_bands/pallas_call | solution.py:361
  57.0 8.4 %blur_bands.15 = (bf16[16,64,512]{2,1,0:T(8,128)(2,1)}, bf16[16,64,512]{2,1,0:T(8,128)(2,1)S(1)}) custom-call(s32[1]{0:T(128)} %bitcast.index_ref, s32[1088]{0:T(1024)S(1)} %copy-done.5, s32[64]{0:T(128)S(1)} %copy-done.20, bf16[64,256,512]{2,1,0:T(8,128)(2,1)} %next_ref.19, bf16[64,256,512]{2,1,0:T(8,128)(2,1)} %next_ref.19, ...), custom_call_target="tpu_custom_call" | custom-call | flops 1024 | bytes 1024 | tf_op jit(solution)/shard_map/blur_bands/pallas_call | solution.py:361
  66.4 17.7 %collective-permute-done.6.refs_1_ = bf16[16,64,512]{2,1,0:T(8,128)(2,1)S(1)} collective-permute-done((bf16[16,64,512]{2,1,0:T(8,128)(2,1)}, bf16[16,64,512]{2,1,0:T(8,128)(2,1)S(1)}, u32[]{:S(2)}, u32[]{:S(2)}) %collective-permute-start.6) | collective-permute-done | bytes 1048608 | tf_op jit(solution)/shard_map/ppermute | solution.py:472
  84.1 1.0 copy-done.16
  85.1 1.7 collective-permute-start.7
  87.1 1.7 collective-permute-start.10
  89.1 5.9 %blur_bands.16.refs_0_ = bf16[16,64,512]{2,1,0:T(8,128)(2,1)S(1)} custom-call(s32[1]{0:T(128)} %bitcast.index_ref, s32[1088]{0:T(1024)S(1)} %copy-done.5, s32[64]{0:T(128)S(1)} %copy-done.20, bf16[64,256,512]{2,1,0:T(8,128)(2,1)} %next_ref.19, bf16[64,256,512]{2,1,0:T(8,128)(2,1)} %next_ref.19, bf16[64,256,512]{2,1,0:T(8,128)(2,1)} %next_ref.19, ...), custom_call_target="tpu_custom_call" | custom-call | flops 1024 | bytes 1024 | tf_op jit(solution)/shard_map/blur_bands/pallas_call | solution.py:361
  95.1 7.7 %blur_bands.17 = (bf16[16,64,512]{2,1,0:T(8,128)(2,1)S(1)}, bf16[16,64,512]{2,1,0:T(8,128)(2,1)S(1)}) custom-call(s32[1]{0:T(128)} %bitcast.index_ref, s32[1088]{0:T(1024)S(1)} %copy-done.5, s32[64]{0:T(128)S(1)} %copy-done.20, bf16[64,256,512]{2,1,0:T(8,128)(2,1)} %next_ref.19, bf16[64,256,512]{2,1,0:T(8,128)(2,1)} %next_ref.19, ...), custom_call_target="tpu_custom_call" | custom-call | flops 1024 | bytes 1024 | tf_op jit(solution)/shard_map/blur_bands/pallas_call | solution.py:361
  104.8 7.7 %blur_bands.18 = (bf16[16,64,512]{2,1,0:T(8,128)(2,1)S(1)}, bf16[16,64,512]{2,1,0:T(8,128)(2,1)S(1)}) custom-call(s32[1]{0:T(128)} %bitcast.index_ref, s32[1088]{0:T(1024)S(1)} %copy-done.5, s32[64]{0:T(128)S(1)} %copy-done.20, bf16[64,256,512]{2,1,0:T(8,128)(2,1)} %next_ref.19, bf16[64,256,512]{2,1,0:T(8,128)(2,1)} %next_ref.19, ...), custom_call_target="tpu_custom_call" | custom-call | flops 1024 | bytes 1024 | tf_op jit(solution)/shard_map/blur_bands/pallas_call | solution.py:361
  113.5 7.7 %blur_bands.19 = (bf16[16,64,512]{2,1,0:T(8,128)(2,1)S(1)}, bf16[16,64,512]{2,1,0:T(8,128)(2,1)S(1)}) custom-call(s32[1]{0:T(128)} %bitcast.index_ref, s32[1088]{0:T(1024)S(1)} %copy-done.5, s32[64]{0:T(128)S(1)} %copy-done.20, bf16[64,256,512]{2,1,0:T(8,128)(2,1)} %next_ref.19, bf16[64,256,512]{2,1,0:T(8,128)(2,1)} %next_ref.19, ...), custom_call_target="tpu_custom_call" | custom-call | flops 1024 | bytes 1024 | tf_op jit(solution)/shard_map/blur_bands/pallas_call | solution.py:361
  121.2 1.0 copy-done.23
  122.3 1.9 project_band.11.total_ref
  124.2 1.9 project_band.12.total_ref
  126.1 3.2 %project_band.13.total_ref = f32[128,128]{1,0:T(8,128)S(1)} custom-call(s32[1]{0:T(128)} %constant.10.clone.1.index_ref.table_ref, s32[1]{0:T(128)} %constant.10.clone.1.index_ref.table_ref, f32[128,128]{1,0:T(8,128)S(1)} %project_band.12.total_ref, bf16[16,64,512]{2,1,0:T(8,128)(2,1)S(1)} %copy-done.13, bf16[16,64,512]{2,1,0:T(8,128)(2,1)S(1)} %copy-done.17, ...), custom_call_target="tpu_custom_call" | custom-call | flops 1024 | bytes 1024 | tf_op jit(solution)/shard_map/project_band/pallas_call | solution.py:408
  129.3 3.6 %collective-permute-done.9.refs_1_ = bf16[16,64,512]{2,1,0:T(8,128)(2,1)} collective-permute-done((bf16[16,64,512]{2,1,0:T(8,128)(2,1)}, bf16[16,64,512]{2,1,0:T(8,128)(2,1)}, u32[]{:S(2)}, u32[]{:S(2)}) %collective-permute-start.9) | collective-permute-done | bytes 1048608 | tf_op jit(solution)/shard_map/ppermute | solution.py:472
  132.9 1.6 collective-permute-start.11
  134.9 1.5 collective-permute-start.13
  137.0 2.8 %project_band.14.total_ref = f32[128,128]{1,0:T(8,128)S(1)} custom-call(s32[1]{0:T(128)} %constant.10.clone.1.index_ref.table_ref, s32[1]{0:T(128)} %constant.10.clone.1.index_ref.table_ref, f32[128,128]{1,0:T(8,128)S(1)} %project_band.13.total_ref, bf16[16,64,512]{2,1,0:T(8,128)(2,1)S(1)} %copy-done.7, bf16[16,64,512]{2,1,0:T(8,128)(2,1)} %collective-permute-done.9.refs_1_, ...), custom_call_target="tpu_custom_call" | custom-call | flops 1024 | bytes 1024 | tf_op jit(solution)/shard_map/project_band/pallas_call | solution.py:408
  139.8 3.2 %project_band.15.total_ref = f32[128,128]{1,0:T(8,128)S(1)} custom-call(s32[1]{0:T(128)} %constant.10.clone.1.index_ref.table_ref, s32[1]{0:T(128)} %constant.10.clone.1.index_ref.table_ref, f32[128,128]{1,0:T(8,128)S(1)} %project_band.14.total_ref, bf16[16,64,512]{2,1,0:T(8,128)(2,1)S(1)} %get-tuple-element.97.refs_0_, ...), custom_call_target="tpu_custom_call" | custom-call | flops 1024 | bytes 1024 | tf_op jit(solution)/shard_map/project_band/pallas_call | solution.py:408
  143.1 18.0 %collective-permute-done.13.refs_1_ = bf16[16,64,512]{2,1,0:T(8,128)(2,1)S(1)} collective-permute-done((bf16[16,64,512]{2,1,0:T(8,128)(2,1)S(1)}, bf16[16,64,512]{2,1,0:T(8,128)(2,1)S(1)}, u32[]{:S(2)}, u32[]{:S(2)}) %collective-permute-start.13) | collective-permute-done | bytes 1048608 | tf_op jit(solution)/shard_map/ppermute | solution.py:472
  161.0 17.9 %collective-permute-done.14.refs_1_ = bf16[16,64,512]{2,1,0:T(8,128)(2,1)S(1)} collective-permute-done((bf16[16,64,512]{2,1,0:T(8,128)(2,1)S(1)}, bf16[16,64,512]{2,1,0:T(8,128)(2,1)S(1)}, u32[]{:S(2)}, u32[]{:S(2)}) %collective-permute-start.14) | collective-permute-done | bytes 1048608 | tf_op jit(solution)/shard_map/ppermute | solution.py:472
  179.0 1.6 collective-permute-start.15
  181.5 1.4 collective-permute-start.17
  182.9 1.2 project_band.16.total_ref
  184.1 1.2 project_band.17.total_ref
  185.3 14.6 %collective-permute-done.15.refs_1_ = bf16[4096,128]{1,0:T(8,128)(2,1)S(1)} collective-permute-done((bf16[4096,128]{1,0:T(8,128)(2,1)S(1)}, bf16[4096,128]{1,0:T(8,128)(2,1)S(1)}, u32[]{:S(2)}, u32[]{:S(2)}) %collective-permute-start.15) | collective-permute-done | bytes 1048608 | tf_op jit(solution)/shard_map/ppermute | solution.py:472
  200.4 1.1 collective-permute-done.16.refs_1_
  203.1 1.6 collective-permute-start.19
  205.0 2.6 %collective-permute-done.19.side_ref = f32[128,128]{1,0:T(8,128)S(1)} collective-permute-done((f32[128,128]{1,0:T(8,128)S(1)}, f32[128,128]{1,0:T(8,128)S(1)}, u32[]{:S(2)}, u32[]{:S(2)}) %collective-permute-start.19) | collective-permute-done | bytes 65568 | tf_op jit(solution)/shard_map/ppermute | solution.py:542
  207.6 1.1 collective-permute-done.20.both_ref
  209.4 1.9 merge.1
  212.2 1.6 collective-permute-start.22
  213.7 1.1 collective-permute-start.23
  216.3 2.5 collective-permute-done.23
  219.6 2.5 %collective-permute-start.24 = (f32[72,128]{1,0:T(8,128)S(1)}, f32[72,128]{1,0:T(8,128)S(1)}, u32[]{:S(2)}, u32[]{:S(2)}) collective-permute-start(f32[72,128]{1,0:T(8,128)S(1)} %add_add_fusion.summed_ref), channel_id=1, source_target_pairs={{0,16},{2,18},{4,20},{6,22},{8,24},{10,26},{12,28},{14,30},{16,0},... | collective-permute-start | bytes 110600 | tf_op jit(solution)/shard_map/ppermute | solution.py:472
  222.1 2.7 %collective-permute-done.24.more_ref = f32[72,128]{1,0:T(8,128)S(1)} collective-permute-done((f32[72,128]{1,0:T(8,128)S(1)}, f32[72,128]{1,0:T(8,128)S(1)}, u32[]{:S(2)}, u32[]{:S(2)}) %collective-permute-start.24) | collective-permute-done | bytes 36896 | tf_op jit(solution)/shard_map/ppermute | solution.py:472
  225.6 22.9 %orthogonal_iteration.1 = (bf16[8192,128]{1,0:T(8,128)(2,1)}, f32[64,128]{1,0:T(8,128)}, f32[1,128]{1,0:T(1,128)}) custom-call(f32[72,128]{1,0:T(8,128)S(1)} %add_add_fusion.summed_ref, f32[72,128]{1,0:T(8,128)S(1)} %collective-permute-done.24.more_ref, f32[1,128]{1,0:T(1,128)S(1)} %bitcast.3, f32[128,128]{1,0:T(8,128)S(1)} %copy-done.19, ...), custom_call_target="tpu_custom_call" | custom-call | tf_op jit(solution)/shard_map/orthogonal_iteration/pallas_call | solution.py:187
  (98 shorter events, 15.8 us)
Async XLA Ops:
  5.7 8.2 %copy-start = (f32[256,512]{1,0:T(8,128)S(1)}, f32[256,512]{1,0:T(8,128)}, u32[]{:S(2)}) copy-start(f32[256,512]{1,0:T(8,128)} %refs_3_.21) | copy-start | bytes 1572868
  5.8 8.2 %copy-start.1 = (s32[256,512]{1,0:T(8,128)S(1)}, s32[256,512]{1,0:T(8,128)}, u32[]{:S(2)}) copy-start(s32[256,512]{1,0:T(8,128)} %refs_6_.16) | copy-start | bytes 1572868
  5.8 15.1 %collective-permute-start = (bf16[16,32,512]{2,1,0:T(8,128)(2,1)}, bf16[16,32,512]{2,1,0:T(8,128)(2,1)S(1)}, u32[]{:S(2)}, u32[]{:S(2)}) collective-permute-start(bf16[16,32,512]{2,1,0:T(8,128)(2,1)} %blur_bands.10), channel_id=1, source_target_pairs={{0,2},{2,0},{4,6},{6,4},{8,10},{10,8},{12,14},{14,12},{16,18},{18,... | collective-permute-start | bytes 1572872 | tf_op jit(solution)/shard_map/ppermute | solution.py:472
  13.9 7.0 %copy-start.29 = (bf16[16,32,512]{2,1,0:T(8,128)(2,1)S(1)}, bf16[16,32,512]{2,1,0:T(8,128)(2,1)}, u32[]{:S(2)}) copy-start(bf16[16,32,512]{2,1,0:T(8,128)(2,1)} %blur_bands.11) | copy-start | bytes 1572868
  13.9 9.7 %copy-start.2 = (bf16[512,512]{1,0:T(8,128)(2,1)S(1)}, bf16[512,512]{1,0:T(8,128)(2,1)}, u32[]{:S(2)}) copy-start(bf16[512,512]{1,0:T(8,128)(2,1)} %constant.27.clone.refs_6_.refs_7_) | copy-start | bytes 1572868
  13.9 9.7 %copy-start.5 = (s32[1088]{0:T(1024)S(1)}, s32[1088]{0:T(1024)}, u32[]{:S(2)}) copy-start(s32[1088]{0:T(1024)} %constant.26.clone.table_ref) | copy-start | bytes 13060
  13.9 9.6 %copy-start.20 = (s32[64]{0:T(128)S(1)}, s32[64]{0:T(128)}, u32[]{:S(2)}) copy-start(s32[64]{0:T(128)} %group_ref.19) | copy-start | bytes 772
  15.6 19.6 %copy-start.3 = (bf16[8192,128]{1,0:T(8,128)(2,1)S(1)}, bf16[8192,128]{1,0:T(8,128)(2,1)}, u32[]{:S(2)}) copy-start(bf16[8192,128]{1,0:T(8,128)(2,1)} %basis_ref.1) | copy-start | bytes 6291460
  20.9 2.7 %collective-permute-start.2 = (bf16[64,16,512]{2,1,0:T(8,128)(2,1)S(1)}, bf16[64,16,512]{2,1,0:T(8,128)(2,1)S(1)}, u32[]{:S(2)}, u32[]{:S(2)}) collective-permute-start(bf16[64,16,512]{2,1,0:T(8,128)(2,1)S(1)} %multiply_convert_fusion), channel_id=1, source_target_pairs={{0,1},{1,0},{2,3},{3,2},{4,5},{5,4},{6,7},{7,6},{8,9},{9,8},{10,11... | collective-permute-start | bytes 3145736 | tf_op jit(solution)/shard_map/ppermute | solution.py:495
  20.9 14.3 %collective-permute-start.1 = (bf16[16,32,512]{2,1,0:T(8,128)(2,1)S(1)}, bf16[16,32,512]{2,1,0:T(8,128)(2,1)S(1)}, u32[]{:S(2)}, u32[]{:S(2)}) collective-permute-start(bf16[16,32,512]{2,1,0:T(8,128)(2,1)S(1)} %copy-done.29), channel_id=1, source_target_pairs={{0,2},{2,0},{4,6},{6,4},{8,10},{10,8},{12,14},{14,12},{16,18},{18,... | collective-permute-start | bytes 1572872 | tf_op jit(solution)/shard_map/ppermute | solution.py:472
  31.3 16.1 %copy-start.10 = (bf16[16,64,512]{2,1,0:T(8,128)(2,1)}, bf16[16,64,512]{2,1,0:T(8,128)(2,1)S(1)}, u32[]{:S(2)}) copy-start(bf16[16,64,512]{2,1,0:T(8,128)(2,1)S(1)} %get-tuple-element.80.refs_0_) | copy-start | bytes 3145732
  35.2 49.8 %collective-permute-start.3 = (bf16[8192,128]{1,0:T(8,128)(2,1)S(1)}, bf16[8192,128]{1,0:T(8,128)(2,1)S(1)}, u32[]{:S(2)}, u32[]{:S(2)}) collective-permute-start(bf16[8192,128]{1,0:T(8,128)(2,1)S(1)} %copy-done.3), channel_id=1, source_target_pairs={{0,8},{2,10},{8,16},{10,18},{16,24},{18,26},{24,28},{26,30},{28,20... | collective-permute-start | bytes 6291464 | tf_op jit(solution)/shard_map/ppermute | solution.py:472
  37.1 48.0 %collective-permute-start.4 = (bf16[8192,128]{1,0:T(8,128)(2,1)S(1)}, bf16[8192,128]{1,0:T(8,128)(2,1)}, u32[]{:S(2)}, u32[]{:S(2)}) collective-permute-start(bf16[8192,128]{1,0:T(8,128)(2,1)S(1)} %copy-done.3), channel_id=1, source_target_pairs={{0,4},{2,6},{8,0},{10,2},{16,8},{18,10},{24,16},{26,18},{28,24},{3... | collective-permute-start | bytes 6291464 | tf_op jit(solution)/shard_map/ppermute | solution.py:472
  37.3 28.1 %collective-permute-start.5 = (bf16[16,64,512]{2,1,0:T(8,128)(2,1)S(1)}, bf16[16,64,512]{2,1,0:T(8,128)(2,1)S(1)}, u32[]{:S(2)}, u32[]{:S(2)}) collective-permute-start(bf16[16,64,512]{2,1,0:T(8,128)(2,1)S(1)} %get-tuple-element.69), channel_id=1, source_target_pairs={{0,2},{2,0},{4,6},{6,4},{8,10},{10,8},{12,14},{14,12},{16,18},{18,... | collective-permute-start | bytes 3145736 | tf_op jit(solution)/shard_map/ppermute | solution.py:472
  48.4 35.7 %collective-permute-start.6 = (bf16[16,64,512]{2,1,0:T(8,128)(2,1)}, bf16[16,64,512]{2,1,0:T(8,128)(2,1)S(1)}, u32[]{:S(2)}, u32[]{:S(2)}) collective-permute-start(bf16[16,64,512]{2,1,0:T(8,128)(2,1)} %get-tuple-element.70), channel_id=1, source_target_pairs={{0,2},{2,0},{4,6},{6,4},{8,10},{10,8},{12,14},{14,12},{16,18},{18,... | collective-permute-start | bytes 3145736 | tf_op jit(solution)/shard_map/ppermute | solution.py:472
  57.0 8.4 %copy-start.6 = (bf16[16,64,512]{2,1,0:T(8,128)(2,1)}, bf16[16,64,512]{2,1,0:T(8,128)(2,1)S(1)}, u32[]{:S(2)}) copy-start(bf16[16,64,512]{2,1,0:T(8,128)(2,1)S(1)} %get-tuple-element.95.refs_0_) | copy-start | bytes 3145732
  85.1 47.9 %collective-permute-start.7 = (bf16[8192,128]{1,0:T(8,128)(2,1)S(1)}, bf16[8192,128]{1,0:T(8,128)(2,1)S(1)}, u32[]{:S(2)}, u32[]{:S(2)}) collective-permute-start(bf16[8192,128]{1,0:T(8,128)(2,1)S(1)} %collective-permute-done.3.refs_4_.refs_3_), channel_id=1, source_target_pairs={{0,8},{2,10},{8,16},{10,18},{16,24},{18,26},{24,28},{26,30},{28,20... | collective-permute-start | bytes 6291464 | tf_op jit(solution)/shard_map/ppermute | solution.py:472
  86.8 46.1 %collective-permute-start.8 = (bf16[8192,128]{1,0:T(8,128)(2,1)}, bf16[8192,128]{1,0:T(8,128)(2,1)}, u32[]{:S(2)}, u32[]{:S(2)}) collective-permute-start(bf16[8192,128]{1,0:T(8,128)(2,1)} %collective-permute-done.4.refs_2_), channel_id=1, source_target_pairs={{0,4},{2,6},{8,0},{10,2},{16,8},{18,10},{24,16},{26,18},{28,24},{3... | collective-permute-start | bytes 6291464 | tf_op jit(solution)/shard_map/ppermute | solution.py:472
  87.1 42.3 %collective-permute-start.10 = (bf16[16,64,512]{2,1,0:T(8,128)(2,1)}, bf16[16,64,512]{2,1,0:T(8,128)(2,1)}, u32[]{:S(2)}, u32[]{:S(2)}) collective-permute-start(bf16[16,64,512]{2,1,0:T(8,128)(2,1)} %get-tuple-element.85), channel_id=1, source_target_pairs={{0,2},{2,0},{4,6},{6,4},{8,10},{10,8},{12,14},{14,12},{16,18},{18,... | collective-permute-start | bytes 3145736 | tf_op jit(solution)/shard_map/ppermute | solution.py:472
  88.7 44.2 %collective-permute-start.9 = (bf16[16,64,512]{2,1,0:T(8,128)(2,1)}, bf16[16,64,512]{2,1,0:T(8,128)(2,1)}, u32[]{:S(2)}, u32[]{:S(2)}) collective-permute-start(bf16[16,64,512]{2,1,0:T(8,128)(2,1)} %get-tuple-element.84), channel_id=1, source_target_pairs={{0,2},{2,0},{4,6},{6,4},{8,10},{10,8},{12,14},{14,12},{16,18},{18,... | collective-permute-start | bytes 3145736 | tf_op jit(solution)/shard_map/ppermute | solution.py:472
  122.3 1.9 copy-start.11
  122.3 1.9 copy-start.15
  124.2 1.9 copy-start.13
  124.2 1.9 copy-start.17
  126.1 8.8 %copy-start.28 = (bf16[16,64,512]{2,1,0:T(8,128)(2,1)S(1)}, bf16[16,64,512]{2,1,0:T(8,128)(2,1)}, u32[]{:S(2)}) copy-start(bf16[16,64,512]{2,1,0:T(8,128)(2,1)} %copy-done.27) | copy-start | bytes 3145732
  126.1 10.3 %copy-start.26 = (bf16[16,64,512]{2,1,0:T(8,128)(2,1)S(1)}, bf16[16,64,512]{2,1,0:T(8,128)(2,1)}, u32[]{:S(2)}) copy-start(bf16[16,64,512]{2,1,0:T(8,128)(2,1)} %copy-done.25) | copy-start | bytes 3145732
  126.1 10.8 %copy-start.7 = (bf16[16,64,512]{2,1,0:T(8,128)(2,1)S(1)}, bf16[16,64,512]{2,1,0:T(8,128)(2,1)}, u32[]{:S(2)}) copy-start(bf16[16,64,512]{2,1,0:T(8,128)(2,1)} %copy-done.6) | copy-start | bytes 3145732
  132.9 46.1 %collective-permute-start.11 = (bf16[8192,128]{1,0:T(8,128)(2,1)S(1)}, bf16[8192,128]{1,0:T(8,128)(2,1)S(1)}, u32[]{:S(2)}, u32[]{:S(2)}) collective-permute-start(bf16[8192,128]{1,0:T(8,128)(2,1)S(1)} %collective-permute-done.7.refs_2_), channel_id=1, source_target_pairs={{0,8},{2,10},{8,16},{10,18},{16,24},{18,26},{24,28},{26,30},{28,20... | collective-permute-start | bytes 6291464 | tf_op jit(solution)/shard_map/ppermute | solution.py:472
  134.5 44.5 %collective-permute-start.12 = (bf16[8192,128]{1,0:T(8,128)(2,1)}, bf16[8192,128]{1,0:T(8,128)(2,1)S(1)}, u32[]{:S(2)}, u32[]{:S(2)}) collective-permute-start(bf16[8192,128]{1,0:T(8,128)(2,1)} %collective-permute-done.8.refs_2_), channel_id=1, source_target_pairs={{0,4},{2,6},{8,0},{10,2},{16,8},{18,10},{24,16},{26,18},{28,24},{3... | collective-permute-start | bytes 6291464 | tf_op jit(solution)/shard_map/ppermute | solution.py:472
  134.9 26.1 %collective-permute-start.13 = (bf16[16,64,512]{2,1,0:T(8,128)(2,1)S(1)}, bf16[16,64,512]{2,1,0:T(8,128)(2,1)S(1)}, u32[]{:S(2)}, u32[]{:S(2)}) collective-permute-start(bf16[16,64,512]{2,1,0:T(8,128)(2,1)S(1)} %copy-done.28), channel_id=1, source_target_pairs={{0,2},{2,0},{4,6},{6,4},{8,10},{10,8},{12,14},{14,12},{16,18},{18,... | collective-permute-start | bytes 3145736 | tf_op jit(solution)/shard_map/ppermute | solution.py:472
  136.4 42.5 %collective-permute-start.14 = (bf16[16,64,512]{2,1,0:T(8,128)(2,1)S(1)}, bf16[16,64,512]{2,1,0:T(8,128)(2,1)S(1)}, u32[]{:S(2)}, u32[]{:S(2)}) collective-permute-start(bf16[16,64,512]{2,1,0:T(8,128)(2,1)S(1)} %copy-done.26), channel_id=1, source_target_pairs={{0,2},{2,0},{4,6},{6,4},{8,10},{10,8},{12,14},{14,12},{16,18},{18,... | collective-permute-start | bytes 3145736 | tf_op jit(solution)/shard_map/ppermute | solution.py:472
  143.0 38.4 %copy-start.24 = (bf16[16,64,512]{2,1,0:T(8,128)(2,1)S(1)}, bf16[16,64,512]{2,1,0:T(8,128)(2,1)}, u32[]{:S(2)}) copy-start(bf16[16,64,512]{2,1,0:T(8,128)(2,1)} %copy-done.23) | copy-start | bytes 3145732
  143.1 39.8 %copy-start.9 = (bf16[16,64,512]{2,1,0:T(8,128)(2,1)S(1)}, bf16[16,64,512]{2,1,0:T(8,128)(2,1)}, u32[]{:S(2)}) copy-start(bf16[16,64,512]{2,1,0:T(8,128)(2,1)} %copy-done.8) | copy-start | bytes 3145732
  179.0 20.9 %collective-permute-start.15 = (bf16[4096,128]{1,0:T(8,128)(2,1)S(1)}, bf16[4096,128]{1,0:T(8,128)(2,1)S(1)}, u32[]{:S(2)}, u32[]{:S(2)}) collective-permute-start(bf16[4096,128]{1,0:T(8,128)(2,1)S(1)} %slice.6), channel_id=1, source_target_pairs={{0,8},{2,10},{8,16},{10,18},{16,24},{18,26},{24,28},{26,30},{28,20... | collective-permute-start | bytes 3145736 | tf_op jit(solution)/shard_map/ppermute | solution.py:472
  180.7 20.8 %collective-permute-start.16 = (bf16[4096,128]{1,0:T(8,128)(2,1)S(1)}, bf16[4096,128]{1,0:T(8,128)(2,1)S(1)}, u32[]{:S(2)}, u32[]{:S(2)}) collective-permute-start(bf16[4096,128]{1,0:T(8,128)(2,1)S(1)} %slice.7), channel_id=1, source_target_pairs={{0,4},{2,6},{8,0},{10,2},{16,8},{18,10},{24,16},{26,18},{28,24},{3... | collective-permute-start | bytes 3145736 | tf_op jit(solution)/shard_map/ppermute | solution.py:472
  181.5 20.5 %collective-permute-start.17 = (bf16[16,64,512]{2,1,0:T(8,128)(2,1)S(1)}, bf16[16,64,512]{2,1,0:T(8,128)(2,1)S(1)}, u32[]{:S(2)}, u32[]{:S(2)}) collective-permute-start(bf16[16,64,512]{2,1,0:T(8,128)(2,1)S(1)} %copy-done.24), channel_id=1, source_target_pairs={{0,2},{2,0},{4,6},{6,4},{8,10},{10,8},{12,14},{14,12},{16,18},{18,... | collective-permute-start | bytes 3145736 | tf_op jit(solution)/shard_map/ppermute | solution.py:472
  202.0 22.8 %copy-start.4 = (bf16[8192,128]{1,0:T(8,128)(2,1)S(1)}, bf16[8192,128]{1,0:T(8,128)(2,1)}, u32[]{:S(2)}) copy-start(bf16[8192,128]{1,0:T(8,128)(2,1)} %basis_ref.1) | copy-start | bytes 6291460
  202.0 22.8 %copy-start.19 = (f32[128,128]{1,0:T(8,128)S(1)}, f32[128,128]{1,0:T(8,128)}, u32[]{:S(2)}) copy-start(f32[128,128]{1,0:T(8,128)} %start_ref.1) | copy-start | bytes 196612
  202.0 22.8 %copy-start.22 = (f32[128]{0:T(128)S(1)}, f32[128]{0:T(128)}, u32[]{:S(2)}) copy-start(f32[128]{0:T(128)} %param.13) | copy-start | bytes 1540
  203.0 5.7 %copy-start.18 = (f32[128,128]{1,0:T(8,128)}, f32[128,128]{1,0:T(8,128)S(1)}, u32[]{:S(2)}) copy-start(f32[128,128]{1,0:T(8,128)S(1)} %project_band.21.total_ref) | copy-start | bytes 196612
  203.0 1.9 collective-permute-start.18
  203.1 4.5 %collective-permute-start.19 = (f32[128,128]{1,0:T(8,128)S(1)}, f32[128,128]{1,0:T(8,128)S(1)}, u32[]{:S(2)}, u32[]{:S(2)}) collective-permute-start(f32[128,128]{1,0:T(8,128)S(1)} %project_band.21.total_ref), channel_id=1, source_target_pairs={{0,2},{1,3},{2,0},{3,1},{4,6},{5,7},{6,4},{7,5},{8,10},{9,11},{10,... | collective-permute-start | bytes 196616 | tf_op jit(solution)/shard_map/ppermute | solution.py:542
  204.7 4.0 %collective-permute-start.20 = (f32[128,128]{1,0:T(8,128)S(1)}, f32[128,128]{1,0:T(8,128)S(1)}, u32[]{:S(2)}, u32[]{:S(2)}) collective-permute-start(f32[128,128]{1,0:T(8,128)S(1)} %project_band.21.total_ref), channel_id=1, source_target_pairs={{0,3},{1,2},{2,1},{3,0},{4,7},{5,6},{6,5},{7,4},{8,11},{9,10},{10,... | collective-permute-start | bytes 196616 | tf_op jit(solution)/shard_map/ppermute | solution.py:542
  205.0 3.8 %copy-start.30 = (f32[128,128]{1,0:T(8,128)}, f32[128,128]{1,0:T(8,128)S(1)}, u32[]{:S(2)}) copy-start(f32[128,128]{1,0:T(8,128)S(1)} %collective-permute-done.18.strip_ref) | copy-start | bytes 196612
  211.3 4.2 %collective-permute-start.21 = (f32[72,128]{1,0:T(8,128)}, f32[72,128]{1,0:T(8,128)S(1)}, u32[]{:S(2)}, u32[]{:S(2)}) collective-permute-start(f32[72,128]{1,0:T(8,128)} %get-tuple-element.112), channel_id=1, source_target_pairs={{0,4},{2,6},{4,0},{6,2},{8,12},{10,14},{12,8},{14,10},{16,20},{18,... | collective-permute-start | bytes 110600 | tf_op jit(solution)/shard_map/ppermute | solution.py:472
  212.2 4.2 %collective-permute-start.22 = (f32[72,128]{1,0:T(8,128)}, f32[72,128]{1,0:T(8,128)S(1)}, u32[]{:S(2)}, u32[]{:S(2)}) collective-permute-start(f32[72,128]{1,0:T(8,128)} %get-tuple-element.112), channel_id=1, source_target_pairs={{0,8},{2,10},{4,12},{6,14},{8,0},{10,2},{12,4},{14,6},{16,24},{18,... | collective-permute-start | bytes 110600 | tf_op jit(solution)/shard_map/ppermute | solution.py:472
  213.7 5.1 %collective-permute-start.23 = (f32[72,128]{1,0:T(8,128)}, f32[72,128]{1,0:T(8,128)S(1)}, u32[]{:S(2)}, u32[]{:S(2)}) collective-permute-start(f32[72,128]{1,0:T(8,128)} %get-tuple-element.112), channel_id=1, source_target_pairs={{0,12},{2,14},{4,8},{6,10},{8,4},{10,6},{12,0},{14,2},{16,28},{18,... | collective-permute-start | bytes 110600 | tf_op jit(solution)/shard_map/ppermute | solution.py:472
  219.6 5.2 %collective-permute-start.24 = (f32[72,128]{1,0:T(8,128)S(1)}, f32[72,128]{1,0:T(8,128)S(1)}, u32[]{:S(2)}, u32[]{:S(2)}) collective-permute-start(f32[72,128]{1,0:T(8,128)S(1)} %add_add_fusion.summed_ref), channel_id=1, source_target_pairs={{0,16},{2,18},{4,20},{6,22},{8,24},{10,26},{12,28},{14,30},{16,0},... | collective-permute-start | bytes 110600 | tf_op jit(solution)/shard_map/ppermute | solution.py:472
  (10 other events, 9.4 us)

commit v5 on v4

--- a/solution.py
+++ b/solution.py
@@ -490,11 +490,11 @@
     near = jnp.where(strip == 0, strip_rows - BAND, 0)
     rows = [lax.dynamic_slice_in_dim(values, near, BAND, axis=-2) for values in (near_raw, near_dark, near_mask)]
     border = ((rows[0].astype(jnp.float32) - rows[1]) * (1 - rows[2]).astype(jnp.float32)).astype(jnp.bfloat16)
-    came_first, sent_rest, border = lax.optimization_barrier((came_first, sent_rest, border))
+    came_first, sent_rest, border, passing = lax.optimization_barrier((came_first, sent_rest, border, basis))
     came_rest = move(sent_rest, swap)
     edge = lax.ppermute(border, "strips", [(0, 1), (1, 0)])
     sent_next, own_next = bands(1, ("sent", "own"), edge)
-    came_rest, sent_next, own_next, passing = lax.optimization_barrier((came_rest, sent_next, own_next, basis))
+    came_rest, sent_next, own_next = lax.optimization_barrier((came_rest, sent_next, own_next))
     half = basis.shape[0] // 2
     blocks = {0: basis}
     send, own, came = ([None, sent_next], [None, own_next], [came_rest])

time: 250 us -> 248 us (level)
  transfers between devices with their start and end apart: 25 -> 25, of which waited for: 15 -> 14; matrix products, arithmetic and copies ran while one was open for 1% -> 1% of each run, Pallas kernels for 34% -> 33%
where the time goes in v5:
time: 248 us; the launch traced here: 247 us
  Pallas kernels  112 us (45%)
  waiting for transfers between devices  94.4 us (38%)
  starting transfers between devices  28.8 us (12%)
  local copies, waits for them, and re-layouts  7.62 us (3%)
    ppermute x21, waiting for transfers between devices, paired_body(): move = lambda values, pairs: lax.ppermute(values, 'frames', pairs)  90.7 us
    pallas_call x10, Pallas kernels, blurred_bands(): pl.pallas_call(functools.partial(blur_kernel, slot, outputs, begin), grid...  71.6 us
    ppermute x21, starting transfers between devices, paired_body(): move = lambda values, pairs: lax.ppermute(values, 'frames', pairs)  26.9 us
    pallas_call x1, Pallas kernels, rotated(): pl.pallas_call(functools.partial(rotate_kernel, total_frames, chunk), in_...  22.9 us
    pallas_call x11, Pallas kernels, projected(): pl.pallas_call(functools.partial(project_kernel, slot, at, len(lines)), g...  15.7 us
    unnamed x66, local copies, waits for them, and re-layouts  7.47 us
  transfers between devices with their start and end apart: 25, of which 14 were waited for; matrix products, arithmetic and copies ran while one was open for 1% of the time, Pallas kernels for 33%

profile of v5, /device:TPU:0, one launch (start us, length us, event | category | flops | bytes accessed | tf_op | source)
XLA Modules:
  0.0 246.7 jit_solution(9342755545000686429)
XLA Ops:
  0.6 5.1 %blur_bands.10 = bf16[16,32,512]{2,1,0:T(8,128)(2,1)} custom-call(s32[1]{0:T(128)} %bitcast.index_ref, s32[1088]{0:T(1024)} %constant.26.clone.table_ref, s32[64]{0:T(128)} %group_ref.19, bf16[64,256,512]{2,1,0:T(8,128)(2,1)} %next_ref.19, bf16[64,256,512]{2,1,0:T(8,128)(2,1)} %next_ref.19, bf16[64,256,512]{2,1,0:T(8,128)(2,1)} %next_ref.19, ...), custom_call_target="tpu_custom_call" | custom-call | flops 1024 | bytes 1024 | tf_op jit(solution)/shard_map/blur_bands/pallas_call | solution.py:361
  5.8 3.0 %collective-permute-start = (bf16[16,32,512]{2,1,0:T(8,128)(2,1)}, bf16[16,32,512]{2,1,0:T(8,128)(2,1)S(1)}, u32[]{:S(2)}, u32[]{:S(2)}) collective-permute-start(bf16[16,32,512]{2,1,0:T(8,128)(2,1)} %blur_bands.10), channel_id=1, source_target_pairs={{0,2},{2,0},{4,6},{6,4},{8,10},{10,8},{12,14},{14,12},{16,18},{18,... | collective-permute-start | bytes 1572872 | tf_op jit(solution)/shard_map/ppermute | solution.py:472
  8.8 5.1 %blur_bands.11 = bf16[16,32,512]{2,1,0:T(8,128)(2,1)} custom-call(s32[1]{0:T(128)} %bitcast.index_ref, s32[1088]{0:T(1024)} %constant.26.clone.table_ref, s32[64]{0:T(128)} %group_ref.19, bf16[64,256,512]{2,1,0:T(8,128)(2,1)} %next_ref.19, bf16[64,256,512]{2,1,0:T(8,128)(2,1)} %next_ref.19, bf16[64,256,512]{2,1,0:T(8,128)(2,1)} %next_ref.19, ...), custom_call_target="tpu_custom_call" | custom-call | flops 1024 | bytes 1024 | tf_op jit(solution)/shard_map/blur_bands/pallas_call | solution.py:361
  14.0 1.6 multiply_convert_fusion
  15.6 5.3 %collective-permute-done.refs_1_ = bf16[16,32,512]{2,1,0:T(8,128)(2,1)S(1)} collective-permute-done((bf16[16,32,512]{2,1,0:T(8,128)(2,1)}, bf16[16,32,512]{2,1,0:T(8,128)(2,1)S(1)}, u32[]{:S(2)}, u32[]{:S(2)}) %collective-permute-start) | collective-permute-done | bytes 524320 | tf_op jit(solution)/shard_map/ppermute | solution.py:472
  20.9 1.8 collective-permute-start.1
  22.9 1.7 collective-permute-start.3
  24.7 7.7 %blur_bands.12 = (bf16[16,64,512]{2,1,0:T(8,128)(2,1)S(1)}, bf16[16,64,512]{2,1,0:T(8,128)(2,1)S(1)}) custom-call(s32[1]{0:T(128)} %bitcast.index_ref, s32[1088]{0:T(1024)S(1)} %copy-done.5, s32[64]{0:T(128)S(1)} %copy-done.20, bf16[64,256,512]{2,1,0:T(8,128)(2,1)} %next_ref.19, bf16[64,256,512]{2,1,0:T(8,128)(2,1)} %next_ref.19, ...), custom_call_target="tpu_custom_call" | custom-call | flops 1024 | bytes 1024 | tf_op jit(solution)/shard_map/blur_bands/pallas_call | solution.py:361
  32.5 4.3 %collective-permute-done.3.refs_2_ = bf16[16,32,512]{2,1,0:T(8,128)(2,1)S(1)} collective-permute-done((bf16[16,32,512]{2,1,0:T(8,128)(2,1)S(1)}, bf16[16,32,512]{2,1,0:T(8,128)(2,1)S(1)}, u32[]{:S(2)}, u32[]{:S(2)}) %collective-permute-start.3) | collective-permute-done | bytes 524320 | tf_op jit(solution)/shard_map/ppermute | solution.py:472
  36.8 1.7 collective-permute-start.5
  38.4 7.7 %blur_bands.13 = (bf16[16,64,512]{2,1,0:T(8,128)(2,1)S(1)}, bf16[16,64,512]{2,1,0:T(8,128)(2,1)S(1)}) custom-call(s32[1]{0:T(128)} %bitcast.index_ref, s32[1088]{0:T(1024)S(1)} %copy-done.5, s32[64]{0:T(128)S(1)} %copy-done.20, bf16[64,256,512]{2,1,0:T(8,128)(2,1)} %next_ref.19, bf16[64,256,512]{2,1,0:T(8,128)(2,1)} %next_ref.19, ...), custom_call_target="tpu_custom_call" | custom-call | flops 1024 | bytes 1024 | tf_op jit(solution)/shard_map/blur_bands/pallas_call | solution.py:361
  46.6 8.4 %blur_bands.14 = (bf16[16,64,512]{2,1,0:T(8,128)(2,1)}, bf16[16,64,512]{2,1,0:T(8,128)(2,1)S(1)}) custom-call(s32[1]{0:T(128)} %bitcast.index_ref, s32[1088]{0:T(1024)S(1)} %copy-done.5, s32[64]{0:T(128)S(1)} %copy-done.20, bf16[64,256,512]{2,1,0:T(8,128)(2,1)} %next_ref.19, bf16[64,256,512]{2,1,0:T(8,128)(2,1)} %next_ref.19, ...), custom_call_target="tpu_custom_call" | custom-call | flops 1024 | bytes 1024 | tf_op jit(solution)/shard_map/blur_bands/pallas_call | solution.py:361
  55.0 1.0 copy-done.6
  56.0 8.4 %blur_bands.15 = (bf16[16,64,512]{2,1,0:T(8,128)(2,1)}, bf16[16,64,512]{2,1,0:T(8,128)(2,1)S(1)}) custom-call(s32[1]{0:T(128)} %bitcast.index_ref, s32[1088]{0:T(1024)S(1)} %copy-done.5, s32[64]{0:T(128)S(1)} %copy-done.20, bf16[64,256,512]{2,1,0:T(8,128)(2,1)} %next_ref.19, bf16[64,256,512]{2,1,0:T(8,128)(2,1)} %next_ref.19, ...), custom_call_target="tpu_custom_call" | custom-call | flops 1024 | bytes 1024 | tf_op jit(solution)/shard_map/blur_bands/pallas_call | solution.py:361
  65.4 18.1 %collective-permute-done.6.refs_1_ = bf16[16,64,512]{2,1,0:T(8,128)(2,1)S(1)} collective-permute-done((bf16[16,64,512]{2,1,0:T(8,128)(2,1)S(1)}, bf16[16,64,512]{2,1,0:T(8,128)(2,1)S(1)}, u32[]{:S(2)}, u32[]{:S(2)}) %collective-permute-start.6) | collective-permute-done | bytes 1048608 | tf_op jit(solution)/shard_map/ppermute | solution.py:472
  83.5 1.7 collective-permute-start.7
  85.6 1.6 collective-permute-start.10
  87.6 5.9 %blur_bands.16.refs_0_ = bf16[16,64,512]{2,1,0:T(8,128)(2,1)S(1)} custom-call(s32[1]{0:T(128)} %bitcast.index_ref, s32[1088]{0:T(1024)S(1)} %copy-done.5, s32[64]{0:T(128)S(1)} %copy-done.20, bf16[64,256,512]{2,1,0:T(8,128)(2,1)} %next_ref.19, bf16[64,256,512]{2,1,0:T(8,128)(2,1)} %next_ref.19, bf16[64,256,512]{2,1,0:T(8,128)(2,1)} %next_ref.19, ...), custom_call_target="tpu_custom_call" | custom-call | flops 1024 | bytes 1024 | tf_op jit(solution)/shard_map/blur_bands/pallas_call | solution.py:361
  93.6 7.7 %blur_bands.17 = (bf16[16,64,512]{2,1,0:T(8,128)(2,1)S(1)}, bf16[16,64,512]{2,1,0:T(8,128)(2,1)S(1)}) custom-call(s32[1]{0:T(128)} %bitcast.index_ref, s32[1088]{0:T(1024)S(1)} %copy-done.5, s32[64]{0:T(128)S(1)} %copy-done.20, bf16[64,256,512]{2,1,0:T(8,128)(2,1)} %next_ref.19, bf16[64,256,512]{2,1,0:T(8,128)(2,1)} %next_ref.19, ...), custom_call_target="tpu_custom_call" | custom-call | flops 1024 | bytes 1024 | tf_op jit(solution)/shard_map/blur_bands/pallas_call | solution.py:361
  103.3 7.7 %blur_bands.18 = (bf16[16,64,512]{2,1,0:T(8,128)(2,1)S(1)}, bf16[16,64,512]{2,1,0:T(8,128)(2,1)S(1)}) custom-call(s32[1]{0:T(128)} %bitcast.index_ref, s32[1088]{0:T(1024)S(1)} %copy-done.5, s32[64]{0:T(128)S(1)} %copy-done.20, bf16[64,256,512]{2,1,0:T(8,128)(2,1)} %next_ref.19, bf16[64,256,512]{2,1,0:T(8,128)(2,1)} %next_ref.19, ...), custom_call_target="tpu_custom_call" | custom-call | flops 1024 | bytes 1024 | tf_op jit(solution)/shard_map/blur_bands/pallas_call | solution.py:361
  112.0 7.7 %blur_bands.19 = (bf16[16,64,512]{2,1,0:T(8,128)(2,1)S(1)}, bf16[16,64,512]{2,1,0:T(8,128)(2,1)S(1)}) custom-call(s32[1]{0:T(128)} %bitcast.index_ref, s32[1088]{0:T(1024)S(1)} %copy-done.5, s32[64]{0:T(128)S(1)} %copy-done.20, bf16[64,256,512]{2,1,0:T(8,128)(2,1)} %next_ref.19, bf16[64,256,512]{2,1,0:T(8,128)(2,1)} %next_ref.19, ...), custom_call_target="tpu_custom_call" | custom-call | flops 1024 | bytes 1024 | tf_op jit(solution)/shard_map/blur_bands/pallas_call | solution.py:361
  119.8 1.0 copy-done.23
  120.8 1.9 project_band.11.total_ref
  122.8 1.9 project_band.12.total_ref
  124.7 1.2 project_band.13.total_ref
  125.9 5.2 %collective-permute-done.9.refs_1_ = bf16[16,64,512]{2,1,0:T(8,128)(2,1)} collective-permute-done((bf16[16,64,512]{2,1,0:T(8,128)(2,1)}, bf16[16,64,512]{2,1,0:T(8,128)(2,1)}, u32[]{:S(2)}, u32[]{:S(2)}) %collective-permute-start.9) | collective-permute-done | bytes 1048608 | tf_op jit(solution)/shard_map/ppermute | solution.py:472
  131.2 1.6 collective-permute-start.11
  133.2 1.5 collective-permute-start.13
  135.2 3.2 %project_band.14.total_ref = f32[128,128]{1,0:T(8,128)S(1)} custom-call(s32[1]{0:T(128)} %constant.10.clone.1.index_ref.table_ref, s32[1]{0:T(128)} %constant.10.clone.1.index_ref.table_ref, f32[128,128]{1,0:T(8,128)S(1)} %project_band.13.total_ref, bf16[16,64,512]{2,1,0:T(8,128)(2,1)S(1)} %copy-done.7, bf16[16,64,512]{2,1,0:T(8,128)(2,1)} %collective-permute-done.9.refs_1_, ...), custom_call_target="tpu_custom_call" | custom-call | flops 1024 | bytes 1024 | tf_op jit(solution)/shard_map/project_band/pallas_call | solution.py:408
  138.4 3.2 %project_band.15.total_ref = f32[128,128]{1,0:T(8,128)S(1)} custom-call(s32[1]{0:T(128)} %constant.10.clone.1.index_ref.table_ref, s32[1]{0:T(128)} %constant.10.clone.1.index_ref.table_ref, f32[128,128]{1,0:T(8,128)S(1)} %project_band.14.total_ref, bf16[16,64,512]{2,1,0:T(8,128)(2,1)S(1)} %get-tuple-element.97.refs_0_, ...), custom_call_target="tpu_custom_call" | custom-call | flops 1024 | bytes 1024 | tf_op jit(solution)/shard_map/project_band/pallas_call | solution.py:408
  141.7 17.6 %collective-permute-done.13.refs_1_ = bf16[16,64,512]{2,1,0:T(8,128)(2,1)S(1)} collective-permute-done((bf16[16,64,512]{2,1,0:T(8,128)(2,1)S(1)}, bf16[16,64,512]{2,1,0:T(8,128)(2,1)S(1)}, u32[]{:S(2)}, u32[]{:S(2)}) %collective-permute-start.13) | collective-permute-done | bytes 1048608 | tf_op jit(solution)/shard_map/ppermute | solution.py:472
  159.3 17.7 %collective-permute-done.14.refs_1_ = bf16[16,64,512]{2,1,0:T(8,128)(2,1)S(1)} collective-permute-done((bf16[16,64,512]{2,1,0:T(8,128)(2,1)S(1)}, bf16[16,64,512]{2,1,0:T(8,128)(2,1)S(1)}, u32[]{:S(2)}, u32[]{:S(2)}) %collective-permute-start.14) | collective-permute-done | bytes 1048608 | tf_op jit(solution)/shard_map/ppermute | solution.py:472
  177.0 1.6 collective-permute-start.15
  179.5 1.5 collective-permute-start.17
  181.0 1.2 project_band.16.total_ref
  182.2 1.2 project_band.17.total_ref
  183.4 14.8 %collective-permute-done.15.refs_1_ = bf16[4096,128]{1,0:T(8,128)(2,1)S(1)} collective-permute-done((bf16[4096,128]{1,0:T(8,128)(2,1)S(1)}, bf16[4096,128]{1,0:T(8,128)(2,1)S(1)}, u32[]{:S(2)}, u32[]{:S(2)}) %collective-permute-start.15) | collective-permute-done | bytes 1048608 | tf_op jit(solution)/shard_map/ppermute | solution.py:472
  200.9 1.6 collective-permute-start.19
  202.8 2.6 %collective-permute-done.19.side_ref = f32[128,128]{1,0:T(8,128)S(1)} collective-permute-done((f32[128,128]{1,0:T(8,128)S(1)}, f32[128,128]{1,0:T(8,128)S(1)}, u32[]{:S(2)}, u32[]{:S(2)}) %collective-permute-start.19) | collective-permute-done | bytes 65568 | tf_op jit(solution)/shard_map/ppermute | solution.py:542
  205.5 1.1 collective-permute-done.20.both_ref
  207.2 1.9 merge.1
  209.1 1.1 collective-permute-start.21
  210.2 1.6 collective-permute-start.22
  213.3 1.1 collective-permute-done.22
  214.4 2.5 %collective-permute-done.23 = f32[72,128]{1,0:T(8,128)S(1)} collective-permute-done((f32[72,128]{1,0:T(8,128)}, f32[72,128]{1,0:T(8,128)S(1)}, u32[]{:S(2)}, u32[]{:S(2)}) %collective-permute-start.23) | collective-permute-done | bytes 36896 | tf_op jit(solution)/shard_map/ppermute | solution.py:472
  217.6 2.5 %collective-permute-start.24 = (f32[72,128]{1,0:T(8,128)S(1)}, f32[72,128]{1,0:T(8,128)S(1)}, u32[]{:S(2)}, u32[]{:S(2)}) collective-permute-start(f32[72,128]{1,0:T(8,128)S(1)} %add_add_fusion.summed_ref), channel_id=1, source_target_pairs={{0,16},{2,18},{4,20},{6,22},{8,24},{10,26},{12,28},{14,30},{16,0},... | collective-permute-start | bytes 110600 | tf_op jit(solution)/shard_map/ppermute | solution.py:472
  220.1 2.7 %collective-permute-done.24.more_ref = f32[72,128]{1,0:T(8,128)S(1)} collective-permute-done((f32[72,128]{1,0:T(8,128)S(1)}, f32[72,128]{1,0:T(8,128)S(1)}, u32[]{:S(2)}, u32[]{:S(2)}) %collective-permute-start.24) | collective-permute-done | bytes 36896 | tf_op jit(solution)/shard_map/ppermute | solution.py:472
  223.6 22.9 %orthogonal_iteration.1 = (bf16[8192,128]{1,0:T(8,128)(2,1)}, f32[64,128]{1,0:T(8,128)}, f32[1,128]{1,0:T(1,128)}) custom-call(f32[72,128]{1,0:T(8,128)S(1)} %add_add_fusion.summed_ref, f32[72,128]{1,0:T(8,128)S(1)} %collective-permute-done.24.more_ref, f32[1,128]{1,0:T(1,128)S(1)} %bitcast.3, f32[128,128]{1,0:T(8,128)S(1)} %copy-done.19, ...), custom_call_target="tpu_custom_call" | custom-call | tf_op jit(solution)/shard_map/orthogonal_iteration/pallas_call | solution.py:187
  (98 shorter events, 14.1 us)
Async XLA Ops:
  5.7 8.2 %copy-start = (f32[256,512]{1,0:T(8,128)S(1)}, f32[256,512]{1,0:T(8,128)}, u32[]{:S(2)}) copy-start(f32[256,512]{1,0:T(8,128)} %refs_3_.21) | copy-start | bytes 1572868
  5.8 8.2 %copy-start.1 = (s32[256,512]{1,0:T(8,128)S(1)}, s32[256,512]{1,0:T(8,128)}, u32[]{:S(2)}) copy-start(s32[256,512]{1,0:T(8,128)} %refs_6_.16) | copy-start | bytes 1572868
  5.8 15.1 %collective-permute-start = (bf16[16,32,512]{2,1,0:T(8,128)(2,1)}, bf16[16,32,512]{2,1,0:T(8,128)(2,1)S(1)}, u32[]{:S(2)}, u32[]{:S(2)}) collective-permute-start(bf16[16,32,512]{2,1,0:T(8,128)(2,1)} %blur_bands.10), channel_id=1, source_target_pairs={{0,2},{2,0},{4,6},{6,4},{8,10},{10,8},{12,14},{14,12},{16,18},{18,... | collective-permute-start | bytes 1572872 | tf_op jit(solution)/shard_map/ppermute | solution.py:472
  13.9 9.0 %copy-start.29 = (bf16[16,32,512]{2,1,0:T(8,128)(2,1)S(1)}, bf16[16,32,512]{2,1,0:T(8,128)(2,1)}, u32[]{:S(2)}) copy-start(bf16[16,32,512]{2,1,0:T(8,128)(2,1)} %blur_bands.11) | copy-start | bytes 1572868
  13.9 10.8 %copy-start.2 = (bf16[512,512]{1,0:T(8,128)(2,1)S(1)}, bf16[512,512]{1,0:T(8,128)(2,1)}, u32[]{:S(2)}) copy-start(bf16[512,512]{1,0:T(8,128)(2,1)} %constant.27.clone.refs_6_.refs_7_) | copy-start | bytes 1572868
  13.9 10.8 %copy-start.5 = (s32[1088]{0:T(1024)S(1)}, s32[1088]{0:T(1024)}, u32[]{:S(2)}) copy-start(s32[1088]{0:T(1024)} %constant.26.clone.table_ref) | copy-start | bytes 13060
  13.9 10.8 %copy-start.20 = (s32[64]{0:T(128)S(1)}, s32[64]{0:T(128)}, u32[]{:S(2)}) copy-start(s32[64]{0:T(128)} %group_ref.19) | copy-start | bytes 772
  20.9 3.8 %collective-permute-start.4 = (bf16[64,16,512]{2,1,0:T(8,128)(2,1)S(1)}, bf16[64,16,512]{2,1,0:T(8,128)(2,1)S(1)}, u32[]{:S(2)}, u32[]{:S(2)}) collective-permute-start(bf16[64,16,512]{2,1,0:T(8,128)(2,1)S(1)} %multiply_convert_fusion), channel_id=1, source_target_pairs={{0,1},{1,0},{2,3},{3,2},{4,5},{5,4},{6,7},{7,6},{8,9},{9,8},{10,11... | collective-permute-start | bytes 3145736 | tf_op jit(solution)/shard_map/ppermute | solution.py:495
  20.9 62.6 %collective-permute-start.1 = (bf16[8192,128]{1,0:T(8,128)(2,1)}, bf16[8192,128]{1,0:T(8,128)(2,1)S(1)}, u32[]{:S(2)}, u32[]{:S(2)}) collective-permute-start(bf16[8192,128]{1,0:T(8,128)(2,1)} %basis_ref.1), channel_id=1, source_target_pairs={{0,8},{2,10},{8,16},{10,18},{16,24},{18,26},{24,28},{26,30},{28,20... | collective-permute-start | bytes 6291464 | tf_op jit(solution)/shard_map/ppermute | solution.py:472
  22.7 60.8 %collective-permute-start.2 = (bf16[8192,128]{1,0:T(8,128)(2,1)}, bf16[8192,128]{1,0:T(8,128)(2,1)S(1)}, u32[]{:S(2)}, u32[]{:S(2)}) collective-permute-start(bf16[8192,128]{1,0:T(8,128)(2,1)} %basis_ref.1), channel_id=1, source_target_pairs={{0,4},{2,6},{8,0},{10,2},{16,8},{18,10},{24,16},{26,18},{28,24},{3... | collective-permute-start | bytes 6291464 | tf_op jit(solution)/shard_map/ppermute | solution.py:472
  22.9 13.9 %collective-permute-start.3 = (bf16[16,32,512]{2,1,0:T(8,128)(2,1)S(1)}, bf16[16,32,512]{2,1,0:T(8,128)(2,1)S(1)}, u32[]{:S(2)}, u32[]{:S(2)}) collective-permute-start(bf16[16,32,512]{2,1,0:T(8,128)(2,1)S(1)} %copy-done.29), channel_id=1, source_target_pairs={{0,2},{2,0},{4,6},{6,4},{8,10},{10,8},{12,14},{14,12},{16,18},{18,... | collective-permute-start | bytes 1572872 | tf_op jit(solution)/shard_map/ppermute | solution.py:472
  32.4 13.7 %copy-start.10 = (bf16[16,64,512]{2,1,0:T(8,128)(2,1)}, bf16[16,64,512]{2,1,0:T(8,128)(2,1)S(1)}, u32[]{:S(2)}) copy-start(bf16[16,64,512]{2,1,0:T(8,128)(2,1)S(1)} %get-tuple-element.80.refs_0_) | copy-start | bytes 3145732
  36.8 27.6 %collective-permute-start.5 = (bf16[16,64,512]{2,1,0:T(8,128)(2,1)S(1)}, bf16[16,64,512]{2,1,0:T(8,128)(2,1)S(1)}, u32[]{:S(2)}, u32[]{:S(2)}) collective-permute-start(bf16[16,64,512]{2,1,0:T(8,128)(2,1)S(1)} %get-tuple-element.69), channel_id=1, source_target_pairs={{0,2},{2,0},{4,6},{6,4},{8,10},{10,8},{12,14},{14,12},{16,18},{18,... | collective-permute-start | bytes 3145736 | tf_op jit(solution)/shard_map/ppermute | solution.py:472
  46.2 8.8 %copy-start.12 = (bf16[16,64,512]{2,1,0:T(8,128)(2,1)}, bf16[16,64,512]{2,1,0:T(8,128)(2,1)S(1)}, u32[]{:S(2)}) copy-start(bf16[16,64,512]{2,1,0:T(8,128)(2,1)S(1)} %get-tuple-element.82.refs_0_) | copy-start | bytes 3145732
  46.2 37.3 %collective-permute-start.6 = (bf16[16,64,512]{2,1,0:T(8,128)(2,1)S(1)}, bf16[16,64,512]{2,1,0:T(8,128)(2,1)S(1)}, u32[]{:S(2)}, u32[]{:S(2)}) collective-permute-start(bf16[16,64,512]{2,1,0:T(8,128)(2,1)S(1)} %get-tuple-element.70), channel_id=1, source_target_pairs={{0,2},{2,0},{4,6},{6,4},{8,10},{10,8},{12,14},{14,12},{16,18},{18,... | collective-permute-start | bytes 3145736 | tf_op jit(solution)/shard_map/ppermute | solution.py:472
  83.5 10.1 %copy-start.16 = (bf16[16,64,512]{2,1,0:T(8,128)(2,1)}, bf16[16,64,512]{2,1,0:T(8,128)(2,1)S(1)}, u32[]{:S(2)}) copy-start(bf16[16,64,512]{2,1,0:T(8,128)(2,1)S(1)} %collective-permute-done.6.refs_1_) | copy-start | bytes 3145732
  83.5 47.6 %collective-permute-start.7 = (bf16[8192,128]{1,0:T(8,128)(2,1)S(1)}, bf16[8192,128]{1,0:T(8,128)(2,1)}, u32[]{:S(2)}, u32[]{:S(2)}) collective-permute-start(bf16[8192,128]{1,0:T(8,128)(2,1)S(1)} %collective-permute-done.1.refs_4_.refs_3_), channel_id=1, source_target_pairs={{0,8},{2,10},{8,16},{10,18},{16,24},{18,26},{24,28},{26,30},{28,20... | collective-permute-start | bytes 6291464 | tf_op jit(solution)/shard_map/ppermute | solution.py:472
  85.2 45.9 %collective-permute-start.8 = (bf16[8192,128]{1,0:T(8,128)(2,1)S(1)}, bf16[8192,128]{1,0:T(8,128)(2,1)}, u32[]{:S(2)}, u32[]{:S(2)}) collective-permute-start(bf16[8192,128]{1,0:T(8,128)(2,1)S(1)} %collective-permute-done.2.refs_2_), channel_id=1, source_target_pairs={{0,4},{2,6},{8,0},{10,2},{16,8},{18,10},{24,16},{26,18},{28,24},{3... | collective-permute-start | bytes 6291464 | tf_op jit(solution)/shard_map/ppermute | solution.py:472
  85.6 40.3 %collective-permute-start.10 = (bf16[16,64,512]{2,1,0:T(8,128)(2,1)}, bf16[16,64,512]{2,1,0:T(8,128)(2,1)}, u32[]{:S(2)}, u32[]{:S(2)}) collective-permute-start(bf16[16,64,512]{2,1,0:T(8,128)(2,1)} %get-tuple-element.85), channel_id=1, source_target_pairs={{0,2},{2,0},{4,6},{6,4},{8,10},{10,8},{12,14},{14,12},{16,18},{18,... | collective-permute-start | bytes 3145736 | tf_op jit(solution)/shard_map/ppermute | solution.py:472
  87.2 44.0 %collective-permute-start.9 = (bf16[16,64,512]{2,1,0:T(8,128)(2,1)}, bf16[16,64,512]{2,1,0:T(8,128)(2,1)}, u32[]{:S(2)}, u32[]{:S(2)}) collective-permute-start(bf16[16,64,512]{2,1,0:T(8,128)(2,1)} %get-tuple-element.84), channel_id=1, source_target_pairs={{0,2},{2,0},{4,6},{6,4},{8,10},{10,8},{12,14},{14,12},{16,18},{18,... | collective-permute-start | bytes 3145736 | tf_op jit(solution)/shard_map/ppermute | solution.py:472
  112.0 8.8 %copy-start.3 = (bf16[8192,128]{1,0:T(8,128)(2,1)S(1)}, bf16[8192,128]{1,0:T(8,128)(2,1)}, u32[]{:S(2)}) copy-start(bf16[8192,128]{1,0:T(8,128)(2,1)} %basis_ref.1) | copy-start | bytes 6291460
  120.8 1.9 copy-start.11
  120.8 1.9 copy-start.15
  122.7 1.9 copy-start.13
  124.7 8.5 %copy-start.28 = (bf16[16,64,512]{2,1,0:T(8,128)(2,1)S(1)}, bf16[16,64,512]{2,1,0:T(8,128)(2,1)}, u32[]{:S(2)}) copy-start(bf16[16,64,512]{2,1,0:T(8,128)(2,1)} %copy-done.27) | copy-start | bytes 3145732
  124.7 10.0 %copy-start.26 = (bf16[16,64,512]{2,1,0:T(8,128)(2,1)S(1)}, bf16[16,64,512]{2,1,0:T(8,128)(2,1)}, u32[]{:S(2)}) copy-start(bf16[16,64,512]{2,1,0:T(8,128)(2,1)} %copy-done.25) | copy-start | bytes 3145732
  124.7 10.5 %copy-start.7 = (bf16[16,64,512]{2,1,0:T(8,128)(2,1)S(1)}, bf16[16,64,512]{2,1,0:T(8,128)(2,1)}, u32[]{:S(2)}) copy-start(bf16[16,64,512]{2,1,0:T(8,128)(2,1)} %copy-done.6) | copy-start | bytes 3145732
  131.2 45.8 %collective-permute-start.11 = (bf16[8192,128]{1,0:T(8,128)(2,1)}, bf16[8192,128]{1,0:T(8,128)(2,1)S(1)}, u32[]{:S(2)}, u32[]{:S(2)}) collective-permute-start(bf16[8192,128]{1,0:T(8,128)(2,1)} %collective-permute-done.7.refs_2_), channel_id=1, source_target_pairs={{0,8},{2,10},{8,16},{10,18},{16,24},{18,26},{24,28},{26,30},{28,20... | collective-permute-start | bytes 6291464 | tf_op jit(solution)/shard_map/ppermute | solution.py:472
  132.7 44.2 %collective-permute-start.12 = (bf16[8192,128]{1,0:T(8,128)(2,1)}, bf16[8192,128]{1,0:T(8,128)(2,1)S(1)}, u32[]{:S(2)}, u32[]{:S(2)}) collective-permute-start(bf16[8192,128]{1,0:T(8,128)(2,1)} %collective-permute-done.8.refs_2_), channel_id=1, source_target_pairs={{0,4},{2,6},{8,0},{10,2},{16,8},{18,10},{24,16},{26,18},{28,24},{3... | collective-permute-start | bytes 6291464 | tf_op jit(solution)/shard_map/ppermute | solution.py:472
  133.2 26.1 %collective-permute-start.13 = (bf16[16,64,512]{2,1,0:T(8,128)(2,1)S(1)}, bf16[16,64,512]{2,1,0:T(8,128)(2,1)S(1)}, u32[]{:S(2)}, u32[]{:S(2)}) collective-permute-start(bf16[16,64,512]{2,1,0:T(8,128)(2,1)S(1)} %copy-done.28), channel_id=1, source_target_pairs={{0,2},{2,0},{4,6},{6,4},{8,10},{10,8},{12,14},{14,12},{16,18},{18,... | collective-permute-start | bytes 3145736 | tf_op jit(solution)/shard_map/ppermute | solution.py:472
  134.7 42.3 %collective-permute-start.14 = (bf16[16,64,512]{2,1,0:T(8,128)(2,1)S(1)}, bf16[16,64,512]{2,1,0:T(8,128)(2,1)S(1)}, u32[]{:S(2)}, u32[]{:S(2)}) collective-permute-start(bf16[16,64,512]{2,1,0:T(8,128)(2,1)S(1)} %copy-done.26), channel_id=1, source_target_pairs={{0,2},{2,0},{4,6},{6,4},{8,10},{10,8},{12,14},{14,12},{16,18},{18,... | collective-permute-start | bytes 3145736 | tf_op jit(solution)/shard_map/ppermute | solution.py:472
  141.7 37.8 %copy-start.24 = (bf16[16,64,512]{2,1,0:T(8,128)(2,1)S(1)}, bf16[16,64,512]{2,1,0:T(8,128)(2,1)}, u32[]{:S(2)}) copy-start(bf16[16,64,512]{2,1,0:T(8,128)(2,1)} %copy-done.23) | copy-start | bytes 3145732
  141.7 39.3 %copy-start.9 = (bf16[16,64,512]{2,1,0:T(8,128)(2,1)S(1)}, bf16[16,64,512]{2,1,0:T(8,128)(2,1)}, u32[]{:S(2)}) copy-start(bf16[16,64,512]{2,1,0:T(8,128)(2,1)} %copy-done.8) | copy-start | bytes 3145732
  177.0 21.1 %collective-permute-start.15 = (bf16[4096,128]{1,0:T(8,128)(2,1)S(1)}, bf16[4096,128]{1,0:T(8,128)(2,1)S(1)}, u32[]{:S(2)}, u32[]{:S(2)}) collective-permute-start(bf16[4096,128]{1,0:T(8,128)(2,1)S(1)} %slice.6), channel_id=1, source_target_pairs={{0,8},{2,10},{8,16},{10,18},{16,24},{18,26},{24,28},{26,30},{28,20... | collective-permute-start | bytes 3145736 | tf_op jit(solution)/shard_map/ppermute | solution.py:472
  178.7 20.6 %collective-permute-start.16 = (bf16[4096,128]{1,0:T(8,128)(2,1)S(1)}, bf16[4096,128]{1,0:T(8,128)(2,1)S(1)}, u32[]{:S(2)}, u32[]{:S(2)}) collective-permute-start(bf16[4096,128]{1,0:T(8,128)(2,1)S(1)} %slice.7), channel_id=1, source_target_pairs={{0,4},{2,6},{8,0},{10,2},{16,8},{18,10},{24,16},{26,18},{28,24},{3... | collective-permute-start | bytes 3145736 | tf_op jit(solution)/shard_map/ppermute | solution.py:472
  179.5 20.4 %collective-permute-start.17 = (bf16[16,64,512]{2,1,0:T(8,128)(2,1)S(1)}, bf16[16,64,512]{2,1,0:T(8,128)(2,1)S(1)}, u32[]{:S(2)}, u32[]{:S(2)}) collective-permute-start(bf16[16,64,512]{2,1,0:T(8,128)(2,1)S(1)} %copy-done.24), channel_id=1, source_target_pairs={{0,2},{2,0},{4,6},{6,4},{8,10},{10,8},{12,14},{14,12},{16,18},{18,... | collective-permute-start | bytes 3145736 | tf_op jit(solution)/shard_map/ppermute | solution.py:472
  199.8 23.0 %copy-start.4 = (bf16[8192,128]{1,0:T(8,128)(2,1)S(1)}, bf16[8192,128]{1,0:T(8,128)(2,1)}, u32[]{:S(2)}) copy-start(bf16[8192,128]{1,0:T(8,128)(2,1)} %basis_ref.1) | copy-start | bytes 6291460
  199.8 23.0 %copy-start.19 = (f32[128,128]{1,0:T(8,128)S(1)}, f32[128,128]{1,0:T(8,128)}, u32[]{:S(2)}) copy-start(f32[128,128]{1,0:T(8,128)} %start_ref.1) | copy-start | bytes 196612
  199.8 23.0 %copy-start.22 = (f32[128]{0:T(128)S(1)}, f32[128]{0:T(128)}, u32[]{:S(2)}) copy-start(f32[128]{0:T(128)} %param.13) | copy-start | bytes 1540
  200.8 5.7 %copy-start.18 = (f32[128,128]{1,0:T(8,128)}, f32[128,128]{1,0:T(8,128)S(1)}, u32[]{:S(2)}) copy-start(f32[128,128]{1,0:T(8,128)S(1)} %project_band.21.total_ref) | copy-start | bytes 196612
  200.9 1.9 collective-permute-start.18
  200.9 4.5 %collective-permute-start.19 = (f32[128,128]{1,0:T(8,128)S(1)}, f32[128,128]{1,0:T(8,128)S(1)}, u32[]{:S(2)}, u32[]{:S(2)}) collective-permute-start(f32[128,128]{1,0:T(8,128)S(1)} %project_band.21.total_ref), channel_id=1, source_target_pairs={{0,2},{1,3},{2,0},{3,1},{4,6},{5,7},{6,4},{7,5},{8,10},{9,11},{10,... | collective-permute-start | bytes 196616 | tf_op jit(solution)/shard_map/ppermute | solution.py:542
  202.5 4.0 %collective-permute-start.20 = (f32[128,128]{1,0:T(8,128)S(1)}, f32[128,128]{1,0:T(8,128)S(1)}, u32[]{:S(2)}, u32[]{:S(2)}) collective-permute-start(f32[128,128]{1,0:T(8,128)S(1)} %project_band.21.total_ref), channel_id=1, source_target_pairs={{0,3},{1,2},{2,1},{3,0},{4,7},{5,6},{6,5},{7,4},{8,11},{9,10},{10,... | collective-permute-start | bytes 196616 | tf_op jit(solution)/shard_map/ppermute | solution.py:542
  202.8 3.7 %copy-start.30 = (f32[128,128]{1,0:T(8,128)}, f32[128,128]{1,0:T(8,128)S(1)}, u32[]{:S(2)}) copy-start(f32[128,128]{1,0:T(8,128)S(1)} %collective-permute-done.18.strip_ref) | copy-start | bytes 196612
  209.1 4.2 %collective-permute-start.21 = (f32[72,128]{1,0:T(8,128)}, f32[72,128]{1,0:T(8,128)S(1)}, u32[]{:S(2)}, u32[]{:S(2)}) collective-permute-start(f32[72,128]{1,0:T(8,128)} %get-tuple-element.112), channel_id=1, source_target_pairs={{0,4},{2,6},{4,0},{6,2},{8,12},{10,14},{12,8},{14,10},{16,20},{18,... | collective-permute-start | bytes 110600 | tf_op jit(solution)/shard_map/ppermute | solution.py:472
  210.2 4.2 %collective-permute-start.22 = (f32[72,128]{1,0:T(8,128)}, f32[72,128]{1,0:T(8,128)S(1)}, u32[]{:S(2)}, u32[]{:S(2)}) collective-permute-start(f32[72,128]{1,0:T(8,128)} %get-tuple-element.112), channel_id=1, source_target_pairs={{0,8},{2,10},{4,12},{6,14},{8,0},{10,2},{12,4},{14,6},{16,24},{18,... | collective-permute-start | bytes 110600 | tf_op jit(solution)/shard_map/ppermute | solution.py:472
  211.8 5.1 %collective-permute-start.23 = (f32[72,128]{1,0:T(8,128)}, f32[72,128]{1,0:T(8,128)S(1)}, u32[]{:S(2)}, u32[]{:S(2)}) collective-permute-start(f32[72,128]{1,0:T(8,128)} %get-tuple-element.112), channel_id=1, source_target_pairs={{0,12},{2,14},{4,8},{6,10},{8,4},{10,6},{12,0},{14,2},{16,28},{18,... | collective-permute-start | bytes 110600 | tf_op jit(solution)/shard_map/ppermute | solution.py:472
  217.6 5.2 %collective-permute-start.24 = (f32[72,128]{1,0:T(8,128)S(1)}, f32[72,128]{1,0:T(8,128)S(1)}, u32[]{:S(2)}, u32[]{:S(2)}) collective-permute-start(f32[72,128]{1,0:T(8,128)S(1)} %add_add_fusion.summed_ref), channel_id=1, source_target_pairs={{0,16},{2,18},{4,20},{6,22},{8,24},{10,26},{12,28},{14,30},{16,0},... | collective-permute-start | bytes 110600 | tf_op jit(solution)/shard_map/ppermute | solution.py:472
  (10 other events, 10.4 us)
